TPU v7x, 32 devices: a whole 2x2x4 slice. The times are simulated.
32 devices in a mesh: dp: 4 (over y, core), shard: 8 (over z, x).
Axes of the slice: x: 2, y: 2, z: 4, core: 2. Of those that a mesh axis runs over, the one named last changes fastest.
Arguments:
- tokens: bfloat16 [3072, 8, 1024], P('shard', 'dp'), may hold values from -6 to 6
- dino: bfloat16 [4096, 8, 768], P('shard', 'dp'), may hold values from -6 to 6
- first_gain: float32 [1024], P(('dp', 'shard')), may hold values from 0.1 to 1.9
- first_shift: float32 [1024], P(('dp', 'shard')), may hold values from -0.625 to 0.625
- image_weight: float32 [768, 1024], P(('dp', 'shard')), may hold values from -0.21875 to 0.21875
- cross_query: float32 [1024, 1024], P(('dp', 'shard')), may hold values from -0.1875 to 0.1875
- cross_keyval: float32 [1024, 2048], P(('dp', 'shard')), may hold values from -0.1875 to 0.1875
- cross_output: float32 [1024, 1024], P(('dp', 'shard')), may hold values from -6 to 6
- second_gain: float32 [1024], P(('dp', 'shard')), may hold values from 0.1 to 1.9
- second_shift: float32 [1024], P(('dp', 'shard')), may hold values from -0.125 to 0.125
- self_project: float32 [1024, 3072], P(('dp', 'shard')), may hold values from -0.1875 to 0.1875
- self_output: float32 [1024, 1024], P(('dp', 'shard')), may hold values from -6 to 6
- third_gain: float32 [1024], P(('dp', 'shard')), may hold values from 0.1 to 1.9
- third_shift: float32 [1024], P(('dp', 'shard')), may hold values from -0.625 to 0.625
- hidden_weight: float32 [1024, 4096], P(('dp', 'shard')), may hold values from -0.1875 to 0.1875
- hidden_bias: float32 [4096], P(('dp', 'shard')), may hold values from -1.75 to 1.75
- output_weight: float32 [4096, 1024], P(('dp', 'shard')), may hold values from -0.09375 to 0.09375
- deconv_weight: float32 [1024, 320], P(('dp', 'shard')), may hold values from -0.1875 to 0.1875
- ray_mask: int32 [8192], P(('dp', 'shard')), may hold values 0 or 1
- block_object: int32 [64], P(('dp', 'shard')), may hold values from 0 to 1
- sample_cell: int32 [3, 262144], P(None, ('dp', 'shard')), may hold values from 0 to 4030
- sample_frac: float32 [6, 262144], P(None, ('dp', 'shard')), may hold values from 0 to 1
- out_grad: bfloat16 [3072, 8, 1024], P('shard', 'dp'), may hold values from -8 to 8
- sampled_grad: bfloat16 [8192, 2560], P(('dp', 'shard')), may hold values from -6 to 6
Outputs:
- tokens_out: bfloat16 [3072, 8, 1024], P('shard', 'dp')
- sampled: bfloat16 [8192, 2560], P(('dp', 'shard'))
- tokens_grad: float32 [3072, 8, 1024], P('shard', 'dp')
- dino_grad: float32 [4096, 8, 768], P('shard', 'dp')
- first_gain_grad: float32 [1024], P(('dp', 'shard'))
- first_shift_grad: float32 [1024], P(('dp', 'shard'))
- image_weight_grad: float32 [768, 1024], P(('dp', 'shard'))
- cross_query_grad: float32 [1024, 1024], P(('dp', 'shard'))
- cross_keyval_grad: float32 [1024, 2048], P(('dp', 'shard'))
- cross_output_grad: float32 [1024, 1024], P(('dp', 'shard'))
- second_gain_grad: float32 [1024], P(('dp', 'shard'))
- second_shift_grad: float32 [1024], P(('dp', 'shard'))
- self_project_grad: float32 [1024, 3072], P(('dp', 'shard'))
- self_output_grad: float32 [1024, 1024], P(('dp', 'shard'))
- third_gain_grad: float32 [1024], P(('dp', 'shard'))
- third_shift_grad: float32 [1024], P(('dp', 'shard'))
- hidden_weight_grad: float32 [1024, 4096], P(('dp', 'shard'))
- hidden_bias_grad: float32 [4096], P(('dp', 'shard'))
- output_weight_grad: float32 [4096, 1024], P(('dp', 'shard'))
- deconv_weight_grad: float32 [1024, 320], P(('dp', 'shard'))
All inputs are finite; a program needn't handle non-finite values. No bound on the sum of `ray_mask` on one device may be relied on, other than what follows from the above.
Results may differ from a plain program's by a relative error of at most 0.019.
The roundings to bfloat16 on the way count: a program that leaves them out, or rounds other values in their place, can miss the bound.
Values may be sent and summed in bfloat16 or wider, within the bound.
No kernel may reach another device: no remote copies, remote signals or barrier semaphores. Data moves between devices by JAX's collectives and lax.ppermute only.
A program may use at most 320 MiB of HBM per device.

v0:
```python
import math

import jax
import jax.numpy as jnp
from jax import lax
from jax.sharding import PartitionSpec as P

D = 1024
H = 16
HD = 64
CH = 80
G = 32
RB = 128
SAMP = 32
TOK_OBJ = 3072


epsilon = 1e-05


def lower(value):
    return value.astype(jnp.bfloat16)


def widen(value):
    return value.astype(jnp.float32)


def product(left, right):
    return jnp.dot(left, right, preferred_element_type=jnp.float32)


def product_back(left, right):
    return lax.dot_general(
        left, right, (((left.ndim - 1,), (1,)), ((), ())), preferred_element_type=jnp.float32
    )


def outer_sum(left, right):
    leading = tuple(range(left.ndim - 1))
    return lax.dot_general(
        left, right, ((leading, leading), ((), ())), preferred_element_type=jnp.float32
    )


def normalize(values, gain, shift):
    centered = values - jnp.mean(values, axis=-1, keepdims=True)
    inverse = lax.rsqrt(jnp.mean(centered * centered, axis=-1, keepdims=True) + epsilon)
    unit = centered * inverse
    return (unit * gain + shift, unit, inverse)


def normalize_back(grad, unit, inverse, gain):
    gain_grad = jnp.sum(grad * unit, axis=(0, 1))
    shift_grad = jnp.sum(grad, axis=(0, 1))
    scaled = grad * gain
    inner = (
        scaled
        - jnp.mean(scaled, axis=-1, keepdims=True)
        - unit * jnp.mean(scaled * unit, axis=-1, keepdims=True)
    )
    return (inverse * inner, gain_grad, shift_grad)


def gelu(values):
    return 0.5 * values * (1.0 + lax.erf(values * 0.7071067811865476))


def attend_forward(query, keys, values):
    length, count, width = query.shape
    block = math.gcd(length, 512)
    scale = width ** (-0.5)

    def one_block(query_part):
        scores = (
            jnp.einsum("qne,kne->nqk", query_part, keys, preferred_element_type=jnp.float32) * scale
        )
        peak = jnp.max(scores, axis=-1, keepdims=True)
        expo = jnp.exp(scores - peak)
        total = jnp.sum(expo, axis=-1, keepdims=True)
        probability = lower(expo / total)
        output = jnp.einsum("nqk,kne->qne", probability, values, preferred_element_type=jnp.float32)
        return (lower(output), jnp.transpose((peak + jnp.log(total))[:, :, 0]))

    outputs, logsum = lax.map(one_block, query.reshape(length // block, block, count, width))
    return (outputs.reshape(length, count, width), logsum.reshape(length, count))


def attend_backward(query, keys, values, logsum, dout):
    length, count, width = query.shape
    block = math.gcd(length, 512)
    scale = width ** (-0.5)
    blocks = length // block

    def one_block(carry, parts):
        keys_grad, values_grad = carry
        query_part, logsum_part, dout_part = parts
        scores = (
            jnp.einsum("qne,kne->nqk", query_part, keys, preferred_element_type=jnp.float32) * scale
        )
        probability = jnp.exp(scores - jnp.transpose(logsum_part)[:, :, None])
        values_grad = values_grad + jnp.einsum(
            "nqk,qne->kne", lower(probability), dout_part, preferred_element_type=jnp.float32
        )
        prob_grad = jnp.einsum(
            "qne,kne->nqk", dout_part, values, preferred_element_type=jnp.float32
        )
        delta = jnp.sum(probability * prob_grad, axis=-1, keepdims=True)
        score_grad = lower(probability * (prob_grad - delta))
        query_grad = (
            jnp.einsum("nqk,kne->qne", score_grad, keys, preferred_element_type=jnp.float32) * scale
        )
        keys_grad = (
            keys_grad
            + jnp.einsum("nqk,qne->kne", score_grad, query_part, preferred_element_type=jnp.float32)
            * scale
        )
        return ((keys_grad, values_grad), query_grad)

    empty = jnp.zeros(keys.shape, jnp.float32)
    parts = (
        query.reshape(blocks, block, count, width),
        logsum.reshape(blocks, block, count),
        dout.reshape(blocks, block, count, width),
    )
    (keys_grad, values_grad), query_grad = lax.scan(one_block, (empty, empty), parts)
    return (query_grad.reshape(length, count, width), keys_grad, values_grad)


def self_attend(packed):
    flat = packed[:, 0]
    output, logsum = attend_forward(flat[:, :, :HD], flat[:, :, HD : 2 * HD], flat[:, :, 2 * HD :])
    return (output[:, None], logsum[:, None], packed)


def cross_attend(parts):
    query, keyval = parts
    flat_query = query[:, 0]
    flat_keyval = keyval[:, 0]
    output, logsum = attend_forward(flat_query, flat_keyval[:, :, :HD], flat_keyval[:, :, HD:])
    return (output[:, None], logsum[:, None], query, keyval)


def plane_table(cells, fractions, plane):
    side = 2 * G
    points = cells.shape[1]
    columns = lax.broadcasted_iota(jnp.int32, (points, G * G * 4), 1)
    table = jnp.zeros((points, G * G * 4), jnp.bfloat16)
    row_start = cells[plane] // side
    col_start = cells[plane] % side
    across = fractions[2 * plane]
    downward = fractions[2 * plane + 1]
    for drow in range(2):
        for dcol in range(2):
            pixel_row = row_start + drow
            pixel_col = col_start + dcol
            local = pixel_row // 2 * G + pixel_col // 2
            flat = local * 4 + pixel_row % 2 * 2 + pixel_col % 2
            vertical = downward if drow == 1 else 1.0 - downward
            horizontal = across if dcol == 1 else 1.0 - across
            weight = lower(vertical * horizontal)
            table = table + jnp.where(
                columns == flat[:, None], weight[:, None], jnp.zeros((), jnp.bfloat16)
            )
    return table


def body(
    tokens,
    dino,
    first_gain,
    first_shift,
    image_weight,
    cross_query,
    cross_keyval,
    cross_output,
    second_gain,
    second_shift,
    self_project,
    self_output,
    third_gain,
    third_shift,
    hidden_weight,
    hidden_bias,
    output_weight,
    deconv_weight,
    ray_mask,
    block_object,
    sample_cell,
    sample_frac,
    out_grad,
    sampled_grad,
):
    rows = tokens.shape[0]
    groups = tokens.shape[1]
    patch_rows = dino.shape[0]
    pairs = groups * H
    members = lax.axis_size("shard")
    local_pairs = pairs // members
    gathered = (
        lax.all_gather(lower(first_gain), ("dp", "shard"), axis=0, tiled=True),
        lax.all_gather(lower(first_shift), ("dp", "shard"), axis=0, tiled=True),
        lax.all_gather(lower(image_weight), ("dp", "shard"), axis=0, tiled=True),
        lax.all_gather(lower(cross_query), ("dp", "shard"), axis=0, tiled=True),
        lax.all_gather(lower(cross_keyval), ("dp", "shard"), axis=0, tiled=True),
        lax.all_gather(lower(cross_output), ("dp", "shard"), axis=0, tiled=True),
        lax.all_gather(lower(second_gain), ("dp", "shard"), axis=0, tiled=True),
        lax.all_gather(lower(second_shift), ("dp", "shard"), axis=0, tiled=True),
        lax.all_gather(lower(self_project), ("dp", "shard"), axis=0, tiled=True),
        lax.all_gather(lower(self_output), ("dp", "shard"), axis=0, tiled=True),
        lax.all_gather(lower(third_gain), ("dp", "shard"), axis=0, tiled=True),
        lax.all_gather(lower(third_shift), ("dp", "shard"), axis=0, tiled=True),
        lax.all_gather(lower(hidden_weight), ("dp", "shard"), axis=0, tiled=True),
        lax.all_gather(lower(hidden_bias), ("dp", "shard"), axis=0, tiled=True),
        lax.all_gather(lower(output_weight), ("dp", "shard"), axis=0, tiled=True),
        lax.all_gather(lower(deconv_weight), ("dp", "shard"), axis=0, tiled=True),
    )
    (
        gain_a,
        shift_a,
        image_w,
        query_w,
        keyval_w,
        cross_w,
        gain_b,
        shift_b,
        project_w,
        self_w,
        gain_c,
        shift_c,
        hidden_w,
        bias_w,
        output_w,
        deconv_w,
    ) = gathered
    token_values = widen(tokens)
    normed_full, unit_a, inverse_a = normalize(token_values, widen(gain_a), widen(shift_a))
    normed_a = lower(normed_full)
    query_full = lower(product(normed_a, query_w))
    image = lower(product(dino, image_w))
    keyval_full = lower(product(image, keyval_w))
    cross_out, cross_logsum, cross_query_kept, cross_keyval_kept = cross_attend(
        (
            lax.all_to_all(
                query_full.reshape(rows, members, local_pairs, HD),
                "shard",
                split_axis=1,
                concat_axis=0,
                tiled=True,
            ),
            lax.all_to_all(
                keyval_full.reshape(patch_rows, members, local_pairs, 2 * HD),
                "shard",
                split_axis=1,
                concat_axis=0,
                tiled=True,
            ),
        )
    )
    cross_logsum = cross_logsum[:, 0]
    cross_query_kept = cross_query_kept[:, 0]
    cross_keyval_kept = cross_keyval_kept[:, 0]
    cross_back = lax.all_to_all(cross_out, "shard", split_axis=0, concat_axis=1, tiled=True)
    cross_mix = cross_back.reshape(rows, groups, D)
    after_cross = token_values + product(cross_mix, cross_w)
    normed_full, unit_b, inverse_b = normalize(after_cross, widen(gain_b), widen(shift_b))
    normed_b = lower(normed_full)
    projected = lower(product(normed_b, project_w))
    self_out, self_logsum, self_kept = self_attend(
        lax.all_to_all(
            projected.reshape(rows, members, local_pairs, 3 * HD),
            "shard",
            split_axis=1,
            concat_axis=0,
            tiled=True,
        )
    )
    self_logsum = self_logsum[:, 0]
    self_kept = self_kept[:, 0]
    self_back = lax.all_to_all(self_out, "shard", split_axis=0, concat_axis=1, tiled=True)
    self_mix = self_back.reshape(rows, groups, D)
    after_self = after_cross + product(self_mix, self_w)
    normed_full, unit_c, inverse_c = normalize(after_self, widen(gain_c), widen(shift_c))
    normed_c = lower(normed_full)
    hidden = product(normed_c, hidden_w) + widen(bias_w)
    activated = lower(gelu(hidden))
    result = after_self + product(activated, output_w)
    result_low = lower(result)
    planes = lower(product(result_low, deconv_w))
    plane_all = lax.all_gather(planes, "shard", axis=0, tiled=True)
    plane_sets = jnp.moveaxis(plane_all, 1, 0).reshape(groups, TOK_OBJ * 4, CH)
    plane_cols = G * G * 4
    ray_rows = ray_mask.shape[0]
    group_rays = math.gcd(RB, max(1, 512 // SAMP))
    turns = ray_rows // group_rays
    point_rows = group_rays * SAMP
    cell_turns = jnp.moveaxis(sample_cell.reshape(3, turns, point_rows), 1, 0)
    frac_turns = jnp.moveaxis(sample_frac.reshape(6, turns, point_rows), 1, 0)
    owners = jnp.repeat(block_object, RB // group_rays)
    alive = ray_mask.reshape(turns, group_rays)

    def sample_turn(parts):
        cells, fractions, owner, live = parts
        chosen = lax.dynamic_index_in_dim(plane_sets, owner, 0, keepdims=False)
        picked = jnp.zeros((point_rows, CH), jnp.float32)
        for plane in range(3):
            table = plane_table(cells, fractions, plane)
            picked = picked + jnp.dot(
                table,
                chosen[plane * plane_cols : (plane + 1) * plane_cols],
                preferred_element_type=jnp.float32,
            )
        return lower(picked.reshape(group_rays, SAMP * CH) * widen(live)[:, None])

    sampled = lax.map(sample_turn, (cell_turns, frac_turns, owners, alive)).reshape(
        ray_rows, SAMP * CH
    )
    masked_grad = jnp.where(
        alive[:, :, None] == 1,
        sampled_grad.reshape(turns, group_rays, SAMP * CH),
        jnp.zeros((), jnp.bfloat16),
    )

    def spread_turn(accum, parts):
        cells, fractions, owner, grad_part = parts
        flat_grad = grad_part.reshape(point_rows, CH)
        terms = []
        for plane in range(3):
            table = plane_table(cells, fractions, plane)
            terms.append(
                lax.dot_general(
                    table, flat_grad, (((0,), (0,)), ((), ())), preferred_element_type=jnp.float32
                )
            )
        term = jnp.concatenate(terms, axis=0)
        current = lax.dynamic_index_in_dim(accum, owner, 0, keepdims=True)
        return (lax.dynamic_update_index_in_dim(accum, current + term[None], owner, 0), None)

    plane_grad, _ = lax.scan(
        spread_turn,
        jnp.zeros((groups, TOK_OBJ * 4, CH), jnp.float32),
        (cell_turns, frac_turns, owners, masked_grad),
    )
    plane_grad = jnp.moveaxis(plane_grad.reshape(groups, TOK_OBJ, 4 * CH), 0, 1)
    plane_low = lower(
        lax.psum_scatter(
            plane_grad.astype(jnp.bfloat16), "shard", scatter_dimension=0, tiled=True
        ).astype(jnp.float32)
    )
    deconv_grad = outer_sum(result_low, plane_low)
    result_grad = widen(out_grad) + product_back(plane_low, deconv_w)
    result_low_grad = lower(result_grad)
    output_weight_grad = outer_sum(activated, result_low_grad)
    activated_grad = product_back(result_low_grad, output_w)
    _, gelu_pull = jax.vjp(gelu, hidden)
    hidden_grad = lower(gelu_pull(activated_grad)[0])
    hidden_bias_grad = jnp.sum(widen(hidden_grad), axis=(0, 1))
    hidden_weight_grad = outer_sum(normed_c, hidden_grad)
    back_c, gain_c_grad, shift_c_grad = normalize_back(
        product_back(hidden_grad, hidden_w), unit_c, inverse_c, widen(gain_c)
    )
    self_grad = result_grad + back_c
    self_low_grad = lower(self_grad)
    self_weight_grad = outer_sum(self_mix, self_low_grad)
    self_mix_grad = lower(product_back(self_low_grad, self_w))
    self_pairs_grad = lax.all_to_all(
        self_mix_grad.reshape(rows, pairs, HD), "shard", split_axis=1, concat_axis=0, tiled=True
    )
    query_g, keys_g, values_g = attend_backward(
        self_kept[:, :, :HD],
        self_kept[:, :, HD : 2 * HD],
        self_kept[:, :, 2 * HD :],
        self_logsum,
        self_pairs_grad,
    )
    project_pairs_grad = lower(jnp.concatenate([query_g, keys_g, values_g], axis=2))
    project_grad = lax.all_to_all(
        project_pairs_grad, "shard", split_axis=0, concat_axis=1, tiled=True
    ).reshape(rows, groups, 3 * D)
    project_weight_grad = outer_sum(normed_b, project_grad)
    back_b, gain_b_grad, shift_b_grad = normalize_back(
        product_back(project_grad, project_w), unit_b, inverse_b, widen(gain_b)
    )
    cross_grad = self_grad + back_b
    cross_low_grad = lower(cross_grad)
    cross_weight_grad = outer_sum(cross_mix, cross_low_grad)
    cross_mix_grad = lower(product_back(cross_low_grad, cross_w))
    cross_pairs_grad = lax.all_to_all(
        cross_mix_grad.reshape(rows, pairs, HD), "shard", split_axis=1, concat_axis=0, tiled=True
    )
    query_h, keys_h, values_h = attend_backward(
        cross_query_kept,
        cross_keyval_kept[:, :, :HD],
        cross_keyval_kept[:, :, HD:],
        cross_logsum,
        cross_pairs_grad,
    )
    query_back, keyval_back = (
        lax.all_to_all(lower(query_h), "shard", split_axis=0, concat_axis=1, tiled=True),
        lax.all_to_all(
            lower(jnp.concatenate([keys_h, values_h], axis=2)),
            "shard",
            split_axis=0,
            concat_axis=1,
            tiled=True,
        ),
    )
    query_back = query_back.reshape(rows, groups, D)
    keyval_back = keyval_back.reshape(patch_rows, groups, 2 * D)
    query_weight_grad = outer_sum(normed_a, query_back)
    back_a, gain_a_grad, shift_a_grad = normalize_back(
        product_back(query_back, query_w), unit_a, inverse_a, widen(gain_a)
    )
    tokens_grad = cross_grad + back_a
    keyval_weight_grad = outer_sum(image, keyval_back)
    image_grad = lower(product_back(keyval_back, keyval_w))
    image_weight_grad = outer_sum(dino, image_grad)
    dino_grad = product_back(image_grad, image_w)
    shares = tuple(
        (
            lax.psum_scatter(gain_a_grad, ("dp", "shard"), scatter_dimension=0, tiled=True),
            lax.psum_scatter(shift_a_grad, ("dp", "shard"), scatter_dimension=0, tiled=True),
            lax.psum_scatter(image_weight_grad, ("dp", "shard"), scatter_dimension=0, tiled=True),
            lax.psum_scatter(query_weight_grad, ("dp", "shard"), scatter_dimension=0, tiled=True),
            lax.psum_scatter(keyval_weight_grad, ("dp", "shard"), scatter_dimension=0, tiled=True),
            lax.psum_scatter(cross_weight_grad, ("dp", "shard"), scatter_dimension=0, tiled=True),
            lax.psum_scatter(gain_b_grad, ("dp", "shard"), scatter_dimension=0, tiled=True),
            lax.psum_scatter(shift_b_grad, ("dp", "shard"), scatter_dimension=0, tiled=True),
            lax.psum_scatter(project_weight_grad, ("dp", "shard"), scatter_dimension=0, tiled=True),
            lax.psum_scatter(self_weight_grad, ("dp", "shard"), scatter_dimension=0, tiled=True),
            lax.psum_scatter(gain_c_grad, ("dp", "shard"), scatter_dimension=0, tiled=True),
            lax.psum_scatter(shift_c_grad, ("dp", "shard"), scatter_dimension=0, tiled=True),
            lax.psum_scatter(hidden_weight_grad, ("dp", "shard"), scatter_dimension=0, tiled=True),
            lax.psum_scatter(hidden_bias_grad, ("dp", "shard"), scatter_dimension=0, tiled=True),
            lax.psum_scatter(output_weight_grad, ("dp", "shard"), scatter_dimension=0, tiled=True),
            lax.psum_scatter(deconv_grad, ("dp", "shard"), scatter_dimension=0, tiled=True),
        )
    )
    return (result_low, sampled, tokens_grad, dino_grad) + shares


def solution(mesh):
    return jax.shard_map(
        body,
        mesh=mesh,
        in_specs=(
            P("shard", "dp", None),
            P("shard", "dp", None),
            P(("dp", "shard")),
            P(("dp", "shard")),
            P(("dp", "shard"), None),
            P(("dp", "shard"), None),
            P(("dp", "shard"), None),
            P(("dp", "shard"), None),
            P(("dp", "shard")),
            P(("dp", "shard")),
            P(("dp", "shard"), None),
            P(("dp", "shard"), None),
            P(("dp", "shard")),
            P(("dp", "shard")),
            P(("dp", "shard"), None),
            P(("dp", "shard")),
            P(("dp", "shard"), None),
            P(("dp", "shard"), None),
            P(("dp", "shard")),
            P(("dp", "shard")),
            P(None, ("dp", "shard")),
            P(None, ("dp", "shard")),
            P("shard", "dp", None),
            P(("dp", "shard"), None),
        ),
        out_specs=(
            P("shard", "dp", None),
            P(("dp", "shard"), None),
            P("shard", "dp", None),
            P("shard", "dp", None),
            P(("dp", "shard")),
            P(("dp", "shard")),
            P(("dp", "shard"), None),
            P(("dp", "shard"), None),
            P(("dp", "shard"), None),
            P(("dp", "shard"), None),
            P(("dp", "shard")),
            P(("dp", "shard")),
            P(("dp", "shard"), None),
            P(("dp", "shard"), None),
            P(("dp", "shard")),
            P(("dp", "shard")),
            P(("dp", "shard"), None),
            P(("dp", "shard")),
            P(("dp", "shard"), None),
            P(("dp", "shard"), None),
        ),
        check_vma=False,
    )
```

profile of v0, /device:TPU:0, one launch (start us, length us, event | category | flops | bytes accessed | tf_op | source)
XLA Modules:
  0.0 4488.1 jit_solution(3275729972312427477)
XLA Ops:
  24.5 413.2 %while.89 = (s32[]{:T(128)}, f32[2,12288,80]{1,2,0:T(8,128)}, s32[16]{0:T(128)S(1)}, s32[16,3,512]{2,1,0:T(4,128)}, f32[16,6,512]{2,1,0:T(8,128)}, /*index=5*/bf16[16,16,2560]{2,1,0:T(8,128)(2,1)}) while((s32[]{:T(128)}, f32[2,12288,80]{1,2,0:T(8,128)}, s32[16]{0:T(128)S(1)}, s32[16,3,512]{2,1,0:T(4,128)}, ...), condition=%wide.region_17.18_spmd.clone, body=%wide.region_16.17_spmd.sunk.clone | while | flops 1110518784 | bytes 16449755 | solution.py:339
  463.5 43.9 all-reduce.14
  538.9 16.2 all-to-all-done
  568.0 101.5 %all-to-all-done.1 = bf16[512,8,4,128]{0,3,2,1:T(8,128)(2,1)} async-done(((bf16[512,8,4,128]{0,3,2,1:T(8,128)(2,1)}), bf16[512,8,4,128]{0,3,2,1:T(8,128)(2,1)}, u32[]{:S(2)}, u32[]{:S(2)}) %all-to-all-start.1) | async-done | bytes 4194336 | tf_op jit(solution)/shard_map/all_to_all | solution.py:251
  692.7 262.8 %while.86 = (s32[]{:T(128)}, bf16[6,512,4,64]{1,3,2,0:T(8,128)(2,1)}, f32[6,512,4]{1,2,0:T(4,128)S(1)}, bf16[6,512,4,64]{1,3,2,0:T(8,128)(2,1)}, bf16[4096,4,64]...) while((s32[]{:T(128)}, bf16[6,512,4,64]{1,3,2,0:T(8,128)(2,1)}, f32[6,512,4]{1,2,0:T(4,128)S(1)}, ...), condition=%wide.region_5.6_spmd.clone, body=%wide.region_2.5_spmd.sunk.clone | while | flops 2223110144 | bytes 105448520 | solution.py:85
  721.2 15.6 fusion.497
  765.4 15.7 fusion.497
  809.2 15.4 fusion.497
  852.9 15.4 fusion.497
  896.5 15.4 fusion.497
  940.1 15.4 fusion.497
  972.8 36.8 all-to-all-done.2
  1048.1 142.4 %all-to-all-done.3 = bf16[384,8,4,192]{0,3,2,1:T(8,128)(2,1)} async-done(((bf16[384,8,4,192]{0,3,2,1:T(8,128)(2,1)}), bf16[384,8,4,192]{0,3,2,1:T(8,128)(2,1)}, u32[]{:S(2)}, u32[]{:S(2)}) %all-to-all-start.3) | async-done | bytes 4718624 | tf_op jit(solution)/shard_map/all_to_all | solution.py:270
  1213.1 149.3 %while.87 = (s32[]{:T(128)}, bf16[6,512,4,64]{1,3,2,0:T(8,128)(2,1)}, f32[6,512,4]{1,2,0:T(4,128)S(1)}, bf16[6,512,4,64]{1,3,2,0:T(8,128)(2,1)}, bf16[3072,4,64]...) while((s32[]{:T(128)}, bf16[6,512,4,64]{1,3,2,0:T(8,128)(2,1)}, f32[6,512,4]{1,2,0:T(4,128)S(1)}, ...), condition=%wide.region_11.12_spmd.clone, body=%wide.region_8.11_spmd.sunk.clone | while | flops 1667364864 | bytes 179897440 | solution.py:85
  1379.2 91.1 %all-gather = bf16[32,1,128]{2,1,0:T(2,128)(2,1)S(1)} all-gather(bf16[1,1,128]{2,1,0:T(2,128)(2,1)S(1)} %convert_bitcast_fusion.1), channel_id=1, replica_groups=mesh['dp'=4,'shard'=8] {'dp','shard'}, dimensions={0}, use_global_device_ids=true | all-gather | bytes 8448 | tf_op jit(solution)/shard_map/all_gather | solution.py:214
  1470.4 68.0 %all_gather.66 = bf16[1024,320]{1,0:T(8,128)(2,1)S(1)} all-gather(bf16[32,320]{1,0:T(8,128)(2,1)S(1)} %convert_element_type.505), channel_id=1, replica_groups=mesh['dp'=4,'shard'=8] {'dp','shard'}, dimensions={0}, use_global_device_ids=true | all-gather | bytes 675840 | tf_op jit(solution)/shard_map/all_gather | solution.py:216
  1579.1 17.2 convert_reduce_fusion
  1640.0 34.5 all-to-all-done.5
  1686.5 501.9 %while.90 = (s32[]{:T(128)}, f32[3072,4,64]{0,2,1:T(8,128)}, f32[3072,4,64]{0,2,1:T(8,128)}, bf16[6,512,4,64]{1,3,2,0:T(8,128)(2,1)}, bf16[6,512,4,64]{1,3,2,0:T...) while((s32[]{:T(128)}, f32[3072,4,64]{0,2,1:T(8,128)}, ...), condition=%wide.region_23.24_spmd.clone.clone, body=%wide.region_21.23_spmd.clone.sunk.clone | while | flops 4106090496 | bytes 207678064 | solution.py:126
  1698.4 16.8 multiply_reduce_fusion.23
  1715.2 21.7 multiply_convert_fusion.50
  1780.5 16.6 multiply_reduce_fusion.23
  1797.2 21.7 multiply_convert_fusion.50
  1837.6 15.4 fusion.531
  1864.3 16.7 multiply_reduce_fusion.23
  1881.0 21.7 multiply_convert_fusion.50
  1921.5 15.4 fusion.531
  1948.2 16.6 multiply_reduce_fusion.23
  1964.8 21.7 multiply_convert_fusion.50
  2005.3 15.4 fusion.531
  2032.0 16.6 multiply_reduce_fusion.23
  2048.6 21.7 multiply_convert_fusion.50
  2089.1 15.4 fusion.531
  2115.7 16.7 multiply_reduce_fusion.23
  2132.4 21.7 multiply_convert_fusion.50
  2172.9 15.4 fusion.531
  2219.5 135.3 %all-to-all-done.6 = bf16[3072,4,192]{2,1,0:T(4,128)(2,1)} async-done(((bf16[3072,4,192]{2,1,0:T(4,128)(2,1)}), bf16[3072,4,192]{2,1,0:T(4,128)(2,1)}, u32[]{:S(2)}, u32[]{:S(2)}) %all-to-all-start.6) | async-done | bytes 4718624 | tf_op jit(solution)/shard_map/all_to_all | solution.py:377
  2394.0 37.8 all-to-all-done.7
  2440.8 609.7 %while.91 = (s32[]{:T(128)}, f32[4096,4,64]{0,2,1:T(8,128)}, f32[4096,4,64]{0,2,1:T(8,128)}, bf16[6,512,4,64]{1,3,2,0:T(8,128)(2,1)}, bf16[6,512,4,64]{1,3,2,0:T...) while((s32[]{:T(128)}, f32[4096,4,64]{0,2,1:T(8,128)}, ...), condition=%wide.region_28.29_spmd.clone.clone, body=%wide.region_26.28_spmd.clone.sunk.clone | while | flops 5474744320 | bytes 351857312 | solution.py:126
  2456.3 23.0 multiply_reduce_fusion.24
  2479.3 27.7 multiply_convert_fusion.51
  2525.2 16.0 fusion.544
  2556.3 23.0 multiply_reduce_fusion.24
  2579.3 27.7 multiply_convert_fusion.51
  2626.4 17.2 fusion.544
  2658.7 23.0 multiply_reduce_fusion.24
  2681.7 27.6 multiply_convert_fusion.51
  2728.4 17.1 fusion.544
  2760.4 22.9 multiply_reduce_fusion.24
  2783.4 27.6 multiply_convert_fusion.51
  2830.0 17.1 fusion.544
  2862.1 22.9 multiply_reduce_fusion.24
  2885.0 27.6 multiply_convert_fusion.51
  2931.7 17.1 fusion.544
  2963.7 22.9 multiply_reduce_fusion.24
  2986.7 27.6 multiply_convert_fusion.51
  3033.4 17.1 fusion.544
  3077.4 23.5 all-to-all-done.8
  3118.9 95.0 %all-to-all-done.9 = bf16[4096,4,128]{2,1,0:T(4,128)(2,1)} async-done(((bf16[4096,4,128]{2,1,0:T(4,128)(2,1)}), bf16[4096,4,128]{2,1,0:T(4,128)(2,1)}, u32[]{:S(2)}, u32[]{:S(2)}) %all-to-all-start.9) | async-done | bytes 4194336 | tf_op jit(solution)/shard_map/all_to_all | solution.py:400
  3313.8 382.1 %while.88 = (s32[]{:T(128)}, bf16[16,16,2560]{2,1,0:T(8,128)(2,1)}, s32[16,3,512]{2,1,0:T(4,128)}, f32[16,6,512]{2,1,0:T(8,128)}, s32[16]{0:T(128)S(1)}, /*index=5*/bf16[2,12288,80]{2,1,0:T(8,128)(2,1)}, s32[16,16]{1,0:T(8,128)}) while((s32[]{:T(128)}, bf16[16,16,2560]{2,1,0:T(8,128)(2,1)}, s32[16,3,512]{2,1,0:T(4,128)}, ...), condition=%wide.region_15.16_spmd.clone, body=%wide.region_14.15_spmd.sunk.clone | while | flops 1107733504 | bytes 5014475 | solution.py:315
  3702.7 43.4 all-reduce.13
  3763.7 170.3 %reduce-scatter.25.cloned.1.call-done = f32[32,4096]{1,0:T(8,128)} async-done(((f32[1024,4096]{1,0:T(8,128)}), f32[32,4096]{1,0:T(8,128)}) %reduce-scatter.25.cloned.1.call-update) | async-done | bytes 524304 | tf_op jit(solution)/shard_map/reduce_scatter | solution.py:433
  3934.0 360.2 %reduce-scatter.27.cloned.1.call-done = f32[128,1024]{1,0:T(8,128)} async-done(((f32[4096,1024]{1,0:T(8,128)}), f32[128,1024]{1,0:T(8,128)}) %reduce-scatter.27.cloned.1.call-update) | async-done | bytes 524304 | tf_op jit(solution)/shard_map/reduce_scatter | solution.py:435
  4294.2 186.4 %reduce-scatter.17.cloned.1.call-done = f32[32,2048]{1,0:T(8,128)} async-done(((f32[1024,2048]{1,0:T(8,128)}), f32[32,2048]{1,0:T(8,128)}) %reduce-scatter.17.cloned.1.call-update) | async-done | bytes 262160 | tf_op jit(solution)/shard_map/reduce_scatter | solution.py:425
  (1090 shorter events, 1995.4 us)
Async XLA Ops:
  8.0 500.6 %all-gather.11.cloned.1.call-start = ((), (), s32[]{:S(2)}) async-start(), calls=%async_computation.20 | async-start | bytes 2162688 | tf_op jit(solution)/shard_map/all_gather | solution.py:204
  9.6 509.2 %all-gather.13.cloned.1.call-start = ((), (), s32[]{:S(2)}) async-start(), calls=%async_computation.21 | async-start | bytes 1622016 | tf_op jit(solution)/shard_map/all_gather | solution.py:203
  11.2 512.2 %all-gather.15.cloned.1.call-start = ((), (), s32[]{:S(2)}) async-start(), calls=%async_computation.22 | async-start | bytes 4325376 | tf_op jit(solution)/shard_map/all_gather | solution.py:205
  12.9 1006.6 %all-gather.17.cloned.1.call-start = ((), (), s32[]{:S(2)}) async-start(), calls=%async_computation.23 | async-start | bytes 2162688 | tf_op jit(solution)/shard_map/all_gather | solution.py:206
  14.5 1011.4 %all-gather.19.cloned.1.call-start = ((), (), s32[]{:S(2)}) async-start(), calls=%async_computation.24 | async-start | bytes 6488064 | tf_op jit(solution)/shard_map/all_gather | solution.py:209
  16.3 1522.0 %reduce-scatter.13.cloned.1.call-start = ((), (), s32[]{:S(2)}) async-start(), calls=%async_computation.29 | async-start | bytes 5308416 | tf_op jit(solution)/shard_map/reduce_scatter | solution.py:346
  461.5 45.9 %copy-start.11 = (bf16[384,2,1024]{2,1,0:T(2,128)(2,1)S(1)}, bf16[384,2,1024]{2,1,0:T(2,128)(2,1)}, u32[]{:S(2)}) copy-start(bf16[384,2,1024]{2,1,0:T(2,128)(2,1)} %param.36) | copy-start | bytes 4718596
  513.8 41.3 all-to-all-start
  555.1 114.4 %all-to-all-start.1 = ((bf16[512,8,4,128]{0,3,2,1:T(8,128)(2,1)}), bf16[512,8,4,128]{0,3,2,1:T(8,128)(2,1)}, u32[]{:S(2)}, u32[]{:S(2)}) async-start(bf16[512,8,4,128]{0,3,2,1:T(8,128)(2,1)} %bitcast.545), calls=%async_computation.1 | async-start | bytes 8388608 | tf_op jit(solution)/shard_map/all_to_all | solution.py:251
  559.9 996.7 %all-gather.21.cloned.1.call-start = ((), (), s32[]{:S(2)}) async-start(), calls=%async_computation.25 | async-start | bytes 2162688 | tf_op jit(solution)/shard_map/all_gather | solution.py:210
  560.7 1003.1 %all-gather.23.cloned.1.call-start = ((), (), s32[]{:S(2)}) async-start(), calls=%async_computation.26 | async-start | bytes 8650752 | tf_op jit(solution)/shard_map/all_gather | solution.py:213
  955.5 12.6 copy-start.2
  955.5 12.6 copy-start.40
  961.2 11.5 copy-start.74
  961.2 11.6 copy-start.73
  968.1 41.5 all-to-all-start.2
  972.7 53.3 %copy-start.53 = (f32[1024]{0:T(1024)}, f32[1024]{0:T(1024)S(1)}, u32[]{:S(2)}) copy-start(f32[1024]{0:T(1024)S(1)} %convert_element_type.487) | copy-start | bytes 12292
  972.7 53.2 %copy-start.69 = (f32[1024]{0:T(1024)}, f32[1024]{0:T(1024)S(1)}, u32[]{:S(2)}) copy-start(f32[1024]{0:T(1024)S(1)} %convert_element_type.489) | copy-start | bytes 12292
  1023.8 12.1 copy-start.44
  1042.6 148.0 %all-to-all-start.3 = ((bf16[384,8,4,192]{0,3,2,1:T(8,128)(2,1)}), bf16[384,8,4,192]{0,3,2,1:T(8,128)(2,1)}, u32[]{:S(2)}, u32[]{:S(2)}) async-start(bf16[384,8,4,192]{0,3,2,1:T(8,128)(2,1)} %bitcast.543), calls=%async_computation.3 | async-start | bytes 9437184 | tf_op jit(solution)/shard_map/all_to_all | solution.py:270
  1047.3 531.8 %all-gather.25.cloned.1.call-start = ((), (), s32[]{:S(2)}) async-start(), calls=%async_computation.27 | async-start | bytes 8650752 | tf_op jit(solution)/shard_map/all_gather | solution.py:215
  1367.9 11.3 copy-start.71
  1367.9 11.3 copy-start.86
  1367.9 102.5 %copy-start.42 = (f32[32,320]{1,0:T(8,128)S(1)}, f32[32,320]{1,0:T(8,128)}, u32[]{:S(2)}) copy-start(f32[32,320]{1,0:T(8,128)} %param.53) | copy-start | bytes 122884
  1374.8 167.3 %all-to-all-start.4 = ((bf16[8,2,49152]{2,1,0:T(2,128)(2,1)}), bf16[8,2,49152]{2,1,0:T(2,128)(2,1)}, u32[]{:S(2)}, u32[]{:S(2)}) async-start(bf16[8,2,49152]{2,1,0:T(2,128)(2,1)} %reshape.2098), calls=%async_computation.4 | async-start | bytes 3145728 | tf_op jit(solution)/shard_map/all_to_all | solution.py:280
  1379.2 231.6 %copy-start.32 = (f32[1024]{0:T(1024)}, f32[1024]{0:T(1024)S(1)}, u32[]{:S(2)}) copy-start(f32[1024]{0:T(1024)S(1)} %convert_element_type.495) | copy-start | bytes 12292
  1379.2 184.6 %copy-start.36 = (f32[1024]{0:T(1024)}, f32[1024]{0:T(1024)S(1)}, u32[]{:S(2)}) copy-start(f32[1024]{0:T(1024)S(1)} %convert_element_type.497) | copy-start | bytes 12292
  1561.7 49.1 %copy-start.34 = (f32[384,2]{0,1:T(2,128)}, f32[384,2]{0,1:T(2,128)S(1)}, u32[]{:S(2)}) copy-start(f32[384,2]{0,1:T(2,128)S(1)} %broadcast_multiply_fusion.6) | copy-start | bytes 9220
  1563.8 47.0 %copy-start.38 = (f32[384,2]{0,1:T(2,128)}, f32[384,2]{0,1:T(2,128)S(1)}, u32[]{:S(2)}) copy-start(f32[384,2]{0,1:T(2,128)S(1)} %add_rsqrt_fusion) | copy-start | bytes 9220
  1579.1 17.2 copy-start.9
  1596.3 14.5 copy-start.25
  1596.3 14.5 copy-start.15
  1596.3 14.5 copy-start.29
  1621.2 53.3 %all-to-all-start.5 = ((bf16[384,32,64]{0,2,1:T(8,128)(2,1)}), bf16[384,32,64]{0,2,1:T(8,128)(2,1)}, u32[]{:S(2)}, u32[]{:S(2)}) async-start(bf16[384,32,64]{0,2,1:T(8,128)(2,1)} %bitcast.554), calls=%async_computation.6 | async-start | bytes 3145728 | tf_op jit(solution)/shard_map/all_to_all | solution.py:366
  1625.5 1661.7 %all-gather.27.cloned.1.call-start = ((), (), s32[]{:S(2)}) async-start(), calls=%async_computation.28 | async-start | bytes 4423680 | tf_op jit(solution)/shard_map/all_gather | solution.py:290
  2204.8 149.9 %all-to-all-start.6 = ((bf16[3072,4,192]{2,1,0:T(4,128)(2,1)}), bf16[3072,4,192]{2,1,0:T(4,128)(2,1)}, u32[]{:S(2)}, u32[]{:S(2)}) async-start(bf16[3072,4,192]{2,1,0:T(4,128)(2,1)} %copy.330), calls=%async_computation.7 | async-start | bytes 12582912 | tf_op jit(solution)/shard_map/all_to_all | solution.py:377
  2210.2 1553.4 %reduce-scatter.29.cloned.1.call-start = ((), (), s32[]{:S(2)}) async-start(), calls=%async_computation.37 | async-start | bytes 1622016 | tf_op jit(solution)/shard_map/reduce_scatter | solution.py:436
  2214.2 1549.5 %reduce-scatter.23.cloned.1.call-start = ((), (), s32[]{:S(2)}) async-start(), calls=%async_computation.34 | async-start | bytes 4325376 | tf_op jit(solution)/shard_map/reduce_scatter | solution.py:430
  2384.4 47.5 %all-to-all-start.7 = ((bf16[384,32,64]{0,2,1:T(8,128)(2,1)}), bf16[384,32,64]{0,2,1:T(8,128)(2,1)}, u32[]{:S(2)}, u32[]{:S(2)}) async-start(bf16[384,32,64]{0,2,1:T(8,128)(2,1)} %bitcast.555), calls=%async_computation.8 | async-start | bytes 3145728 | tf_op jit(solution)/shard_map/all_to_all | solution.py:388
  2388.7 1375.0 %reduce-scatter.19.cloned.1.call-start = ((), (), s32[]{:S(2)}) async-start(), calls=%async_computation.32 | async-start | bytes 4325376 | tf_op jit(solution)/shard_map/reduce_scatter | solution.py:426
  2441.2 15.1 copy-start.7
  2507.1 12.3 copy-start
  2541.2 15.1 copy-start.7
  2607.1 13.4 copy-start
  2643.6 15.1 copy-start.7
  2709.3 13.2 copy-start
  2745.4 15.0 copy-start.7
  2810.9 13.2 copy-start
  2847.1 15.0 copy-start.7
  2912.6 13.2 copy-start
  2948.8 15.0 copy-start.7
  3014.3 13.2 copy-start
  3059.2 41.7 all-to-all-start.8
  3100.9 112.9 %all-to-all-start.9 = ((bf16[4096,4,128]{2,1,0:T(4,128)(2,1)}), bf16[4096,4,128]{2,1,0:T(4,128)(2,1)}, u32[]{:S(2)}, u32[]{:S(2)}) async-start(bf16[4096,4,128]{2,1,0:T(4,128)(2,1)} %copy.345), calls=%async_computation.10 | async-start | bytes 8388608 | tf_op jit(solution)/shard_map/all_to_all | solution.py:400
  3105.5 658.1 %reduce-scatter.15.cloned.1.call-start = ((), (), s32[]{:S(2)}) async-start(), calls=%async_computation.30 | async-start | bytes 4325376 | tf_op jit(solution)/shard_map/reduce_scatter | solution.py:424
  3118.8 644.9 %reduce-scatter.31.cloned.1.call-start = ((), (), s32[]{:S(2)}) async-start(), calls=%async_computation.38 | async-start | bytes 3244032
  3238.8 524.9 %reduce-scatter.21.cloned.1.call-start = ((), (), s32[]{:S(2)}) async-start(), calls=%async_computation.33 | async-start | bytes 12976128 | tf_op jit(solution)/shard_map/reduce_scatter | solution.py:429
  3251.8 682.2 %reduce-scatter.25.cloned.1.call-start = ((), (), s32[]{:S(2)}) async-start(), calls=%async_computation.35 | async-start | bytes 17301504 | tf_op jit(solution)/shard_map/reduce_scatter | solution.py:433
  3267.5 1026.6 %reduce-scatter.27.cloned.1.call-start = ((), (), s32[]{:S(2)}) async-start(), calls=%async_computation.36 | async-start | bytes 17301504 | tf_op jit(solution)/shard_map/reduce_scatter | solution.py:435
  3283.0 1197.6 %reduce-scatter.17.cloned.1.call-start = ((), (), s32[]{:S(2)}) async-start(), calls=%async_computation.31 | async-start | bytes 8650752 | tf_op jit(solution)/shard_map/reduce_scatter | solution.py:425
  3313.8 382.1 %copy-start.14 = (bf16[384,2,1024]{2,1,0:T(2,128)(2,1)S(1)}, bf16[384,2,1024]{2,1,0:T(2,128)(2,1)}, u32[]{:S(2)}) copy-start(bf16[384,2,1024]{2,1,0:T(2,128)(2,1)} %param.36) | copy-start | bytes 4718596
  3313.8 382.1 %copy-start.49 = (f32[384,2]{0,1:T(2,128)S(1)}, f32[384,2]{0,1:T(2,128)}, u32[]{:S(2)}) copy-start(f32[384,2]{0,1:T(2,128)} %copy-done.47) | copy-start | bytes 9220
  3313.8 382.1 %copy-start.52 = (f32[1024]{0:T(1024)S(1)}, f32[1024]{0:T(1024)}, u32[]{:S(2)}) copy-start(f32[1024]{0:T(1024)} %copy-done.50) | copy-start | bytes 12292
  3313.8 382.1 %copy-start.62 = (f32[384,2]{0,1:T(2,128)S(1)}, f32[384,2]{0,1:T(2,128)}, u32[]{:S(2)}) copy-start(f32[384,2]{0,1:T(2,128)} %copy-done.60) | copy-start | bytes 9220
  (72 other events, 338.1 us)
Sparse Core Ops, SparseCore 0:
  12.4 59.2 all-gather.10
  75.2 53.9 all-gather.12
  132.8 61.0 all-gather.14
  197.3 55.1 all-gather.16
  255.8 68.3 all-gather.18
  564.0 124.6 all-gather.20
  692.2 76.2 all-gather.22
  1051.7 139.8 all-gather.24
  2216.9 156.4 reduce-scatter.28
  2376.0 157.7 reduce-scatter.22
  2536.7 143.5 reduce-scatter.18
  3118.9 184.6 reduce-scatter.14
  3309.6 102.0 reduce-scatter.30
  3418.2 154.3 reduce-scatter.20
  3575.4 358.5 reduce-scatter.24
  3936.8 357.3 reduce-scatter.26
  4297.0 183.5 reduce-scatter.16
Sparse Core Ops, SparseCore 1:
  461.6 129.4 reduce-scatter.12
  1640.1 82.7 all-gather.26
where the time goes:
time: 4510 us; the launch traced here: 4490 us
  matrix products  1810 us (40%)
  waiting for transfers between devices  1340 us (30%)
  other arithmetic  554 us (12%)
  local copies, waits for them, and re-layouts  407 us (9%)
  blocking collectives  246 us (5%)
  loops' own time  66.6 us (1%)
  starting transfers between devices  47.4 us (1%)
    reduce_scatter x1, waiting for transfers between devices, body(): lax.psum_scatter(output_weight_grad, ('dp', 'shard'), scatter_dimension=0...  360 us
    convert_element_type x123, other arithmetic, lower(): return value.astype(jnp.bfloat16)  307 us
    dot_general x48, matrix products, sample_turn(): jnp.dot(table, chosen[plane * plane_cols:(plane + 1) * plane_cols], prefe...  281 us
    dot_general x24, matrix products, one_block(): jnp.einsum('qne,kne->nqk', query_part, keys, preferred_element_type=jnp.f...  266 us
    dot_general x48, matrix products, spread_turn(): lax.dot_general(table, flat_grad, (((0,), (0,)), ((), ())), preferred_ele...  245 us
    dot_general x12, matrix products, one_block(): jnp.einsum('qne,kne->nqk', dout_part, values, preferred_element_type=jnp....  238 us
    dot_general x12, matrix products, one_block(): jnp.einsum('nqk,qne->kne', lower(probability), dout_part, preferred_eleme...  193 us
    reduce_scatter x1, waiting for transfers between devices, body(): lax.psum_scatter(keyval_weight_grad, ('dp', 'shard'), scatter_dimension=0...  186 us
  transfers between devices with their start and end apart: 29, of which 12 were waited for; matrix products, arithmetic and copies ran while one was open for 60% of the time, Pallas kernels for 0%

commit v1 on v0

v1 whole, which is shorter than its diff:
```python
import functools
import math

import jax
import jax.numpy as jnp
from jax import lax
from jax.experimental import pallas as pl
from jax.experimental.pallas import tpu as pltpu
from jax.sharding import Mesh
from jax.sharding import PartitionSpec as P

D = 1024
H = 16
HD = 64
FF = 4096
DINO = 768
CH = 80
G = 32
RB = 128
SAMP = 32
TOK_OBJ = 3072
PIX = G * G
SCALE = HD ** (-0.5)
VMEM = 58 * 2**20

epsilon = 1e-05
NN = ((1,), (0,))
NT = ((1,), (1,))
TN = ((0,), (0,))
bf16 = jnp.bfloat16
f32 = jnp.float32


def lower(value):
    return value.astype(bf16)


def widen(value):
    return value.astype(f32)


def dot(left, right, dims):
    return lax.dot_general(left, right, (dims, ((), ())), preferred_element_type=f32)


def normalize(values, gain, shift):
    centered = values - jnp.mean(values, axis=-1, keepdims=True)
    inverse = lax.rsqrt(jnp.mean(centered * centered, axis=-1, keepdims=True) + epsilon)
    unit = centered * inverse
    return (unit * gain + shift, unit, inverse)


def normalize_back(grad, unit, inverse, gain):
    gain_grad = jnp.sum(grad * unit, axis=0)
    shift_grad = jnp.sum(grad, axis=0)
    scaled = grad * gain
    inner = (
        scaled
        - jnp.mean(scaled, axis=-1, keepdims=True)
        - unit * jnp.mean(scaled * unit, axis=-1, keepdims=True)
    )
    return (inverse * inner, gain_grad, shift_grad)


def gelu(values):
    return 0.5 * values * (1.0 + lax.erf(values * 0.7071067811865476))


def fixed(shape):
    return pl.BlockSpec(shape, lambda *_: (0,) * len(shape))


def forward_kernel(*refs, chunks, block, packed):
    q_refs, refs = refs[:chunks], refs[chunks:]
    if packed:
        kv_refs = q_refs
    else:
        kv_refs, refs = refs[:chunks], refs[chunks:]
    out_refs, refs = refs[:chunks], refs[chunks:]
    lse_ref, query_ref, keys_ref = refs
    first = HD if packed else 0
    turn = pl.program_id(0)

    @pl.when(turn == 0)
    def _():
        for r in range(chunks):
            keys_ref[r] = kv_refs[r][first : first + HD, :].T
            query_ref[r] = q_refs[r][:HD, :] * jnp.asarray(SCALE, bf16)

    query = query_ref[turn]
    count = query.shape[1]
    peak = jnp.full((1, count), -jnp.inf, f32)
    total = jnp.zeros((1, count), f32)
    mixed = jnp.zeros((HD, count), f32)
    places = [(r, c) for r in range(chunks) for c in range(0, keys_ref.shape[1], block)]

    def score(place):
        r, c = place
        return dot(keys_ref[r, c : c + block, :], query, NN)

    ahead = score(places[0])
    for step, (r, c) in enumerate(places):
        scores = ahead
        if step + 1 < len(places):
            ahead = score(places[step + 1])
        higher = jnp.maximum(peak, jnp.max(scores, axis=0, keepdims=True))
        expo = jnp.exp(scores - higher)
        shrink = jnp.exp(peak - higher)
        total = total * shrink + jnp.sum(expo, axis=0, keepdims=True)
        values = kv_refs[r][first + HD : first + 2 * HD, c : c + block]
        mixed = mixed * shrink + dot(values, lower(expo), NN)
        peak = higher
    out = lower(mixed / total)
    for r in range(chunks):

        @pl.when(turn == r)
        def _():
            out_refs[r][...] = out

    lse_ref[0] = peak + jnp.log(total)


def attend_forward(queries, keyvals):
    packed = keyvals is None
    sources = list(queries) if packed else list(queries) + list(keyvals)
    chunks = len(queries)
    count = queries[0].shape[1]
    length = sources[-1].shape[1]
    block = math.gcd(length, 256)
    steps = chunks * chunks * count * length
    *outs, lse = pl.pallas_call(
        functools.partial(forward_kernel, chunks=chunks, block=block, packed=packed),
        grid=(chunks,),
        in_specs=[fixed(s.shape) for s in sources],
        out_specs=[fixed((HD, count))] * chunks + [pl.BlockSpec((1, 1, count), lambda i: (i, 0, 0))],
        out_shape=[jax.ShapeDtypeStruct((HD, count), bf16)] * chunks
        + [jax.ShapeDtypeStruct((chunks, 1, count), f32)],
        scratch_shapes=[
            pltpu.VMEM((chunks, HD, count), bf16),
            pltpu.VMEM((chunks, length, HD), bf16),
        ],
        compiler_params=pltpu.CompilerParams(vmem_limit_bytes=VMEM),
        cost_estimate=pl.CostEstimate(
            flops=steps * 2 * 2 * 256, bytes_accessed=4 * chunks * length * 64, transcendentals=steps
        ),
        name="attend_forward",
    )(*sources)
    return outs, lse


def backward_kernel(*refs, chunks, block, packed):
    q_refs, refs = refs[:chunks], refs[chunks:]
    if packed:
        kv_refs = q_refs
    else:
        kv_refs, refs = refs[:chunks], refs[chunks:]
    dout_refs, out_refs, refs = refs[:chunks], refs[chunks : 2 * chunks], refs[2 * chunks :]
    lse_ref, refs = refs[0], refs[1:]
    query_grads, refs = refs[:chunks], refs[chunks:]
    if packed:
        grads = query_grads
    else:
        grads, refs = refs[:chunks], refs[chunks:]
    query_ref, dout_ref, delta_ref, keys_ref, keys_acc, values_acc = refs
    first = HD if packed else 0
    turn = pl.program_id(0)
    length = keys_ref.shape[1]

    @pl.when(turn == 0)
    def _():
        for r in range(chunks):
            keys_ref[r] = kv_refs[r][first : first + HD, :].T
            query_ref[r] = q_refs[r][:HD, :] * jnp.asarray(SCALE, bf16)
            dout_ref[r] = dout_refs[r][...]
            delta_ref[r] = jnp.sum(
                widen(dout_refs[r][...]) * widen(out_refs[r][...]), axis=0, keepdims=True
            )
        keys_acc[...] = jnp.zeros_like(keys_acc)
        values_acc[...] = jnp.zeros_like(values_acc)

    query = query_ref[turn]
    dout = dout_ref[turn]
    count = query.shape[1]

    def across(row):
        if block % 128:
            return jnp.broadcast_to(row, (block, count)).T
        return jnp.concatenate([jnp.broadcast_to(row, (128, count)).T] * (block // 128), axis=1)

    lse_cols = across(lse_ref[0])
    delta_cols = across(delta_ref[turn])
    query_rows = query.T
    dout_rows = dout.T
    query_grad = jnp.zeros((count, HD), f32)
    places = [(r, c) for r in range(chunks) for c in range(0, length, block)]

    def score(place):
        r, c = place
        span = slice(c, c + block)
        return (
            dot(query_rows, kv_refs[r][first : first + HD, span], NN),
            dot(dout_rows, kv_refs[r][first + HD : first + 2 * HD, span], NN),
        )

    ahead = score(places[0])
    for step, (r, c) in enumerate(places):
        scores, prob_grad = ahead
        if step + 1 < len(places):
            ahead = score(places[step + 1])
        span = slice(c, c + block)
        probability = jnp.exp(scores - lse_cols)
        score_grad = lower(probability * (prob_grad - delta_cols))
        query_grad = query_grad + dot(score_grad, keys_ref[r, span, :], NN)
        values_acc[r, :, span] += dot(dout, lower(probability), NN)
        keys_acc[r, :, span] += dot(query, score_grad, NN)
    query_grad = lower((query_grad * SCALE).T)
    for r in range(chunks):

        @pl.when(turn == r)
        def _():
            query_grads[r][:HD, :] = query_grad

    @pl.when(turn == chunks - 1)
    def _():
        for r in range(chunks):
            grads[r][first : first + HD, :] = lower(keys_acc[r])
            grads[r][first + HD : first + 2 * HD, :] = lower(values_acc[r])


def attend_backward(queries, keyvals, douts, outs, lse):
    packed = keyvals is None
    sources = list(queries) if packed else list(queries) + list(keyvals)
    chunks = len(queries)
    count = queries[0].shape[1]
    length = sources[-1].shape[1]
    block = math.gcd(length, 256)
    steps = chunks * chunks * count * length
    results = [s.shape for s in sources]
    sources = sources + list(douts) + list(outs)
    grads = pl.pallas_call(
        functools.partial(backward_kernel, chunks=chunks, block=block, packed=packed),
        grid=(chunks,),
        in_specs=[fixed(s.shape) for s in sources] + [pl.BlockSpec((1, 1, count), lambda i: (i, 0, 0))],
        out_specs=[fixed(s) for s in results],
        out_shape=[jax.ShapeDtypeStruct(s, bf16) for s in results],
        scratch_shapes=[
            pltpu.VMEM((chunks, HD, count), bf16),
            pltpu.VMEM((chunks, HD, count), bf16),
            pltpu.VMEM((chunks, 1, count), f32),
            pltpu.VMEM((chunks, length, HD), bf16),
            pltpu.VMEM((chunks, HD, length), f32),
            pltpu.VMEM((chunks, HD, length), f32),
        ],
        compiler_params=pltpu.CompilerParams(vmem_limit_bytes=VMEM),
        cost_estimate=pl.CostEstimate(
            flops=steps * 2 * 5 * 200, bytes_accessed=8 * chunks * length * 64, transcendentals=steps
        ),
        name="attend_backward",
    )(*sources, lse)
    return grads[:chunks], grads[chunks:]


def split_kernel(me_ref, source_ref, *out_refs, heads):
    turn = pl.program_id(0)
    for k in range(len(out_refs) // heads):

        @pl.when(turn == k)
        def _():
            for j in range(heads):
                out_refs[k * heads + j][...] = source_ref[0, j]


def split(values, me):
    chunks, heads, height, count = values.shape
    outs = pl.pallas_call(
        functools.partial(split_kernel, heads=heads),
        grid_spec=pltpu.PrefetchScalarGridSpec(
            num_scalar_prefetch=1,
            grid=(chunks,),
            in_specs=[pl.BlockSpec((1, heads, height, count), lambda k, m: (m[0] ^ k, 0, 0, 0))],
            out_specs=[fixed((height, count))] * (chunks * heads),
        ),
        out_shape=[jax.ShapeDtypeStruct((height, count), bf16)] * (chunks * heads),
        compiler_params=pltpu.CompilerParams(vmem_limit_bytes=VMEM),
        cost_estimate=pl.CostEstimate(flops=0, bytes_accessed=4 * values.size, transcendentals=0),
        name="split",
    )(me, values)
    return [[outs[k * heads + j] for k in range(chunks)] for j in range(heads)]


def assemble_kernel(me_ref, *refs, heads):
    turn = pl.program_id(0)
    out_ref = refs[-1]
    for k in range((len(refs) - 1) // heads):

        @pl.when(turn == k)
        def _():
            for j in range(heads):
                out_ref[0, j] = refs[k * heads + j][...]


def assemble(parts, me):
    heads, chunks = len(parts), len(parts[0])
    height, count = parts[0][0].shape
    sources = [parts[j][k] for k in range(chunks) for j in range(heads)]
    return pl.pallas_call(
        functools.partial(assemble_kernel, heads=heads),
        grid_spec=pltpu.PrefetchScalarGridSpec(
            num_scalar_prefetch=1,
            grid=(chunks,),
            in_specs=[fixed((height, count))] * (chunks * heads),
            out_specs=pl.BlockSpec((1, heads, height, count), lambda k, m: (m[0] ^ k, 0, 0, 0)),
        ),
        out_shape=jax.ShapeDtypeStruct((chunks, heads, height, count), bf16),
        compiler_params=pltpu.CompilerParams(vmem_limit_bytes=VMEM),
        cost_estimate=pl.CostEstimate(
            flops=0, bytes_accessed=4 * chunks * heads * height * count, transcendentals=0
        ),
        name="assemble",
    )(me, *sources)


def tap_rows(cell_ref, frac_ref, live, plane, points):
    cell = cell_ref[0, plane : plane + 1, points]
    row = cell // (2 * G)
    col = cell - row * (2 * G)
    across = frac_ref[0, 2 * plane : 2 * plane + 1, points]
    downward = frac_ref[0, 2 * plane + 1 : 2 * plane + 2, points]
    half = lax.broadcasted_iota(jnp.int32, (G, cell.shape[1]), 0) * 2

    def spread(start, fraction, odd, gate):
        place = half + odd
        return jnp.where(
            place == start,
            (1.0 - fraction) * gate,
            jnp.where(place == start + 1, fraction * gate, 0.0),
        )

    return (
        [spread(row, downward, odd, live) for odd in range(2)],
        [spread(col, across, odd, 1.0) for odd in range(2)],
    )


def tap_table(table_ref, down, side):
    for ty in range(G):
        table_ref[ty * G : (ty + 1) * G, :] = lower(down[ty : ty + 1, :] * side)


def sample_kernel(object_ref, cell_ref, frac_ref, live_ref, plane_ref, out_ref, table_ref, picked_ref, *, width):
    turn = pl.program_id(1)
    lanes = pl.ds(pl.multiple_of(turn * width, width), width)
    live = jnp.concatenate([live_ref[0]] * (width // RB), axis=1)
    picked = jnp.zeros((CH, width), f32)
    slot = 0
    for plane in range(3):
        downs, sides = tap_rows(cell_ref, frac_ref, live, plane, lanes)
        for dy in range(2):
            for dx in range(2):
                tap_table(table_ref.at[slot], downs[dy], sides[dx])
                part = (2 * dy + dx) * CH
                features = plane_ref[0, part : part + CH, plane * PIX : (plane + 1) * PIX]
                picked = picked + dot(features, table_ref[slot], NN)
                slot = 1 - slot
    picked_ref[:, lanes] = picked

    @pl.when(turn == pl.num_programs(1) - 1)
    def _():
        for s in range(SAMP):
            out_ref[:, s * CH : (s + 1) * CH] = lower(picked_ref[:, s * RB : (s + 1) * RB].T)


def sample_points(planes, owners, cells, fractions, live):
    blocks = owners.shape[0]
    points = RB * SAMP
    width = 512
    return pl.pallas_call(
        functools.partial(sample_kernel, width=width),
        grid_spec=pltpu.PrefetchScalarGridSpec(
            num_scalar_prefetch=1,
            grid=(blocks, points // width),
            in_specs=[
                pl.BlockSpec((1, 3, points), lambda b, t, o: (b, 0, 0)),
                pl.BlockSpec((1, 6, points), lambda b, t, o: (b, 0, 0)),
                pl.BlockSpec((1, 1, RB), lambda b, t, o: (b, 0, 0)),
                pl.BlockSpec((1, 4 * CH, TOK_OBJ), lambda b, t, o: (o[b], 0, 0)),
            ],
            out_specs=pl.BlockSpec((RB, SAMP * CH), lambda b, t, o: (b, 0)),
            scratch_shapes=[
                pltpu.VMEM((2, PIX, width), bf16),
                pltpu.VMEM((CH, points), f32),
            ],
        ),
        out_shape=jax.ShapeDtypeStruct((blocks * RB, SAMP * CH), bf16),
        compiler_params=pltpu.CompilerParams(vmem_limit_bytes=VMEM),
        cost_estimate=pl.CostEstimate(
            flops=blocks * points * 3 * 4096 * 2 * 256,
            bytes_accessed=blocks * 5 * 2**20,
            transcendentals=0,
        ),
        name="sample_points",
    )(owners, cells, fractions, live, planes)


def scatter_kernel(object_ref, cell_ref, frac_ref, live_ref, grad_ref, out_ref, table_ref, rows_ref, total_ref, *, width):
    block = pl.program_id(0)
    turn = pl.program_id(1)
    owner = object_ref[block]

    @pl.when((block == 0) & (turn == 0))
    def _():
        total_ref[...] = jnp.zeros_like(total_ref)

    @pl.when(turn == 0)
    def _():
        for s in range(SAMP):
            rows_ref[:, s * RB : (s + 1) * RB] = grad_ref[:, s * CH : (s + 1) * CH].T

    lanes = pl.ds(pl.multiple_of(turn * width, width), width)
    live = jnp.concatenate([live_ref[0]] * (width // RB), axis=1)
    grads = rows_ref[:, lanes]
    slot = 0
    for plane in range(3):
        downs, sides = tap_rows(cell_ref, frac_ref, live, plane, lanes)
        for dy in range(2):
            for dx in range(2):
                tap_table(table_ref.at[slot], downs[dy], sides[dx])
                part = (2 * dy + dx) * CH
                total_ref[owner, part : part + CH, plane * PIX : (plane + 1) * PIX] += dot(
                    grads, table_ref[slot], NT
                )
                slot = 1 - slot

    @pl.when((block == pl.num_programs(0) - 1) & (turn == pl.num_programs(1) - 1))
    def _():
        out_ref[...] = lower(total_ref[...])


def scatter_points(grads, owners, cells, fractions, live, objects):
    blocks = owners.shape[0]
    points = RB * SAMP
    width = 512
    shape = (objects, 4 * CH, TOK_OBJ)
    return pl.pallas_call(
        functools.partial(scatter_kernel, width=width),
        grid_spec=pltpu.PrefetchScalarGridSpec(
            num_scalar_prefetch=1,
            grid=(blocks, points // width),
            in_specs=[
                pl.BlockSpec((1, 3, points), lambda b, t, o: (b, 0, 0)),
                pl.BlockSpec((1, 6, points), lambda b, t, o: (b, 0, 0)),
                pl.BlockSpec((1, 1, RB), lambda b, t, o: (b, 0, 0)),
                pl.BlockSpec((RB, SAMP * CH), lambda b, t, o: (b, 0)),
            ],
            out_specs=pl.BlockSpec(shape, lambda b, t, o: (0, 0, 0)),
            scratch_shapes=[
                pltpu.VMEM((2, PIX, width), bf16),
                pltpu.VMEM((CH, points), bf16),
                pltpu.VMEM(shape, f32),
            ],
        ),
        out_shape=jax.ShapeDtypeStruct(shape, bf16),
        compiler_params=pltpu.CompilerParams(vmem_limit_bytes=VMEM),
        cost_estimate=pl.CostEstimate(
            flops=blocks * points * 3 * 4096 * 2 * 256,
            bytes_accessed=blocks * 5 * 2**20,
            transcendentals=0,
        ),
        name="scatter_points",
    )(owners, cells, fractions, live, grads)


SWAP = [(0, 1), (1, 0)]


def body(
    dp_axes,
    group_axes,
    tokens,
    dino,
    first_gain,
    first_shift,
    image_weight,
    cross_query,
    cross_keyval,
    cross_output,
    second_gain,
    second_shift,
    self_project,
    self_output,
    third_gain,
    third_shift,
    hidden_weight,
    hidden_bias,
    output_weight,
    deconv_weight,
    ray_mask,
    block_object,
    sample_cell,
    sample_frac,
    out_grad,
    sampled_grad,
):
    shard_axes = ("h",) + group_axes
    every = dp_axes + shard_axes
    outer, core = dp_axes
    group = 2 ** len(group_axes)
    heads = H // group
    half = lax.axis_index("h")
    side = lax.axis_index(core)
    over = lax.axis_index(outer)
    place = lax.axis_index(group_axes)
    me = place.reshape(1).astype(jnp.int32)
    rows = tokens.shape[0]
    count = 2 * rows
    patches = 2 * dino.shape[0]
    share = first_gain.shape[0]
    join = lax.optimization_barrier

    def own_object(values):
        mine = lax.dynamic_index_in_dim(values, half, 1, keepdims=False)
        other = lax.dynamic_index_in_dim(values, 1 - half, 1, keepdims=False)
        got = lax.ppermute(other, "h", SWAP)
        return jnp.concatenate(
            [jnp.where(half == 0, mine, got), jnp.where(half == 0, got, mine)], axis=0
        )

    def both_objects(values):
        size = values.shape[0] // 2
        mine = lax.dynamic_slice_in_dim(values, half * size, size, 0)
        away = lower(lax.dynamic_slice_in_dim(values, (1 - half) * size, size, 0))
        got = lax.ppermute(away, "h", SWAP).astype(mine.dtype)
        return jnp.stack(
            [jnp.where(half == 0, mine, got), jnp.where(half == 0, got, mine)], axis=1
        )

    def gather(pieces):
        return lax.all_gather(jnp.concatenate(pieces, axis=1), every, axis=0, tiled=True)

    def exchange(chunks):
        return [chunks[0]] + [
            lax.ppermute(chunks[k], group_axes, [(i, i ^ k) for i in range(group)])
            for k in range(1, group)
        ]

    def exchange_all(parts):
        done = []
        for chunks in parts:
            if done:
                chunks, done[-1] = join((chunks, done[-1]))
            done.append(exchange(chunks))
        return done

    columns = jnp.stack(
        [first_gain, first_shift, second_gain, second_shift, third_gain, third_shift], axis=1
    )
    columns = jnp.concatenate([columns, hidden_bias.reshape(share, FF // D)], axis=1)
    columns = jnp.pad(columns, ((0, 0), (0, 128 - columns.shape[1])))
    early = gather(
        [
            lower(cross_query),
            lower(cross_keyval),
            lower(image_weight).reshape(share, DINO),
            lower(columns),
        ]
    )
    middle = gather([lower(cross_output), lower(self_project), lower(self_output)])
    late = gather([lower(hidden_weight), lower(deconv_weight)])
    output_w = lax.all_gather(lower(output_weight), every, axis=0, tiled=True)
    query_w = early[:, :D]
    keyval_w = early[:, D : 3 * D]
    image_w = early[:, 3 * D : 3 * D + DINO].reshape(DINO, D)
    vectors = widen(early[:, 3 * D + DINO :])
    gain_a, shift_a, gain_b, shift_b, gain_c, shift_c = [vectors[:, i] for i in range(6)]
    bias = vectors[:, 6 : 6 + FF // D].reshape(FF)
    cross_w = middle[:, :D]
    project_w = middle[:, D : 4 * D]
    self_w = middle[:, 4 * D :]
    hidden_w = late[:, :FF]
    deconv_w = late[:, FF:]

    blocks = ray_mask.shape[0] // RB

    def by_sample(values):
        kinds = values.shape[0]
        values = values.reshape(kinds, blocks, RB, SAMP)
        return values.transpose(1, 0, 3, 2).reshape(blocks, kinds, SAMP * RB)

    cells = by_sample(sample_cell)
    fractions = by_sample(sample_frac)
    live = widen(ray_mask).reshape(blocks, 1, RB)
    plane_grad = scatter_points(sampled_grad, block_object, cells, fractions, live, 2)
    token_low = own_object(tokens)
    dino_values = own_object(dino)
    plane_grad, token_low, dino_values = join((plane_grad, token_low, dino_values))
    out_cotangent = own_object(out_grad)
    parts = plane_grad.reshape(2, 4 * CH, 2, group, rows)
    parts = parts.transpose(0, 3, 1, 2, 4).reshape(2 * group * 4 * CH, count)
    plane_low = lax.psum_scatter(parts, shard_axes, scatter_dimension=0, tiled=True)
    token_values = widen(token_low)

    normed_full, unit_a, inverse_a = normalize(token_values, gain_a, shift_a)
    normed_a = lower(normed_full)
    image = lower(dot(dino_values, image_w, NN))
    queries = lower(dot(query_w, normed_a, ((0,), (1,)))).reshape(group, heads, HD, count)
    keyvals = lower(dot(keyval_w, image, ((0,), (1,)))).reshape(group, heads, 2 * HD, patches)
    queries, keyvals = split(queries, me), split(keyvals, me)
    sent = exchange_all([list(zip(queries[j], keyvals[j])) for j in range(heads)])
    cross_q = [[c[0] for c in x] for x in sent]
    cross_kv = [[c[1] for c in x] for x in sent]
    cross_out = [attend_forward(q, kv) for q, kv in zip(cross_q, cross_kv)]
    cross_mix = assemble([exchange(o) for o, _ in cross_out], me).reshape(D, count)
    after_cross = token_values + dot(cross_mix, cross_w, TN)

    normed_full, unit_b, inverse_b = normalize(after_cross, gain_b, shift_b)
    normed_b = lower(normed_full)
    projected = lower(dot(project_w, normed_b, ((0,), (1,)))).reshape(group, heads, 3 * HD, count)
    self_qkv = exchange_all(split(projected, me))
    self_out = [attend_forward(x, None) for x in self_qkv]
    self_mix = assemble([exchange(o) for o, _ in self_out], me).reshape(D, count)
    after_self = after_cross + dot(self_mix, self_w, TN)

    normed_full, unit_c, inverse_c = normalize(after_self, gain_c, shift_c)
    normed_c = lower(normed_full)
    hidden = dot(normed_c, hidden_w, NN) + bias
    activated = lower(gelu(hidden))
    result_low = lower(after_self + dot(activated, output_w, NN))
    tokens_out = both_objects(result_low)

    planes = lower(dot(deconv_w, result_low, ((0,), (1,))))
    plane_all = lax.all_gather(planes, shard_axes, axis=0, tiled=True)
    plane_all = plane_all.reshape(2, group, 4 * CH, 2, rows).transpose(0, 2, 3, 1, 4)
    plane_all = plane_all.reshape(2, 4 * CH, TOK_OBJ)

    def dp_grad(left, axis, right, right_axis):
        quarter = left.shape[axis] // 4
        dims = ((1 - axis,), (right_axis,))

        def block(y, c):
            part = lax.dynamic_slice_in_dim(left, (2 * y + c) * quarter, quarter, axis)
            return dot(part, right, dims)

        def chip(y):
            away = lower(block(y, 1 - side))
            return block(y, side) + widen(lax.ppermute(away, core, SWAP))

        other = lower(chip(1 - over))
        return lower(chip(over) + widen(lax.ppermute(other, outer, SWAP)))

    def scatter_sum(values):
        return widen(lax.psum_scatter(values, shard_axes, scatter_dimension=0, tiled=True))

    result_grad = widen(out_cotangent) + dot(plane_low, deconv_w, ((0,), (1,)))
    result_low_grad = lower(result_grad)
    activated_grad = dot(result_low_grad, output_w, NT)
    _, gelu_pull = jax.vjp(gelu, hidden)
    hidden_grad = lower(gelu_pull(activated_grad)[0])
    bias_grad = jnp.sum(widen(hidden_grad), axis=0)
    output_part = dp_grad(activated, 1, result_low_grad, 0)
    hidden_part = dp_grad(normed_c, 1, hidden_grad, 0)
    back_c, gain_c_grad, shift_c_grad = normalize_back(
        dot(hidden_grad, hidden_w, NT), unit_c, inverse_c, gain_c
    )
    self_grad = result_grad + back_c

    self_low = lower(self_grad)
    self_part = jnp.concatenate(
        [dp_grad(self_mix, 0, self_low, 0), dp_grad(result_low, 1, plane_low, 1)], axis=1
    )
    self_mix_grad = lower(dot(self_w, self_low, NT)).reshape(group, heads, HD, count)
    self_dout = exchange_all(split(self_mix_grad, me))
    self_dout[0], output_part, hidden_part, self_part = join(
        (self_dout[0], output_part, hidden_part, self_part)
    )
    output_weight_grad = scatter_sum(output_part)
    hidden_weight_grad = scatter_sum(hidden_part)
    self_sum = scatter_sum(self_part)
    self_back = [
        attend_backward(self_qkv[j], None, self_dout[j], *self_out[j])[0] for j in range(heads)
    ]
    project_grad = assemble([exchange(g) for g in self_back], me).reshape(3 * D, count)
    back_b, gain_b_grad, shift_b_grad = normalize_back(
        dot(project_grad, project_w, ((0,), (1,))), unit_b, inverse_b, gain_b
    )
    cross_grad = self_grad + back_b

    cross_low = lower(cross_grad)
    cross_mix_grad = lower(dot(cross_w, cross_low, NT)).reshape(group, heads, HD, count)
    cross_dout = exchange_all(split(cross_mix_grad, me))
    project_part = dp_grad(normed_b, 1, project_grad, 1)
    cross_part = dp_grad(cross_mix, 0, cross_low, 0)
    cross_dout[-1], project_part, cross_part = join((cross_dout[-1], project_part, cross_part))
    project_weight_grad = scatter_sum(project_part)
    cross_back = [
        attend_backward(cross_q[j], cross_kv[j], cross_dout[j], *cross_out[j])
        for j in range(heads)
    ]
    query_parts = [exchange(g) for g, _ in cross_back]
    keyval_parts = [exchange(g) for _, g in cross_back]
    query_back = assemble(query_parts, me).reshape(D, count)
    keyval_back = assemble(keyval_parts, me).reshape(2 * D, patches)
    image_grad = lower(dot(keyval_back, keyval_w, ((0,), (1,))))
    keyval_part = dp_grad(image, 1, keyval_back, 1)
    image_part = dp_grad(dino_values, 1, image_grad, 0)
    query_part = dp_grad(normed_a, 1, query_back, 1)
    back_a, gain_a_grad, shift_a_grad = normalize_back(
        dot(query_back, query_w, ((0,), (1,))), unit_a, inverse_a, gain_a
    )
    dino_grad = both_objects(dot(image_grad, image_w, NT))
    tokens_grad = both_objects(cross_grad + back_a)

    sums = jnp.stack(
        [gain_a_grad, shift_a_grad, gain_b_grad, shift_b_grad, gain_c_grad, shift_c_grad], axis=1
    )
    sums = jnp.concatenate([sums, bias_grad.reshape(D, FF // D)], axis=1)
    sums = jnp.pad(sums, ((0, 0), (0, 128 - sums.shape[1])))

    def quarter_rows(y, c):
        return lax.dynamic_slice_in_dim(sums, (2 * y + c) * (D // 4), D // 4, 0)

    def chip_rows(y):
        return quarter_rows(y, side) + lax.ppermute(quarter_rows(y, 1 - side), core, SWAP)

    vector_part = lower(chip_rows(over) + lax.ppermute(chip_rows(1 - over), outer, SWAP))
    last_part = jnp.concatenate([cross_part, keyval_part, query_part, vector_part], axis=1)
    last = scatter_sum(last_part)
    image_sum = scatter_sum(image_part)
    vector_sums = last[:, 4 * D :]

    late_cells, _ = join((cells, (keyval_part, image_part, query_part)))
    sampled = sample_points(plane_all, block_object, late_cells, fractions, live)

    return (
        tokens_out,
        sampled,
        tokens_grad,
        dino_grad,
        vector_sums[:, 0],
        vector_sums[:, 1],
        image_sum,
        last[:, 3 * D : 4 * D],
        last[:, D : 3 * D],
        last[:, :D],
        vector_sums[:, 2],
        vector_sums[:, 3],
        project_weight_grad,
        self_sum[:, :D],
        vector_sums[:, 4],
        vector_sums[:, 5],
        hidden_weight_grad,
        vector_sums[:, 6 : 6 + FF // D].reshape(share * (FF // D)),
        output_weight_grad,
        self_sum[:, D:],
    )


def solution(mesh):
    dp_bits = mesh.shape["dp"].bit_length() - 1
    shard_bits = mesh.shape["shard"].bit_length() - 1
    dp_axes = tuple(f"d{i}" for i in range(dp_bits))
    group_axes = tuple(f"r{i}" for i in range(shard_bits - 1))
    shard_axes = ("h",) + group_axes
    fine = Mesh(mesh.devices.reshape((2,) * (dp_bits + shard_bits)), dp_axes + shard_axes)
    every = dp_axes + shard_axes
    rows = P(shard_axes, dp_axes, None)
    vector = P(every)
    matrix = P(every, None)
    points = P(None, every)
    return jax.shard_map(
        functools.partial(body, dp_axes, group_axes),
        mesh=fine,
        in_specs=(
            rows, rows,
            vector, vector, matrix, matrix, matrix, matrix,
            vector, vector, matrix, matrix,
            vector, vector, matrix, vector, matrix, matrix,
            vector, vector, points, points, rows, matrix,
        ),
        out_specs=(
            rows, matrix, rows, rows,
            vector, vector, matrix, matrix, matrix, matrix,
            vector, vector, matrix, matrix,
            vector, vector, matrix, vector, matrix, matrix,
        ),
        check_vma=False,
    )
```

time: 4510 us -> 1500 us (0.33)
  matrix products: 1810 us -> 221 us
  waiting for transfers between devices: 1340 us -> 370 us
  Pallas kernels: 0 us -> 523 us
  other arithmetic: 554 us -> 62.4 us
  local copies, waits for them, and re-layouts: 407 us -> 118 us
  blocking collectives: 246 us -> 0 us
  starting transfers between devices: 47.4 us -> 175 us
  loops' own time: 66.6 us -> 0 us
    dot_general x207 -> x54, matrix products: 1810 us -> 221 us  [dot(): lax.dot_general(left, right, (dims, ((), ())), preferred_element_type=f32)]
    reduce_scatter x9 -> x7, waiting for transfers between devices: 717 us -> 22 us  [the longest x6 22 us: scatter_sum(): lax.psum_scatter(values, shard_axes, scatter_dimension=0, tiled=True)]
    all_to_all x10 -> x0, waiting for transfers between devices: 623 us -> none  [the longest x1 142 us: body(): lax.all_to_all(projected.reshape(rows, members, local_pairs, 3 * HD), 'sh...]
    pallas_call x0 -> x28, Pallas kernels: none -> 523 us  [the longest x8 231 us: attend_backward(): pl.pallas_call(functools.partial(backward_kernel, chunks=chunks, block=bl...]
    ppermute x0 -> x156, waiting for transfers between devices: none -> 340 us  [the longest x120 177 us: exchange(): lax.ppermute(chunks[k], group_axes, [(i, i ^ k) for i in range(group)])]
    convert_element_type x147 -> x26, other arithmetic: 324 us -> 35.7 us  [the longest x19 26.5 us: lower(): return value.astype(bf16)]
    ppermute x0 -> x156, starting transfers between devices: none -> 174 us  [the longest x120 137 us: exchange(): lax.ppermute(chunks[k], group_axes, [(i, i ^ k) for i in range(group)])]
    all_gather x2 -> x0, blocking collectives: 159 us -> none  [the longest x1 91.1 us: body(): lax.all_gather(lower(hidden_bias), ('dp', 'shard'), axis=0, tiled=True)]
  transfers between devices with their start and end apart: 29 -> 168, of which waited for: 12 -> 44; matrix products, arithmetic and copies ran while one was open for 60% -> 22% of each run, Pallas kernels for 0% -> 35%
where the time goes in v1:
time: 1500 us; the launch traced here: 1490 us
  Pallas kernels  523 us (35%)
  waiting for transfers between devices  370 us (25%)
  matrix products  221 us (15%)
  starting transfers between devices  175 us (12%)
  local copies, waits for them, and re-layouts  118 us (8%)
  other arithmetic  62.4 us (4%)
  between operations  18.4 us (1%)
    pallas_call x8, Pallas kernels, attend_backward(): pl.pallas_call(functools.partial(backward_kernel, chunks=chunks, block=bl...  231 us
    dot_general x54, matrix products, dot(): lax.dot_general(left, right, (dims, ((), ())), preferred_element_type=f32)  221 us
    ppermute x120, waiting for transfers between devices, exchange(): lax.ppermute(chunks[k], group_axes, [(i, i ^ k) for i in range(group)])  177 us
    ppermute x120, starting transfers between devices, exchange(): lax.ppermute(chunks[k], group_axes, [(i, i ^ k) for i in range(group)])  137 us
    pallas_call x8, Pallas kernels, attend_forward(): pl.pallas_call(functools.partial(forward_kernel, chunks=chunks, block=blo...  133 us
    ppermute x9, waiting for transfers between devices, dp_grad(): return lower(chip(over) + widen(lax.ppermute(other, outer, SWAP)))  84.6 us
    ppermute x3, waiting for transfers between devices, both_objects(): got = lax.ppermute(away, 'h', SWAP).astype(mine.dtype)  78.9 us
    pallas_call x1, Pallas kernels, scatter_points(): pl.pallas_call(functools.partial(scatter_kernel, width=width), grid_spec=...  72.2 us
  transfers between devices with their start and end apart: 168, of which 44 were waited for; matrix products, arithmetic and copies ran while one was open for 22% of the time, Pallas kernels for 35%

profile of v1, /device:TPU:0, one launch (start us, length us, event | category | flops | bytes accessed | tf_op | source)
XLA Modules:
  0.0 1486.6 jit_solution(17877295647074586768)
XLA Ops:
  21.0 9.0 constant_dynamic-slice_fusion.1
  47.3 72.2 %scatter_points.1 = bf16[2,320,3072]{2,1,0:T(8,128)(2,1)} custom-call(s32[2]{0:T(128)} %object_ref.3, s32[2,3,4096]{2,1,0:T(4,128)} %copy.157.cell_ref, f32[2,6,4096]{2,1,0:T(8,128)} %reshape.208.frac_ref, f32[2,1,128]{2,1,0:T(1,128)} %bitcast.188, bf16[256,2560]{1,0:T(8,128)(2,1)} %grad_ref.1), custom_call_target="tpu_custom_call" | custom-call | flops 51539607552 | bytes 10485760 | tf_op jit(solution)/shard_map/scatter_points/pallas_call | solution.py:444
  124.4 8.1 reshape.197
  132.5 5.1 copy.171
  143.9 7.1 all-gather.6.cloned.1.call-done
  164.2 9.3 convolution_convert_fusion.4
  182.9 5.2 fusion.55
  194.3 7.7 collective-permute-done.2.refs_1_
  219.5 15.9 %collective-permute-done.10.refs_2_ = bf16[64,768]{1,0:T(8,128)(2,1)S(1)} collective-permute-done((bf16[64,768]{1,0:T(8,128)(2,1)}, bf16[64,768]{1,0:T(8,128)(2,1)S(1)}, u32[]{:S(2)}, u32[]{:S(2)}) %collective-permute-start.10) | collective-permute-done | bytes 98336 | tf_op jit(solution)/shard_map/ppermute | solution.py:542
  236.3 6.6 collective-permute-done.12.refs_3_
  252.5 18.5 %attend_forward.8 = (bf16[64,768]{1,0:T(8,128)(2,1)}, bf16[64,768]{1,0:T(8,128)(2,1)}, bf16[64,768]{1,0:T(8,128)(2,1)}, bf16[64,768]{1,0:T(8,128)(2,1)}, f32[4,1,768]{2,1,0:T(1,128)}) custom-call(bf16[64,768]{1,0:T(8,128)(2,1)} %get-tuple-element.343.refs_0_, bf16[64,768]{1,0:T(8,128)(2,1)} %copy-done.175, bf16[64,768]{1,0:T(8,128)(2,1)} %copy-done.177, ...), custom_call_target="tpu_custom_call" | custom-call | flops 12884901888 | bytes 1048576 | tf_op jit(solution)/shard_map/attend_forward/pallas_call | solution.py:131
  271.1 10.2 collective-permute-done.16.refs_2_
  288.9 18.8 %attend_forward.9 = (bf16[64,768]{1,0:T(8,128)(2,1)}, bf16[64,768]{1,0:T(8,128)(2,1)}, bf16[64,768]{1,0:T(8,128)(2,1)}, bf16[64,768]{1,0:T(8,128)(2,1)}, f32[4,1,768]{2,1,0:T(1,128)}) custom-call(bf16[64,768]{1,0:T(8,128)(2,1)} %get-tuple-element.368.refs_0_, bf16[64,768]{1,0:T(8,128)(2,1)} %copy-done.178, bf16[64,768]{1,0:T(8,128)(2,1)} %copy-done.174, ...), custom_call_target="tpu_custom_call" | custom-call | flops 12884901888 | bytes 1048576 | tf_op jit(solution)/shard_map/attend_forward/pallas_call | solution.py:131
  314.3 18.7 %attend_forward.10 = (bf16[64,768]{1,0:T(8,128)(2,1)}, bf16[64,768]{1,0:T(8,128)(2,1)}, bf16[64,768]{1,0:T(8,128)(2,1)}, bf16[64,768]{1,0:T(8,128)(2,1)}, f32[4,1,768]{2,1,0:T(1,128)}) custom-call(bf16[64,768]{1,0:T(8,128)(2,1)} %get-tuple-element.393.refs_0_, bf16[64,768]{1,0:T(8,128)(2,1)} %copy-done.171, bf16[64,768]{1,0:T(8,128)(2,1)} %copy-done.172, ...), custom_call_target="tpu_custom_call" | custom-call | flops 12884901888 | bytes 1048576 | tf_op jit(solution)/shard_map/attend_forward/pallas_call | solution.py:131
  335.0 5.7 collective-permute-done.22.refs_3_
  345.1 18.3 %attend_forward.11 = (bf16[64,768]{1,0:T(8,128)(2,1)}, bf16[64,768]{1,0:T(8,128)(2,1)}, bf16[64,768]{1,0:T(8,128)(2,1)}, bf16[64,768]{1,0:T(8,128)(2,1)}, f32[4,1,768]{2,1,0:T(1,128)}) custom-call(bf16[64,768]{1,0:T(8,128)(2,1)} %get-tuple-element.402.refs_0_, bf16[64,768]{1,0:T(8,128)(2,1)} %copy-done.168, bf16[64,768]{1,0:T(8,128)(2,1)} %copy-done.169, ...), custom_call_target="tpu_custom_call" | custom-call | flops 12884901888 | bytes 1048576 | tf_op jit(solution)/shard_map/attend_forward/pallas_call | solution.py:131
  371.7 12.5 collective-permute-done.36.refs_14_
  401.0 6.9 fusion.8
  407.9 5.5 split.7
  418.9 5.7 collective-permute-done.38.refs_1_
  426.8 8.2 collective-permute-done.40.refs_3_
  438.6 14.5 attend_forward.12
  453.7 6.4 collective-permute-done.43.refs_3_
  463.7 14.7 attend_forward.13
  478.4 6.4 collective-permute-done.46.refs_3_
  488.4 14.5 attend_forward.14
  511.4 14.6 attend_forward.15
  548.8 9.0 fusion.2
  557.8 18.0 %convert_reduce_fusion = (f32[4096]{0:T(1024)}, bf16[768,4096]{1,0:T(8,128)(2,1)S(1)}, bf16[768,4096]{1,0:T(8,128)(2,1)}) fusion(f32[768,4096]{1,0:T(8,128)} %fusion.2, f32[4096]{0:T(1024)S(1)} %add.356, bf16[768,1024]{1,0:T(8,128)(2,1)} %get-tuple-element.785, bf16[4096,1024]{1,0:T(8,128)(2,1)} %all-gather.12.cloned.1.call-done), kind=kOutput, calls=%fused_computation | convolution fusion | flops 6499069952 | bytes 35160064 | tf_op jit(solution)/shard_map/dot_general | solution.py:43
  575.8 14.0 multiply_reduce_fusion
  618.1 5.3 fusion.74
  627.0 9.5 add_convert_fusion.5
  644.7 7.7 collective-permute-start.72
  668.2 34.4 %collective-permute-done.78 = bf16[256,320]{0,1:T(8,128)(2,1)S(1)} collective-permute-done((bf16[256,320]{0,1:T(8,128)(2,1)S(1)}, bf16[256,320]{0,1:T(8,128)(2,1)S(1)}, u32[]{:S(2)}, u32[]{:S(2)}) %collective-permute-start.78) | collective-permute-done | bytes 163872 | tf_op jit(solution)/shard_map/ppermute | solution.py:648
  705.2 8.7 collective-permute-done.75
  716.8 5.8 add_convert_fusion.1
  722.6 36.0 %collective-permute-done.69 = bf16[1024,1024]{1,0:T(8,128)(2,1)} collective-permute-done((bf16[1024,1024]{1,0:T(8,128)(2,1)}, bf16[1024,1024]{1,0:T(8,128)(2,1)}, u32[]{:S(2)}, u32[]{:S(2)}) %collective-permute-start.69) | collective-permute-done | bytes 2097184 | tf_op jit(solution)/shard_map/ppermute | solution.py:648
  758.7 6.0 add_convert_fusion.3
  779.3 25.0 %attend_backward.9 = (bf16[192,768]{1,0:T(8,128)(2,1)}, bf16[192,768]{1,0:T(8,128)(2,1)}, bf16[192,768]{1,0:T(8,128)(2,1)}, bf16[192,768]{1,0:T(8,128)(2,1)}) custom-call(bf16[192,768]{1,0:T(8,128)(2,1)} %get-tuple-element.444.refs_0_, bf16[192,768]{1,0:T(8,128)(2,1)} %copy-done.130, bf16[192,768]{1,0:T(8,128)(2,1)} %copy-done.131, ...), custom_call_target="tpu_custom_call" | custom-call | flops 18874368000 | bytes 1572864 | tf_op jit(solution)/shard_map/attend_backward/pallas_call | solution.py:240
  810.0 25.0 %attend_backward.10 = (bf16[192,768]{1,0:T(8,128)(2,1)}, bf16[192,768]{1,0:T(8,128)(2,1)}, bf16[192,768]{1,0:T(8,128)(2,1)}, bf16[192,768]{1,0:T(8,128)(2,1)}) custom-call(bf16[192,768]{1,0:T(8,128)(2,1)} %get-tuple-element.457.refs_0_, bf16[192,768]{1,0:T(8,128)(2,1)} %copy-done.127, bf16[192,768]{1,0:T(8,128)(2,1)} %copy-done.128, ...), custom_call_target="tpu_custom_call" | custom-call | flops 18874368000 | bytes 1572864 | tf_op jit(solution)/shard_map/attend_backward/pallas_call | solution.py:240
  838.5 25.0 %attend_backward.11 = (bf16[192,768]{1,0:T(8,128)(2,1)}, bf16[192,768]{1,0:T(8,128)(2,1)}, bf16[192,768]{1,0:T(8,128)(2,1)}, bf16[192,768]{1,0:T(8,128)(2,1)}) custom-call(bf16[192,768]{1,0:T(8,128)(2,1)} %get-tuple-element.462.refs_0_, bf16[192,768]{1,0:T(8,128)(2,1)} %copy-done.124, bf16[192,768]{1,0:T(8,128)(2,1)} %copy-done.125, ...), custom_call_target="tpu_custom_call" | custom-call | flops 18874368000 | bytes 1572864 | tf_op jit(solution)/shard_map/attend_backward/pallas_call | solution.py:240
  865.7 25.2 %attend_backward.8 = (bf16[192,768]{1,0:T(8,128)(2,1)}, bf16[192,768]{1,0:T(8,128)(2,1)}, bf16[192,768]{1,0:T(8,128)(2,1)}, bf16[192,768]{1,0:T(8,128)(2,1)}) custom-call(bf16[192,768]{1,0:T(8,128)(2,1)} %get-tuple-element.431.refs_0_, bf16[192,768]{1,0:T(8,128)(2,1)} %copy-done.123, bf16[192,768]{1,0:T(8,128)(2,1)} %collective-permute-done.39.refs_2_, ...), custom_call_target="tpu_custom_call" | custom-call | flops 18874368000 | bytes 1572864 | tf_op jit(solution)/shard_map/attend_backward/pallas_call | solution.py:240
  897.5 6.0 collective-permute-done.95.refs_11_
  903.5 17.2 %collective-permute-done.99.refs_15_ = bf16[192,768]{1,0:T(8,128)(2,1)S(1)} collective-permute-done((bf16[192,768]{1,0:T(8,128)(2,1)S(1)}, bf16[192,768]{1,0:T(8,128)(2,1)S(1)}, u32[]{:S(2)}, u32[]{:S(2)}) %collective-permute-start.99) | collective-permute-done | bytes 294944 | tf_op jit(solution)/shard_map/ppermute | solution.py:542
  920.7 5.9 collective-permute-done.92.refs_8_
  931.5 5.2 assemble.7
  944.4 8.9 multiply_reduce_fusion.1
  976.0 32.5 %attend_backward.12 = (bf16[64,768]{1,0:T(8,128)(2,1)}, bf16[64,768]{1,0:T(8,128)(2,1)}, bf16[64,768]{1,0:T(8,128)(2,1)}, bf16[64,768]{1,0:T(8,128)(2,1)}, bf16[...) custom-call(bf16[64,768]{1,0:T(8,128)(2,1)} %get-tuple-element.343.refs, ...), custom_call_target="tpu_custom_call" | custom-call | flops 25165824000 | bytes 2097152 | tf_op jit(solution)/shard_map/attend_backward/pallas_call | solution.py:240
  1012.2 32.5 %attend_backward.13 = (bf16[64,768]{1,0:T(8,128)(2,1)}, bf16[64,768]{1,0:T(8,128)(2,1)}, bf16[64,768]{1,0:T(8,128)(2,1)}, bf16[64,768]{1,0:T(8,128)(2,1)}, bf16[...) custom-call(bf16[64,768]{1,0:T(8,128)(2,1)} %get-tuple-element.368.refs, ...), custom_call_target="tpu_custom_call" | custom-call | flops 25165824000 | bytes 2097152 | tf_op jit(solution)/shard_map/attend_backward/pallas_call | solution.py:240
  1048.5 5.5 fusion.13
  1054.2 32.6 %attend_backward.14 = (bf16[64,768]{1,0:T(8,128)(2,1)}, bf16[64,768]{1,0:T(8,128)(2,1)}, bf16[64,768]{1,0:T(8,128)(2,1)}, bf16[64,768]{1,0:T(8,128)(2,1)}, bf16[...) custom-call(bf16[64,768]{1,0:T(8,128)(2,1)} %get-tuple-element.393.refs, ...), custom_call_target="tpu_custom_call" | custom-call | flops 25165824000 | bytes 2097152 | tf_op jit(solution)/shard_map/attend_backward/pallas_call | solution.py:240
  1095.9 6.0 fusion.12
  1108.5 32.8 %attend_backward.15 = (bf16[64,768]{1,0:T(8,128)(2,1)}, bf16[64,768]{1,0:T(8,128)(2,1)}, bf16[64,768]{1,0:T(8,128)(2,1)}, bf16[64,768]{1,0:T(8,128)(2,1)}, bf16[...) custom-call(bf16[64,768]{1,0:T(8,128)(2,1)} %get-tuple-element.402.refs, ...), custom_call_target="tpu_custom_call" | custom-call | flops 25165824000 | bytes 2097152 | tf_op jit(solution)/shard_map/attend_backward/pallas_call | solution.py:240
  1150.9 5.9 collective-permute-done.128.refs_14_
  1169.8 8.0 fusion.35
  1203.7 23.8 %collective-permute-done.62 = bf16[384,1024]{1,0:T(8,128)(2,1)} collective-permute-done((bf16[384,1024]{1,0:T(8,128)(2,1)S(1)}, bf16[384,1024]{1,0:T(8,128)(2,1)}, u32[]{:S(2)}, u32[]{:S(2)}) %collective-permute-start.62) | collective-permute-done | bytes 786464 | tf_op jit(solution)/shard_map/ppermute | solution.py:532
  1246.9 8.6 reshape.204
  1255.5 9.1 copy.213
  1264.7 7.4 reshape.205.plane_ref
  1282.2 5.7 fusion.29
  1323.8 46.6 %collective-permute-done.151 = bf16[384,1024]{1,0:T(8,128)(2,1)} collective-permute-done((bf16[384,1024]{1,0:T(8,128)(2,1)}, bf16[384,1024]{1,0:T(8,128)(2,1)}, u32[]{:S(2)}, u32[]{:S(2)}) %collective-permute-start.151) | collective-permute-done | bytes 786464 | tf_op jit(solution)/shard_map/ppermute | solution.py:532
  1378.1 8.5 collective-permute-done.152
  1403.3 45.9 %sample_points.1 = bf16[256,2560]{1,0:T(8,128)(2,1)} custom-call(s32[2]{0:T(128)} %object_ref.3, s32[2,3,4096]{2,1,0:T(4,128)} %copy.174.cell_ref, f32[2,6,4096]{2,1,0:T(8,128)} %reshape.208.frac_ref, f32[2,1,128]{2,1,0:T(1,128)} %bitcast.189, bf16[2,320,3072]{2,1,0:T(8,128)(2,1)} %reshape.205.plane_ref), custom_call_target="tpu_custom_call" | custom-call | flops 51539607552 | bytes 10485760 | tf_op jit(solution)/shard_map/sample_points/pallas_call | solution.py:377
  1450.9 22.0 %reduce-scatter.10.cloned.1.call-done = bf16[32,4224]{1,0:T(8,128)(2,1)} async-done(((bf16[256,4224]{1,0:T(8,128)(2,1)}), bf16[32,4224]{1,0:T(8,128)(2,1)}) %reduce-scatter.10.cloned.1.call-update) | async-done | bytes 270352 | tf_op jit(solution)/shard_map/reduce_scatter | solution.py:651
  (981 shorter events, 490.4 us)
Async XLA Ops:
  8.0 143.0 %all-gather.6.cloned.1.call-start = ((), (), s32[]{:S(2)}) async-start(), calls=%async_computation.7 | async-start | bytes 8380416 | tf_op jit(solution)/shard_map/all_gather | solution.py:538
  17.2 376.6 %all-gather.8.cloned.1.call-start = ((), (), s32[]{:S(2)}) async-start(), calls=%async_computation.8 | async-start | bytes 10813440 | tf_op jit(solution)/shard_map/all_gather | solution.py:538
  20.9 511.5 %reduce-scatter.8.cloned.1.call-start = ((), (), s32[]{:S(2)}) async-start(), calls=%async_computation.11 | async-start | bytes 4423680 | tf_op jit(solution)/shard_map/reduce_scatter | solution.py:599
  31.1 88.4 %collective-permute-start = (bf16[384,1024]{1,0:T(8,128)(2,1)}, bf16[384,1024]{1,0:T(8,128)(2,1)}, u32[]{:S(2)}, u32[]{:S(2)}) collective-permute-start(bf16[384,1024]{1,0:T(8,128)(2,1)} %bitcast.141), channel_id=1, source_target_pairs={{0,4},{4,0},{1,5},{5,1},{2,6},{6,2},{3,7},{7,3},{8,12},{12,8},{9,1... | collective-permute-start | bytes 2359304 | tf_op jit(solution)/shard_map/ppermute | solution.py:523
  39.4 81.7 %collective-permute-start.1 = (bf16[512,768]{1,0:T(8,128)(2,1)}, bf16[512,768]{1,0:T(8,128)(2,1)}, u32[]{:S(2)}, u32[]{:S(2)}) collective-permute-start(bf16[512,768]{1,0:T(8,128)(2,1)} %bitcast.140), channel_id=1, source_target_pairs={{0,4},{4,0},{1,5},{5,1},{2,6},{6,2},{3,7},{7,3},{8,12},{12,8},{9,1... | collective-permute-start | bytes 2359304 | tf_op jit(solution)/shard_map/ppermute | solution.py:523
  140.3 392.1 %all-gather.10.cloned.1.call-start = ((), (), s32[]{:S(2)}) async-start(), calls=%async_computation.9 | async-start | bytes 9461760 | tf_op jit(solution)/shard_map/all_gather | solution.py:538
  142.2 415.6 %all-gather.12.cloned.1.call-start = ((), (), s32[]{:S(2)}) async-start(), calls=%async_computation.10 | async-start | bytes 8650752 | tf_op jit(solution)/shard_map/all_gather | solution.py:569
  143.0 1101.1 %reduce-scatter.16.cloned.1.call-start = ((), (), s32[]{:S(2)}) async-start(), calls=%async_computation.16 | async-start | bytes 811008 | tf_op jit(solution)/shard_map/reduce_scatter | solution.py:651
  178.6 34.7 %collective-permute-start.3 = (bf16[128,1024]{1,0:T(8,128)(2,1)}, bf16[128,1024]{1,0:T(8,128)(2,1)S(1)}, u32[]{:S(2)}, u32[]{:S(2)}) collective-permute-start(bf16[128,1024]{1,0:T(8,128)(2,1)} %get-tuple-element.338), channel_id=1, source_target_pairs={{0,1},{1,0},{2,3},{3,2},{4,5},{5,4},{6,7},{7,6},{8,9},{9,8},{10,11... | collective-permute-start | bytes 786440 | tf_op jit(solution)/shard_map/ppermute | solution.py:542
  245.9 42.6 %collective-permute-start.15 = (bf16[128,1024]{1,0:T(8,128)(2,1)S(1)}, bf16[128,1024]{1,0:T(8,128)(2,1)S(1)}, u32[]{:S(2)}, u32[]{:S(2)}) collective-permute-start(bf16[128,1024]{1,0:T(8,128)(2,1)S(1)} %copy-done.164), channel_id=1, source_target_pairs={{0,1},{1,0},{2,3},{3,2},{4,5},{5,4},{6,7},{7,6},{8,9},{9,8},{10,11... | collective-permute-start | bytes 786440 | tf_op jit(solution)/shard_map/ppermute | solution.py:542
  246.0 42.5 %collective-permute-start.17 = (bf16[128,1024]{1,0:T(8,128)(2,1)S(1)}, bf16[128,1024]{1,0:T(8,128)(2,1)S(1)}, u32[]{:S(2)}, u32[]{:S(2)}) collective-permute-start(bf16[128,1024]{1,0:T(8,128)(2,1)S(1)} %copy-done.163), channel_id=1, source_target_pairs={{0,2},{1,3},{2,0},{3,1},{4,6},{5,7},{6,4},{7,5},{8,10},{9,11},{10,... | collective-permute-start | bytes 786440 | tf_op jit(solution)/shard_map/ppermute | solution.py:542
  246.1 42.4 %collective-permute-start.19 = (bf16[128,1024]{1,0:T(8,128)(2,1)S(1)}, bf16[128,1024]{1,0:T(8,128)(2,1)S(1)}, u32[]{:S(2)}, u32[]{:S(2)}) collective-permute-start(bf16[128,1024]{1,0:T(8,128)(2,1)S(1)} %copy-done.162), channel_id=1, source_target_pairs={{0,3},{1,2},{2,1},{3,0},{4,7},{5,6},{6,5},{7,4},{8,11},{9,10},{10,... | collective-permute-start | bytes 786440 | tf_op jit(solution)/shard_map/ppermute | solution.py:542
  251.9 36.6 %collective-permute-start.18 = (bf16[64,768]{1,0:T(8,128)(2,1)}, bf16[64,768]{1,0:T(8,128)(2,1)S(1)}, u32[]{:S(2)}, u32[]{:S(2)}) collective-permute-start(bf16[64,768]{1,0:T(8,128)(2,1)} %get-tuple-element.391), channel_id=1, source_target_pairs={{0,3},{1,2},{2,1},{3,0},{4,7},{5,6},{6,5},{7,4},{8,11},{9,10},{10,... | collective-permute-start | bytes 294920 | tf_op jit(solution)/shard_map/ppermute | solution.py:542
  371.6 45.3 %collective-permute-start.63 = (bf16[384,1024]{1,0:T(8,128)(2,1)S(1)}, bf16[384,1024]{1,0:T(8,128)(2,1)}, u32[]{:S(2)}, u32[]{:S(2)}) collective-permute-start(bf16[384,1024]{1,0:T(8,128)(2,1)S(1)} %bitcast.179), channel_id=1, source_target_pairs={{0,4},{4,0},{1,5},{5,1},{2,6},{6,2},{3,7},{7,3},{8,12},{12,8},{9,1... | collective-permute-start | bytes 2359304 | tf_op jit(solution)/shard_map/ppermute | solution.py:523
  453.1 49.9 %collective-permute-start.50 = (bf16[64,768]{1,0:T(8,128)(2,1)}, bf16[64,768]{1,0:T(8,128)(2,1)S(1)}, u32[]{:S(2)}, u32[]{:S(2)}) collective-permute-start(bf16[64,768]{1,0:T(8,128)(2,1)} %get-tuple-element.467.refs_9_), channel_id=1, source_target_pairs={{0,1},{1,0},{2,3},{3,2},{4,5},{5,4},{6,7},{7,6},{8,9},{9,8},{10,11... | collective-permute-start | bytes 294920 | tf_op jit(solution)/shard_map/ppermute | solution.py:542
  453.1 49.9 %collective-permute-start.54 = (bf16[64,768]{1,0:T(8,128)(2,1)}, bf16[64,768]{1,0:T(8,128)(2,1)S(1)}, u32[]{:S(2)}, u32[]{:S(2)}) collective-permute-start(bf16[64,768]{1,0:T(8,128)(2,1)} %get-tuple-element.471.refs_10_), channel_id=1, source_target_pairs={{0,2},{1,3},{2,0},{3,1},{4,6},{5,7},{6,4},{7,5},{8,10},{9,11},{10,... | collective-permute-start | bytes 294920 | tf_op jit(solution)/shard_map/ppermute | solution.py:542
  612.9 45.7 %collective-permute-start.74 = (bf16[256,1024]{1,0:T(8,128)(2,1)}, bf16[256,1024]{1,0:T(8,128)(2,1)S(1)}, u32[]{:S(2)}, u32[]{:S(2)}) collective-permute-start(bf16[256,1024]{1,0:T(8,128)(2,1)} %convolution_convert_fusion.14), channel_id=1, source_target_pairs={{0,8},{8,0},{1,9},{9,1},{2,10},{10,2},{3,11},{11,3},{4,12},{12,4},... | collective-permute-start | bytes 1572872 | tf_op jit(solution)/shard_map/ppermute | solution.py:645
  626.9 34.9 %collective-permute-start.68 = (bf16[1024,1024]{1,0:T(8,128)(2,1)S(1)}, bf16[1024,1024]{1,0:T(8,128)(2,1)S(1)}, u32[]{:S(2)}, u32[]{:S(2)}) collective-permute-start(bf16[1024,1024]{1,0:T(8,128)(2,1)S(1)} %convolution_convert_fusion.7), channel_id=1, source_target_pairs={{0,8},{8,0},{1,9},{9,1},{2,10},{10,2},{3,11},{11,3},{4,12},{12,4},... | collective-permute-start | bytes 6291464 | tf_op jit(solution)/shard_map/ppermute | solution.py:645
  644.6 72.2 %collective-permute-start.70 = (bf16[256,4096]{1,0:T(8,128)(2,1)}, bf16[256,4096]{1,0:T(8,128)(2,1)}, u32[]{:S(2)}, u32[]{:S(2)}) collective-permute-start(bf16[256,4096]{1,0:T(8,128)(2,1)} %convolution_convert_fusion.1), channel_id=1, source_target_pairs={{0,8},{8,0},{1,9},{9,1},{2,10},{10,2},{3,11},{11,3},{4,12},{12,4},... | collective-permute-start | bytes 6291464 | tf_op jit(solution)/shard_map/ppermute | solution.py:645
  644.7 72.2 %collective-permute-start.72 = (bf16[256,4096]{1,0:T(8,128)(2,1)}, bf16[256,4096]{1,0:T(8,128)(2,1)}, u32[]{:S(2)}, u32[]{:S(2)}) collective-permute-start(bf16[256,4096]{1,0:T(8,128)(2,1)} %add_convert_fusion.2), channel_id=1, source_target_pairs={{0,16},{16,0},{1,17},{17,1},{2,18},{18,2},{3,19},{19,3},{4,20},{20... | collective-permute-start | bytes 6291464 | tf_op jit(solution)/shard_map/ppermute | solution.py:648
  658.6 44.0 %collective-permute-start.73 = (bf16[256,1024]{1,0:T(8,128)(2,1)S(1)}, bf16[256,1024]{1,0:T(8,128)(2,1)S(1)}, u32[]{:S(2)}, u32[]{:S(2)}) collective-permute-start(bf16[256,1024]{1,0:T(8,128)(2,1)S(1)} %convolution_convert_fusion.15), channel_id=1, source_target_pairs={{0,8},{8,0},{1,9},{9,1},{2,10},{10,2},{3,11},{11,3},{4,12},{12,4},... | collective-permute-start | bytes 1572872 | tf_op jit(solution)/shard_map/ppermute | solution.py:645
  661.5 41.2 %collective-permute-start.78 = (bf16[256,320]{0,1:T(8,128)(2,1)S(1)}, bf16[256,320]{0,1:T(8,128)(2,1)S(1)}, u32[]{:S(2)}, u32[]{:S(2)}) collective-permute-start(bf16[256,320]{0,1:T(8,128)(2,1)S(1)} %add_convert_fusion.11), channel_id=1, source_target_pairs={{0,16},{16,0},{1,17},{17,1},{2,18},{18,2},{3,19},{19,3},{4,20},{20... | collective-permute-start | bytes 491528 | tf_op jit(solution)/shard_map/ppermute | solution.py:648
  661.8 52.2 %collective-permute-start.75 = (bf16[256,1024]{1,0:T(8,128)(2,1)}, bf16[256,1024]{1,0:T(8,128)(2,1)}, u32[]{:S(2)}, u32[]{:S(2)}) collective-permute-start(bf16[256,1024]{1,0:T(8,128)(2,1)} %fusion.79), channel_id=1, source_target_pairs={{0,16},{16,0},{1,17},{17,1},{2,18},{18,2},{3,19},{19,3},{4,20},{20... | collective-permute-start | bytes 1572872 | tf_op jit(solution)/shard_map/ppermute | solution.py:648
  702.7 56.0 %collective-permute-start.69 = (bf16[1024,1024]{1,0:T(8,128)(2,1)}, bf16[1024,1024]{1,0:T(8,128)(2,1)}, u32[]{:S(2)}, u32[]{:S(2)}) collective-permute-start(bf16[1024,1024]{1,0:T(8,128)(2,1)} %add_convert_fusion.4), channel_id=1, source_target_pairs={{0,16},{16,0},{1,17},{17,1},{2,18},{18,2},{3,19},{19,3},{4,20},{20... | collective-permute-start | bytes 6291464 | tf_op jit(solution)/shard_map/ppermute | solution.py:648
  764.7 482.2 %all-gather.14.cloned.1.call-start = ((), (), s32[]{:S(2)}) async-start(), calls=%async_computation.12 | async-start | bytes 4423680 | tf_op jit(solution)/shard_map/all_gather | solution.py:631
  767.8 545.5 %reduce-scatter.18.cloned.1.call-start = ((), (), s32[]{:S(2)}) async-start(), calls=%async_computation.17 | async-start | bytes 2359296 | tf_op jit(solution)/shard_map/reduce_scatter | solution.py:651
  804.3 59.3 %collective-permute-start.89 = (bf16[192,768]{1,0:T(8,128)(2,1)}, bf16[192,768]{1,0:T(8,128)(2,1)S(1)}, u32[]{:S(2)}, u32[]{:S(2)}) collective-permute-start(bf16[192,768]{1,0:T(8,128)(2,1)} %get-tuple-element.533), channel_id=1, source_target_pairs={{0,1},{1,0},{2,3},{3,2},{4,5},{5,4},{6,7},{7,6},{8,9},{9,8},{10,11... | collective-permute-start | bytes 884744 | tf_op jit(solution)/shard_map/ppermute | solution.py:542
  804.9 60.2 %collective-permute-start.93 = (bf16[192,768]{1,0:T(8,128)(2,1)}, bf16[192,768]{1,0:T(8,128)(2,1)S(1)}, u32[]{:S(2)}, u32[]{:S(2)}) collective-permute-start(bf16[192,768]{1,0:T(8,128)(2,1)} %get-tuple-element.537), channel_id=1, source_target_pairs={{0,2},{1,3},{2,0},{3,1},{4,6},{5,7},{6,4},{7,5},{8,10},{9,11},{10,... | collective-permute-start | bytes 884744 | tf_op jit(solution)/shard_map/ppermute | solution.py:542
  809.9 505.2 %reduce-scatter.20.cloned.1.call-start = ((), (), s32[]{:S(2)}) async-start(), calls=%async_computation.18 | async-start | bytes 2359296 | tf_op jit(solution)/shard_map/reduce_scatter | solution.py:651
  834.9 56.0 %collective-permute-start.97 = (bf16[192,768]{1,0:T(8,128)(2,1)S(1)}, bf16[192,768]{1,0:T(8,128)(2,1)S(1)}, u32[]{:S(2)}, u32[]{:S(2)}) collective-permute-start(bf16[192,768]{1,0:T(8,128)(2,1)S(1)} %copy-done.135), channel_id=1, source_target_pairs={{0,3},{1,2},{2,1},{3,0},{4,7},{5,6},{6,5},{7,4},{8,11},{9,10},{10,... | collective-permute-start | bytes 884744 | tf_op jit(solution)/shard_map/ppermute | solution.py:542
  836.6 55.9 %collective-permute-start.90 = (bf16[192,768]{1,0:T(8,128)(2,1)}, bf16[192,768]{1,0:T(8,128)(2,1)S(1)}, u32[]{:S(2)}, u32[]{:S(2)}) collective-permute-start(bf16[192,768]{1,0:T(8,128)(2,1)} %get-tuple-element.534), channel_id=1, source_target_pairs={{0,1},{1,0},{2,3},{3,2},{4,5},{5,4},{6,7},{7,6},{8,9},{9,8},{10,11... | collective-permute-start | bytes 884744 | tf_op jit(solution)/shard_map/ppermute | solution.py:542
  837.2 56.8 %collective-permute-start.94 = (bf16[192,768]{1,0:T(8,128)(2,1)}, bf16[192,768]{1,0:T(8,128)(2,1)S(1)}, u32[]{:S(2)}, u32[]{:S(2)}) collective-permute-start(bf16[192,768]{1,0:T(8,128)(2,1)} %get-tuple-element.538), channel_id=1, source_target_pairs={{0,2},{1,3},{2,0},{3,1},{4,6},{5,7},{6,4},{7,5},{8,10},{9,11},{10,... | collective-permute-start | bytes 884744 | tf_op jit(solution)/shard_map/ppermute | solution.py:542
  896.1 34.6 %collective-permute-start.96 = (bf16[192,768]{1,0:T(8,128)(2,1)}, bf16[192,768]{1,0:T(8,128)(2,1)S(1)}, u32[]{:S(2)}, u32[]{:S(2)}) collective-permute-start(bf16[192,768]{1,0:T(8,128)(2,1)} %get-tuple-element.540), channel_id=1, source_target_pairs={{0,3},{1,2},{2,1},{3,0},{4,7},{5,6},{6,5},{7,4},{8,11},{9,10},{10,... | collective-permute-start | bytes 884744 | tf_op jit(solution)/shard_map/ppermute | solution.py:542
  897.5 497.6 %reduce-scatter.12.cloned.1.call-start = ((), (), s32[]{:S(2)}) async-start(), calls=%async_computation.14 | async-start | bytes 442368 | tf_op jit(solution)/shard_map/reduce_scatter | solution.py:651
  969.1 77.0 %collective-permute-start.116 = (bf16[256,1024]{1,0:T(8,128)(2,1)S(1)}, bf16[256,1024]{1,0:T(8,128)(2,1)S(1)}, u32[]{:S(2)}, u32[]{:S(2)}) collective-permute-start(bf16[256,1024]{1,0:T(8,128)(2,1)S(1)} %convolution_convert_fusion.12), channel_id=1, source_target_pairs={{0,8},{8,0},{1,9},{9,1},{2,10},{10,2},{3,11},{11,3},{4,12},{12,4},... | collective-permute-start | bytes 1572872 | tf_op jit(solution)/shard_map/ppermute | solution.py:645
  969.2 79.3 %collective-permute-start.113 = (bf16[256,3072]{1,0:T(8,128)(2,1)}, bf16[256,3072]{1,0:T(8,128)(2,1)}, u32[]{:S(2)}, u32[]{:S(2)}) collective-permute-start(bf16[256,3072]{1,0:T(8,128)(2,1)} %convolution_convert_fusion.2), channel_id=1, source_target_pairs={{0,8},{8,0},{1,9},{9,1},{2,10},{10,2},{3,11},{11,3},{4,12},{12,4},... | collective-permute-start | bytes 4718600 | tf_op jit(solution)/shard_map/ppermute | solution.py:645
  972.5 36.1 %collective-permute-start.103 = (bf16[64,768]{1,0:T(8,128)(2,1)}, bf16[64,768]{1,0:T(8,128)(2,1)}, u32[]{:S(2)}, u32[]{:S(2)}) collective-permute-start(bf16[64,768]{1,0:T(8,128)(2,1)} %get-tuple-element.563), channel_id=1, source_target_pairs={{0,1},{1,0},{2,3},{3,2},{4,5},{5,4},{6,7},{7,6},{8,9},{9,8},{10,11... | collective-permute-start | bytes 294920 | tf_op jit(solution)/shard_map/ppermute | solution.py:542
  973.3 35.3 %collective-permute-start.104 = (bf16[64,768]{1,0:T(8,128)(2,1)}, bf16[64,768]{1,0:T(8,128)(2,1)}, u32[]{:S(2)}, u32[]{:S(2)}) collective-permute-start(bf16[64,768]{1,0:T(8,128)(2,1)} %get-tuple-element.564), channel_id=1, source_target_pairs={{0,2},{1,3},{2,0},{3,1},{4,6},{5,7},{6,4},{7,5},{8,10},{9,11},{10,... | collective-permute-start | bytes 294920 | tf_op jit(solution)/shard_map/ppermute | solution.py:542
  1008.6 36.1 %collective-permute-start.106 = (bf16[64,768]{1,0:T(8,128)(2,1)S(1)}, bf16[64,768]{1,0:T(8,128)(2,1)}, u32[]{:S(2)}, u32[]{:S(2)}) collective-permute-start(bf16[64,768]{1,0:T(8,128)(2,1)S(1)} %copy-done.217), channel_id=1, source_target_pairs={{0,1},{1,0},{2,3},{3,2},{4,5},{5,4},{6,7},{7,6},{8,9},{9,8},{10,11... | collective-permute-start | bytes 294920 | tf_op jit(solution)/shard_map/ppermute | solution.py:542
  1009.5 35.3 %collective-permute-start.107 = (bf16[64,768]{1,0:T(8,128)(2,1)S(1)}, bf16[64,768]{1,0:T(8,128)(2,1)}, u32[]{:S(2)}, u32[]{:S(2)}) collective-permute-start(bf16[64,768]{1,0:T(8,128)(2,1)S(1)} %copy-done.216), channel_id=1, source_target_pairs={{0,2},{1,3},{2,0},{3,1},{4,6},{5,7},{6,4},{7,5},{8,10},{9,11},{10,... | collective-permute-start | bytes 294920 | tf_op jit(solution)/shard_map/ppermute | solution.py:542
  1011.1 34.2 %collective-permute-start.108 = (bf16[64,768]{1,0:T(8,128)(2,1)S(1)}, bf16[64,768]{1,0:T(8,128)(2,1)}, u32[]{:S(2)}, u32[]{:S(2)}) collective-permute-start(bf16[64,768]{1,0:T(8,128)(2,1)S(1)} %copy-done.215), channel_id=1, source_target_pairs={{0,3},{1,2},{2,1},{3,0},{4,7},{5,6},{6,5},{7,4},{8,11},{9,10},{10,... | collective-permute-start | bytes 294920 | tf_op jit(solution)/shard_map/ppermute | solution.py:542
  1044.7 42.1 %collective-permute-start.115 = (bf16[256,1024]{1,0:T(8,128)(2,1)}, bf16[256,1024]{1,0:T(8,128)(2,1)}, u32[]{:S(2)}, u32[]{:S(2)}) collective-permute-start(bf16[256,1024]{1,0:T(8,128)(2,1)} %convolution_convert_fusion.13), channel_id=1, source_target_pairs={{0,8},{8,0},{1,9},{9,1},{2,10},{10,2},{3,11},{11,3},{4,12},{12,4},... | collective-permute-start | bytes 1572872 | tf_op jit(solution)/shard_map/ppermute | solution.py:645
  1044.8 46.8 %collective-permute-start.112 = (bf16[256,3072]{1,0:T(8,128)(2,1)}, bf16[256,3072]{1,0:T(8,128)(2,1)}, u32[]{:S(2)}, u32[]{:S(2)}) collective-permute-start(bf16[256,3072]{1,0:T(8,128)(2,1)} %convolution_convert_fusion.3), channel_id=1, source_target_pairs={{0,8},{8,0},{1,9},{9,1},{2,10},{10,2},{3,11},{11,3},{4,12},{12,4},... | collective-permute-start | bytes 4718600 | tf_op jit(solution)/shard_map/ppermute | solution.py:645
  1045.3 60.7 %collective-permute-start.118 = (bf16[128,1024]{1,0:T(8,128)(2,1)}, bf16[128,1024]{1,0:T(8,128)(2,1)S(1)}, u32[]{:S(2)}, u32[]{:S(2)}) collective-permute-start(bf16[128,1024]{1,0:T(8,128)(2,1)} %get-tuple-element.596), channel_id=1, source_target_pairs={{0,1},{1,0},{2,3},{3,2},{4,5},{5,4},{6,7},{7,6},{8,9},{9,8},{10,11... | collective-permute-start | bytes 786440 | tf_op jit(solution)/shard_map/ppermute | solution.py:542
  1046.7 41.8 %collective-permute-start.117 = (bf16[256,1024]{1,0:T(8,128)(2,1)S(1)}, bf16[256,1024]{1,0:T(8,128)(2,1)S(1)}, u32[]{:S(2)}, u32[]{:S(2)}) collective-permute-start(bf16[256,1024]{1,0:T(8,128)(2,1)S(1)} %fusion.80), channel_id=1, source_target_pairs={{0,16},{16,0},{1,17},{17,1},{2,18},{18,2},{3,19},{19,3},{4,20},{20... | collective-permute-start | bytes 1572872 | tf_op jit(solution)/shard_map/ppermute | solution.py:648
  1053.9 40.3 %collective-permute-start.114 = (bf16[256,3072]{1,0:T(8,128)(2,1)}, bf16[256,3072]{1,0:T(8,128)(2,1)}, u32[]{:S(2)}, u32[]{:S(2)}) collective-permute-start(bf16[256,3072]{1,0:T(8,128)(2,1)} %fusion.13), channel_id=1, source_target_pairs={{0,16},{16,0},{1,17},{17,1},{2,18},{18,2},{3,19},{19,3},{4,20},{20... | collective-permute-start | bytes 4718600 | tf_op jit(solution)/shard_map/ppermute | solution.py:648
  1101.8 39.5 %collective-permute-start.126 = (bf16[128,1024]{1,0:T(8,128)(2,1)S(1)}, bf16[128,1024]{1,0:T(8,128)(2,1)S(1)}, u32[]{:S(2)}, u32[]{:S(2)}) collective-permute-start(bf16[128,1024]{1,0:T(8,128)(2,1)S(1)} %copy-done.157), channel_id=1, source_target_pairs={{0,3},{1,2},{2,1},{3,0},{4,7},{5,6},{6,5},{7,4},{8,11},{9,10},{10,... | collective-permute-start | bytes 786440 | tf_op jit(solution)/shard_map/ppermute | solution.py:542
  1103.8 38.6 %collective-permute-start.119 = (bf16[128,1024]{1,0:T(8,128)(2,1)S(1)}, bf16[128,1024]{1,0:T(8,128)(2,1)S(1)}, u32[]{:S(2)}, u32[]{:S(2)}) collective-permute-start(bf16[128,1024]{1,0:T(8,128)(2,1)S(1)} %copy-done.161), channel_id=1, source_target_pairs={{0,1},{1,0},{2,3},{3,2},{4,5},{5,4},{6,7},{7,6},{8,9},{9,8},{10,11... | collective-permute-start | bytes 786440 | tf_op jit(solution)/shard_map/ppermute | solution.py:542
  1105.0 38.8 %collective-permute-start.123 = (bf16[128,1024]{1,0:T(8,128)(2,1)S(1)}, bf16[128,1024]{1,0:T(8,128)(2,1)S(1)}, u32[]{:S(2)}, u32[]{:S(2)}) collective-permute-start(bf16[128,1024]{1,0:T(8,128)(2,1)S(1)} %copy-done.160), channel_id=1, source_target_pairs={{0,2},{1,3},{2,0},{3,1},{4,6},{5,7},{6,4},{7,5},{8,10},{9,11},{10,... | collective-permute-start | bytes 786440 | tf_op jit(solution)/shard_map/ppermute | solution.py:542
  1106.0 38.9 %collective-permute-start.127 = (bf16[128,1024]{1,0:T(8,128)(2,1)S(1)}, bf16[128,1024]{1,0:T(8,128)(2,1)S(1)}, u32[]{:S(2)}, u32[]{:S(2)}) collective-permute-start(bf16[128,1024]{1,0:T(8,128)(2,1)S(1)} %copy-done.159), channel_id=1, source_target_pairs={{0,3},{1,2},{2,1},{3,0},{4,7},{5,6},{6,5},{7,4},{8,11},{9,10},{10,... | collective-permute-start | bytes 786440 | tf_op jit(solution)/shard_map/ppermute | solution.py:542
  1107.4 38.6 %collective-permute-start.120 = (bf16[128,1024]{1,0:T(8,128)(2,1)}, bf16[128,1024]{1,0:T(8,128)(2,1)S(1)}, u32[]{:S(2)}, u32[]{:S(2)}) collective-permute-start(bf16[128,1024]{1,0:T(8,128)(2,1)} %get-tuple-element.598), channel_id=1, source_target_pairs={{0,1},{1,0},{2,3},{3,2},{4,5},{5,4},{6,7},{7,6},{8,9},{9,8},{10,11... | collective-permute-start | bytes 786440 | tf_op jit(solution)/shard_map/ppermute | solution.py:542
  1185.5 42.0 %collective-permute-start.62 = (bf16[384,1024]{1,0:T(8,128)(2,1)S(1)}, bf16[384,1024]{1,0:T(8,128)(2,1)}, u32[]{:S(2)}, u32[]{:S(2)}) collective-permute-start(bf16[384,1024]{1,0:T(8,128)(2,1)S(1)} %constant_dynamic-slice_fusion.2), channel_id=1, source_target_pairs={{0,4},{4,0},{1,5},{5,1},{2,6},{6,2},{3,7},{7,3},{8,12},{12,8},{9,1... | collective-permute-start | bytes 2359304 | tf_op jit(solution)/shard_map/ppermute | solution.py:532
  1195.6 253.6 %reduce-scatter.14.cloned.1.call-start = ((), (), s32[]{:S(2)}) async-start(), calls=%async_computation.15 | async-start | bytes 1769472 | tf_op jit(solution)/shard_map/reduce_scatter | solution.py:651
  1232.8 39.3 %collective-permute-start.142 = (bf16[64,768]{1,0:T(8,128)(2,1)S(1)}, bf16[64,768]{1,0:T(8,128)(2,1)S(1)}, u32[]{:S(2)}, u32[]{:S(2)}) collective-permute-start(bf16[64,768]{1,0:T(8,128)(2,1)S(1)} %copy-done.196), channel_id=1, source_target_pairs={{0,2},{1,3},{2,0},{3,1},{4,6},{5,7},{6,4},{7,5},{8,10},{9,11},{10,... | collective-permute-start | bytes 294920 | tf_op jit(solution)/shard_map/ppermute | solution.py:542
  1233.5 38.6 %collective-permute-start.146 = (bf16[64,768]{1,0:T(8,128)(2,1)S(1)}, bf16[64,768]{1,0:T(8,128)(2,1)S(1)}, u32[]{:S(2)}, u32[]{:S(2)}) collective-permute-start(bf16[64,768]{1,0:T(8,128)(2,1)S(1)} %copy-done.195), channel_id=1, source_target_pairs={{0,3},{1,2},{2,1},{3,0},{4,7},{5,6},{6,5},{7,4},{8,11},{9,10},{10,... | collective-permute-start | bytes 294920 | tf_op jit(solution)/shard_map/ppermute | solution.py:542
  1235.3 36.8 %collective-permute-start.139 = (bf16[64,768]{1,0:T(8,128)(2,1)S(1)}, bf16[64,768]{1,0:T(8,128)(2,1)S(1)}, u32[]{:S(2)}, u32[]{:S(2)}) collective-permute-start(bf16[64,768]{1,0:T(8,128)(2,1)S(1)} %copy-done.201), channel_id=1, source_target_pairs={{0,1},{1,0},{2,3},{3,2},{4,5},{5,4},{6,7},{7,6},{8,9},{9,8},{10,11... | collective-permute-start | bytes 294920 | tf_op jit(solution)/shard_map/ppermute | solution.py:542
  1236.5 35.6 %collective-permute-start.143 = (bf16[64,768]{1,0:T(8,128)(2,1)S(1)}, bf16[64,768]{1,0:T(8,128)(2,1)S(1)}, u32[]{:S(2)}, u32[]{:S(2)}) collective-permute-start(bf16[64,768]{1,0:T(8,128)(2,1)S(1)} %copy-done.200), channel_id=1, source_target_pairs={{0,2},{1,3},{2,0},{3,1},{4,6},{5,7},{6,4},{7,5},{8,10},{9,11},{10,... | collective-permute-start | bytes 294920 | tf_op jit(solution)/shard_map/ppermute | solution.py:542
  1237.2 35.0 %collective-permute-start.147 = (bf16[64,768]{1,0:T(8,128)(2,1)S(1)}, bf16[64,768]{1,0:T(8,128)(2,1)S(1)}, u32[]{:S(2)}, u32[]{:S(2)}) collective-permute-start(bf16[64,768]{1,0:T(8,128)(2,1)S(1)} %copy-done.199), channel_id=1, source_target_pairs={{0,3},{1,2},{2,1},{3,0},{4,7},{5,6},{6,5},{7,4},{8,11},{9,10},{10,... | collective-permute-start | bytes 294920 | tf_op jit(solution)/shard_map/ppermute | solution.py:542
  1272.0 200.9 %reduce-scatter.10.cloned.1.call-start = ((), (), s32[]{:S(2)}) async-start(), calls=%async_computation.13 | async-start | bytes 2433024 | tf_op jit(solution)/shard_map/reduce_scatter | solution.py:651
  1294.1 98.4 %collective-permute-start.148 = (bf16[256,1024]{1,0:T(8,128)(2,1)}, bf16[256,1024]{1,0:T(8,128)(2,1)}, u32[]{:S(2)}, u32[]{:S(2)}) collective-permute-start(bf16[256,1024]{1,0:T(8,128)(2,1)} %convolution_convert_fusion.11), channel_id=1, source_target_pairs={{0,8},{8,0},{1,9},{9,1},{2,10},{10,2},{3,11},{11,3},{4,12},{12,4},... | collective-permute-start | bytes 1572872 | tf_op jit(solution)/shard_map/ppermute | solution.py:645
  1308.7 61.7 %collective-permute-start.151 = (bf16[384,1024]{1,0:T(8,128)(2,1)}, bf16[384,1024]{1,0:T(8,128)(2,1)}, u32[]{:S(2)}, u32[]{:S(2)}) collective-permute-start(bf16[384,1024]{1,0:T(8,128)(2,1)} %dynamic-slice_convert_fusion.1), channel_id=1, source_target_pairs={{0,4},{4,0},{1,5},{5,1},{2,6},{6,2},{3,7},{7,3},{8,12},{12,8},{9,1... | collective-permute-start | bytes 2359304 | tf_op jit(solution)/shard_map/ppermute | solution.py:532
  1311.6 84.9 %collective-permute-start.130 = (bf16[256,2048]{1,0:T(8,128)(2,1)}, bf16[256,2048]{1,0:T(8,128)(2,1)}, u32[]{:S(2)}, u32[]{:S(2)}) collective-permute-start(bf16[256,2048]{1,0:T(8,128)(2,1)} %convolution_convert_fusion.6), channel_id=1, source_target_pairs={{0,8},{8,0},{1,9},{9,1},{2,10},{10,2},{3,11},{11,3},{4,12},{12,4},... | collective-permute-start | bytes 3145736 | tf_op jit(solution)/shard_map/ppermute | solution.py:645
  1311.7 75.0 %collective-permute-start.152 = (bf16[512,768]{1,0:T(8,128)(2,1)}, bf16[512,768]{1,0:T(8,128)(2,1)}, u32[]{:S(2)}, u32[]{:S(2)}) collective-permute-start(bf16[512,768]{1,0:T(8,128)(2,1)} %dynamic-slice_convert_fusion), channel_id=1, source_target_pairs={{0,4},{4,0},{1,5},{5,1},{2,6},{6,2},{3,7},{7,3},{8,12},{12,8},{9,1... | collective-permute-start | bytes 2359304 | tf_op jit(solution)/shard_map/ppermute | solution.py:532
  1316.9 75.7 %collective-permute-start.150 = (bf16[256,1024]{1,0:T(8,128)(2,1)}, bf16[256,1024]{1,0:T(8,128)(2,1)S(1)}, u32[]{:S(2)}, u32[]{:S(2)}) collective-permute-start(bf16[256,1024]{1,0:T(8,128)(2,1)} %fusion.81), channel_id=1, source_target_pairs={{0,16},{16,0},{1,17},{17,1},{2,18},{18,2},{3,19},{19,3},{4,20},{20... | collective-permute-start | bytes 1572872 | tf_op jit(solution)/shard_map/ppermute | solution.py:648
  (348 other events, 6655.4 us)
Sparse Core Ops, SparseCore 0:
  17.4 133.6 all-gather.5
  154.5 136.3 all-gather.7
  293.7 113.7 all-gather.9
  410.8 102.1 all-gather.11
Sparse Core Ops, SparseCore 1:
  140.4 158.4 reduce-scatter.7
  764.8 65.1 reduce-scatter.15
  832.6 91.5 all-gather.13
  927.8 74.2 reduce-scatter.17
  1005.6 67.4 reduce-scatter.19
  1195.7 72.1 reduce-scatter.11
  1272.1 115.3 reduce-scatter.13
  1403.4 69.5 reduce-scatter.9

commit v2 on v1

v2 whole, which is shorter than its diff:
```python
import functools
import math

import jax
import jax.numpy as jnp
from jax import lax
from jax.experimental import pallas as pl
from jax.experimental.pallas import tpu as pltpu
from jax.sharding import Mesh
from jax.sharding import PartitionSpec as P

D = 1024
H = 16
HD = 64
FF = 4096
DINO = 768
CH = 80
G = 32
RB = 128
SAMP = 32
TOK_OBJ = 3072
PIX = G * G
SCALE = HD ** (-0.5)
VMEM = 58 * 2**20
ONES = 16

epsilon = 1e-05
NN = ((1,), (0,))
NT = ((1,), (1,))
TN = ((0,), (0,))
bf16 = jnp.bfloat16
f32 = jnp.float32


def lower(value):
    return value.astype(bf16)


def widen(value):
    return value.astype(f32)


def dot(left, right, dims):
    return lax.dot_general(left, right, (dims, ((), ())), preferred_element_type=f32)


def normalize(values, gain, shift):
    centered = values - jnp.mean(values, axis=-1, keepdims=True)
    inverse = lax.rsqrt(jnp.mean(centered * centered, axis=-1, keepdims=True) + epsilon)
    unit = centered * inverse
    return (unit * gain + shift, unit, inverse)


def normalize_back(grad, unit, inverse, gain):
    gain_grad = jnp.sum(grad * unit, axis=0)
    shift_grad = jnp.sum(grad, axis=0)
    scaled = grad * gain
    inner = (
        scaled
        - jnp.mean(scaled, axis=-1, keepdims=True)
        - unit * jnp.mean(scaled * unit, axis=-1, keepdims=True)
    )
    return (inverse * inner, gain_grad, shift_grad)


def gelu(values):
    return 0.5 * values * (1.0 + lax.erf(values * 0.7071067811865476))


def fixed(shape):
    return pl.BlockSpec(shape, lambda *_: (0,) * len(shape))


class Places:
    def __init__(self, shape, count):
        self.beside = shape[0] == HD
        self.count = count
        self.length = (shape[1] - count) // 2 if self.beside else shape[1]

    def query(self):
        return (slice(0, HD), slice(0, self.count))

    def keys(self, start, stop):
        if self.beside:
            return (slice(0, HD), slice(self.count + start, self.count + stop))
        return (slice(HD, 2 * HD), slice(start, stop))

    def values(self, start, stop):
        if self.beside:
            return self.keys(self.length + start, self.length + stop)
        return (slice(2 * HD, 3 * HD), slice(start, stop))


def forward_kernel(*refs, chunks, block, places):
    refs, out_refs = refs[:chunks], refs[chunks:]
    out_refs, (lse_ref, query_ref, keys_ref, values_ref) = out_refs[:chunks], out_refs[chunks:]
    turn = pl.program_id(0)
    length = places.length

    @pl.when(turn == 0)
    def _():
        for r in range(chunks):
            keys_ref[r] = refs[r][places.keys(0, length)].T
            query_ref[r] = refs[r][places.query()] * jnp.asarray(SCALE, bf16)
            values_ref[r, :HD, :] = refs[r][places.values(0, length)]
            values_ref[r, HD:, :] = jnp.ones((ONES, length), bf16)

    query = query_ref[turn]
    count = query.shape[1]
    peak = jnp.full((1, count), -jnp.inf, f32)
    mixed = jnp.zeros((HD + ONES, count), f32)
    spots = [(r, c) for r in range(chunks) for c in range(0, length, block)]

    def score(spot):
        r, c = spot
        return dot(keys_ref[r, c : c + block, :], query, NN)

    ahead = score(spots[0])
    for step, (r, c) in enumerate(spots):
        scores = ahead
        if step + 1 < len(spots):
            ahead = score(spots[step + 1])
        higher = jnp.maximum(peak, jnp.max(scores, axis=0, keepdims=True))
        expo = jnp.exp(scores - higher)
        shrink = jnp.exp(peak - higher)
        mixed = mixed * shrink + dot(values_ref[r, :, c : c + block], lower(expo), NN)
        peak = higher
    total = mixed[HD : HD + 1]
    out = lower(mixed[:HD] / total)
    for r in range(chunks):

        @pl.when(turn == r)
        def _():
            out_refs[r][...] = out

    lse_ref[0] = peak + jnp.log(total)


def attend_forward(sources, count):
    chunks = len(sources)
    places = Places(sources[0].shape, count)
    length = places.length
    block = math.gcd(length, 256)
    steps = chunks * chunks * count * length
    *outs, lse = pl.pallas_call(
        functools.partial(forward_kernel, chunks=chunks, block=block, places=places),
        grid=(chunks,),
        in_specs=[fixed(s.shape) for s in sources],
        out_specs=[fixed((HD, count))] * chunks + [pl.BlockSpec((1, 1, count), lambda i: (i, 0, 0))],
        out_shape=[jax.ShapeDtypeStruct((HD, count), bf16)] * chunks
        + [jax.ShapeDtypeStruct((chunks, 1, count), f32)],
        scratch_shapes=[
            pltpu.VMEM((chunks, HD, count), bf16),
            pltpu.VMEM((chunks, length, HD), bf16),
            pltpu.VMEM((chunks, HD + ONES, length), bf16),
        ],
        compiler_params=pltpu.CompilerParams(vmem_limit_bytes=VMEM),
        cost_estimate=pl.CostEstimate(
            flops=steps * 2 * 2 * 256, bytes_accessed=4 * chunks * length * 64, transcendentals=steps
        ),
        name="attend_forward",
    )(*sources)
    return outs, lse


def backward_kernel(*refs, chunks, block, places):
    refs, dout_refs, out_refs, refs_left = (
        refs[:chunks],
        refs[chunks : 2 * chunks],
        refs[2 * chunks : 3 * chunks],
        refs[3 * chunks :],
    )
    lse_ref, grads, scratch = refs_left[0], refs_left[1 : 1 + chunks], refs_left[1 + chunks :]
    query_ref, dout_ref, delta_ref, keys_ref, keys_acc, values_acc = scratch
    turn = pl.program_id(0)
    length = places.length

    @pl.when(turn == 0)
    def _():
        for r in range(chunks):
            keys_ref[r] = refs[r][places.keys(0, length)].T
            query_ref[r] = refs[r][places.query()] * jnp.asarray(SCALE, bf16)
            dout_ref[r] = dout_refs[r][...]
            delta_ref[r] = jnp.sum(
                widen(dout_refs[r][...]) * widen(out_refs[r][...]), axis=0, keepdims=True
            )
        keys_acc[...] = jnp.zeros_like(keys_acc)
        values_acc[...] = jnp.zeros_like(values_acc)

    query = query_ref[turn]
    dout = dout_ref[turn]
    count = query.shape[1]

    def across(row):
        if block % 128:
            return jnp.broadcast_to(row, (block, count)).T
        return jnp.concatenate([jnp.broadcast_to(row, (128, count)).T] * (block // 128), axis=1)

    lse_cols = across(lse_ref[0])
    delta_cols = across(delta_ref[turn])
    query_rows = query.T
    dout_rows = dout.T
    query_grad = jnp.zeros((count, HD), f32)
    spots = [(r, c) for r in range(chunks) for c in range(0, length, block)]

    def score(spot):
        r, c = spot
        return (
            dot(query_rows, refs[r][places.keys(c, c + block)], NN),
            dot(dout_rows, refs[r][places.values(c, c + block)], NN),
        )

    ahead = score(spots[0])
    for step, (r, c) in enumerate(spots):
        scores, prob_grad = ahead
        if step + 1 < len(spots):
            ahead = score(spots[step + 1])
        span = slice(c, c + block)
        probability = jnp.exp(scores - lse_cols)
        score_grad = lower(probability * (prob_grad - delta_cols))
        query_grad = query_grad + dot(score_grad, keys_ref[r, span, :], NN)
        values_acc[r, :, span] += dot(dout, lower(probability), NN)
        keys_acc[r, :, span] += dot(query, score_grad, NN)
    query_grad = lower((query_grad * SCALE).T)
    for r in range(chunks):

        @pl.when(turn == r)
        def _():
            grads[r][places.query()] = query_grad

    @pl.when(turn == chunks - 1)
    def _():
        for r in range(chunks):
            grads[r][places.keys(0, length)] = lower(keys_acc[r])
            grads[r][places.values(0, length)] = lower(values_acc[r])


def attend_backward(sources, douts, outs, lse):
    chunks = len(sources)
    count = douts[0].shape[1]
    places = Places(sources[0].shape, count)
    length = places.length
    block = math.gcd(length, 256)
    steps = chunks * chunks * count * length
    results = [s.shape for s in sources]
    sources = list(sources) + list(douts) + list(outs)
    return pl.pallas_call(
        functools.partial(backward_kernel, chunks=chunks, block=block, places=places),
        grid=(chunks,),
        in_specs=[fixed(s.shape) for s in sources] + [pl.BlockSpec((1, 1, count), lambda i: (i, 0, 0))],
        out_specs=[fixed(s) for s in results],
        out_shape=[jax.ShapeDtypeStruct(s, bf16) for s in results],
        scratch_shapes=[
            pltpu.VMEM((chunks, HD, count), bf16),
            pltpu.VMEM((chunks, HD, count), bf16),
            pltpu.VMEM((chunks, 1, count), f32),
            pltpu.VMEM((chunks, length, HD), bf16),
            pltpu.VMEM((chunks, HD, length), f32),
            pltpu.VMEM((chunks, HD, length), f32),
        ],
        compiler_params=pltpu.CompilerParams(vmem_limit_bytes=VMEM),
        cost_estimate=pl.CostEstimate(
            flops=steps * 2 * 5 * 200, bytes_accessed=8 * chunks * length * 64, transcendentals=steps
        ),
        name="attend_backward",
    )(*sources, lse)


def split_kernel(me_ref, source_ref, *out_refs, heads):
    turn = pl.program_id(0)
    for k in range(len(out_refs) // heads):

        @pl.when(turn == k)
        def _():
            for j in range(heads):
                out_refs[k * heads + j][...] = source_ref[0, j]


def split(values, me):
    chunks, heads, height, count = values.shape
    outs = pl.pallas_call(
        functools.partial(split_kernel, heads=heads),
        grid_spec=pltpu.PrefetchScalarGridSpec(
            num_scalar_prefetch=1,
            grid=(chunks,),
            in_specs=[pl.BlockSpec((1, heads, height, count), lambda k, m: (m[0] ^ k, 0, 0, 0))],
            out_specs=[fixed((height, count))] * (chunks * heads),
        ),
        out_shape=[jax.ShapeDtypeStruct((height, count), bf16)] * (chunks * heads),
        compiler_params=pltpu.CompilerParams(vmem_limit_bytes=VMEM),
        cost_estimate=pl.CostEstimate(flops=0, bytes_accessed=4 * values.size, transcendentals=0),
        name="split",
    )(me, values)
    return [[outs[k * heads + j] for k in range(chunks)] for j in range(heads)]


def split_pair_kernel(me_ref, query_ref, keyval_ref, *out_refs, heads):
    turn = pl.program_id(0)
    places = Places(out_refs[0].shape, query_ref.shape[3])
    length = places.length
    for k in range(len(out_refs) // heads):

        @pl.when(turn == k)
        def _():
            for j in range(heads):
                out_ref = out_refs[k * heads + j]
                out_ref[places.query()] = query_ref[0, j]
                out_ref[places.keys(0, length)] = keyval_ref[0, j, :HD, :]
                out_ref[places.values(0, length)] = keyval_ref[0, j, HD:, :]


def split_pair(queries, keyvals, me):
    chunks, heads, _, count = queries.shape
    length = keyvals.shape[3]
    shape = (HD, count + 2 * length)
    outs = pl.pallas_call(
        functools.partial(split_pair_kernel, heads=heads),
        grid_spec=pltpu.PrefetchScalarGridSpec(
            num_scalar_prefetch=1,
            grid=(chunks,),
            in_specs=[
                pl.BlockSpec((1, heads, HD, count), lambda k, m: (m[0] ^ k, 0, 0, 0)),
                pl.BlockSpec((1, heads, 2 * HD, length), lambda k, m: (m[0] ^ k, 0, 0, 0)),
            ],
            out_specs=[fixed(shape)] * (chunks * heads),
        ),
        out_shape=[jax.ShapeDtypeStruct(shape, bf16)] * (chunks * heads),
        compiler_params=pltpu.CompilerParams(vmem_limit_bytes=VMEM),
        cost_estimate=pl.CostEstimate(
            flops=0, bytes_accessed=4 * (queries.size + keyvals.size), transcendentals=0
        ),
        name="split_pair",
    )(me, queries, keyvals)
    return [[outs[k * heads + j] for k in range(chunks)] for j in range(heads)]


def assemble_pair_kernel(me_ref, *refs, heads):
    turn = pl.program_id(0)
    refs, (query_ref, keyval_ref) = refs[:-2], refs[-2:]
    places = Places(refs[0].shape, query_ref.shape[3])
    length = places.length
    for k in range(len(refs) // heads):

        @pl.when(turn == k)
        def _():
            for j in range(heads):
                source = refs[k * heads + j]
                query_ref[0, j] = source[places.query()]
                keyval_ref[0, j, :HD, :] = source[places.keys(0, length)]
                keyval_ref[0, j, HD:, :] = source[places.values(0, length)]


def assemble_pair(parts, me, count):
    heads, chunks = len(parts), len(parts[0])
    shape = parts[0][0].shape
    length = (shape[1] - count) // 2
    sources = [parts[j][k] for k in range(chunks) for j in range(heads)]
    return pl.pallas_call(
        functools.partial(assemble_pair_kernel, heads=heads),
        grid_spec=pltpu.PrefetchScalarGridSpec(
            num_scalar_prefetch=1,
            grid=(chunks,),
            in_specs=[fixed(shape)] * (chunks * heads),
            out_specs=[
                pl.BlockSpec((1, heads, HD, count), lambda k, m: (m[0] ^ k, 0, 0, 0)),
                pl.BlockSpec((1, heads, 2 * HD, length), lambda k, m: (m[0] ^ k, 0, 0, 0)),
            ],
        ),
        out_shape=[
            jax.ShapeDtypeStruct((chunks, heads, HD, count), bf16),
            jax.ShapeDtypeStruct((chunks, heads, 2 * HD, length), bf16),
        ],
        compiler_params=pltpu.CompilerParams(vmem_limit_bytes=VMEM),
        cost_estimate=pl.CostEstimate(
            flops=0, bytes_accessed=4 * chunks * heads * HD * shape[1], transcendentals=0
        ),
        name="assemble_pair",
    )(me, *sources)


def assemble_kernel(me_ref, *refs, heads):
    turn = pl.program_id(0)
    out_ref = refs[-1]
    for k in range((len(refs) - 1) // heads):

        @pl.when(turn == k)
        def _():
            for j in range(heads):
                out_ref[0, j] = refs[k * heads + j][...]


def assemble(parts, me):
    heads, chunks = len(parts), len(parts[0])
    height, count = parts[0][0].shape
    sources = [parts[j][k] for k in range(chunks) for j in range(heads)]
    return pl.pallas_call(
        functools.partial(assemble_kernel, heads=heads),
        grid_spec=pltpu.PrefetchScalarGridSpec(
            num_scalar_prefetch=1,
            grid=(chunks,),
            in_specs=[fixed((height, count))] * (chunks * heads),
            out_specs=pl.BlockSpec((1, heads, height, count), lambda k, m: (m[0] ^ k, 0, 0, 0)),
        ),
        out_shape=jax.ShapeDtypeStruct((chunks, heads, height, count), bf16),
        compiler_params=pltpu.CompilerParams(vmem_limit_bytes=VMEM),
        cost_estimate=pl.CostEstimate(
            flops=0, bytes_accessed=4 * chunks * heads * height * count, transcendentals=0
        ),
        name="assemble",
    )(me, *sources)


def tap_rows(cell_ref, frac_ref, live, plane, points):
    cell = cell_ref[0, plane : plane + 1, points]
    row = cell // (2 * G)
    col = cell - row * (2 * G)
    across = frac_ref[0, 2 * plane : 2 * plane + 1, points]
    downward = frac_ref[0, 2 * plane + 1 : 2 * plane + 2, points]
    half = lax.broadcasted_iota(jnp.int32, (G, cell.shape[1]), 0) * 2

    def spread(start, fraction, odd, gate):
        place = half + odd
        return jnp.where(
            place == start,
            (1.0 - fraction) * gate,
            jnp.where(place == start + 1, fraction * gate, 0.0),
        )

    return (
        [spread(row, downward, odd, live) for odd in range(2)],
        [spread(col, across, odd, 1.0) for odd in range(2)],
    )


def tap_table(table_ref, down, side):
    for ty in range(G):
        table_ref[ty * G : (ty + 1) * G, :] = lower(down[ty : ty + 1, :] * side)


def sample_kernel(
    object_ref, cell_ref, frac_ref, live_ref, chunk_ref, out_ref, table_ref, picked_ref, plane_ref, *, width
):
    turn = pl.program_id(1)

    @pl.when(turn == 0)
    def _():
        chunks = chunk_ref.shape[1]
        rows = TOK_OBJ // (2 * chunks)
        for r in range(chunks):
            for s in range(2):
                start = (s * chunks + r) * rows
                plane_ref[:, start : start + rows] = chunk_ref[0, r, :, s * rows : (s + 1) * rows]

    lanes = pl.ds(pl.multiple_of(turn * width, width), width)
    live = jnp.concatenate([live_ref[0]] * (width // RB), axis=1)
    picked = jnp.zeros((CH, width), f32)
    slot = 0
    for plane in range(3):
        downs, sides = tap_rows(cell_ref, frac_ref, live, plane, lanes)
        for dy in range(2):
            for dx in range(2):
                tap_table(table_ref.at[slot], downs[dy], sides[dx])
                part = (2 * dy + dx) * CH
                features = plane_ref[part : part + CH, plane * PIX : (plane + 1) * PIX]
                picked = picked + dot(features, table_ref[slot], NN)
                slot = 1 - slot
    picked_ref[:, lanes] = picked

    @pl.when(turn == pl.num_programs(1) - 1)
    def _():
        for s in range(out_ref.shape[1] // CH):
            out_ref[:, s * CH : (s + 1) * CH] = lower(picked_ref[:, s * RB : (s + 1) * RB].T)


def sample_points(planes, owner, cells, fractions, live):
    points = cells.shape[2]
    width = 512
    out = (RB, points // RB * CH)
    return pl.pallas_call(
        functools.partial(sample_kernel, width=width),
        grid_spec=pltpu.PrefetchScalarGridSpec(
            num_scalar_prefetch=1,
            grid=(1, points // width),
            in_specs=[
                fixed((1, 3, points)),
                fixed((1, 6, points)),
                fixed((1, 1, RB)),
                pl.BlockSpec((1,) + planes.shape[1:], lambda b, t, o: (o[b], 0, 0, 0)),
            ],
            out_specs=fixed(out),
            scratch_shapes=[
                pltpu.VMEM((2, PIX, width), bf16),
                pltpu.VMEM((CH, points), f32),
                pltpu.VMEM((4 * CH, TOK_OBJ), bf16),
            ],
        ),
        out_shape=jax.ShapeDtypeStruct(out, bf16),
        compiler_params=pltpu.CompilerParams(vmem_limit_bytes=VMEM),
        cost_estimate=pl.CostEstimate(
            flops=points * 3 * 4096 * 2 * 256, bytes_accessed=5 * 2**20, transcendentals=0
        ),
        name="sample_points",
    )(owner, cells, fractions, live, planes)


def scatter_kernel(object_ref, cell_ref, frac_ref, live_ref, grad_ref, out_ref, table_ref, rows_ref, total_ref, *, width):
    block = pl.program_id(0)
    turn = pl.program_id(1)
    owner = object_ref[block]

    @pl.when((block == 0) & (turn == 0))
    def _():
        total_ref[...] = jnp.zeros_like(total_ref)

    @pl.when(turn == 0)
    def _():
        for s in range(SAMP):
            rows_ref[:, s * RB : (s + 1) * RB] = grad_ref[:, s * CH : (s + 1) * CH].T

    lanes = pl.ds(pl.multiple_of(turn * width, width), width)
    live = jnp.concatenate([live_ref[0]] * (width // RB), axis=1)
    grads = rows_ref[:, lanes]
    slot = 0
    for plane in range(3):
        downs, sides = tap_rows(cell_ref, frac_ref, live, plane, lanes)
        for dy in range(2):
            for dx in range(2):
                tap_table(table_ref.at[slot], downs[dy], sides[dx])
                part = (2 * dy + dx) * CH
                total_ref[owner, part : part + CH, plane * PIX : (plane + 1) * PIX] += dot(
                    grads, table_ref[slot], NT
                )
                slot = 1 - slot

    @pl.when((block == pl.num_programs(0) - 1) & (turn == pl.num_programs(1) - 1))
    def _():
        objects, chunks = out_ref.shape[:2]
        rows = TOK_OBJ // (2 * chunks)
        for o in range(objects):
            for r in range(chunks):
                for s in range(2):
                    start = (s * chunks + r) * rows
                    out_ref[o, r, :, s * rows : (s + 1) * rows] = lower(
                        total_ref[o, :, start : start + rows]
                    )


def scatter_points(grads, owners, cells, fractions, live, objects, chunks):
    blocks = owners.shape[0]
    points = RB * SAMP
    width = 512
    shape = (objects, 4 * CH, TOK_OBJ)
    spread = (objects, chunks, 4 * CH, TOK_OBJ // chunks)
    return pl.pallas_call(
        functools.partial(scatter_kernel, width=width),
        grid_spec=pltpu.PrefetchScalarGridSpec(
            num_scalar_prefetch=1,
            grid=(blocks, points // width),
            in_specs=[
                pl.BlockSpec((1, 3, points), lambda b, t, o: (b, 0, 0)),
                pl.BlockSpec((1, 6, points), lambda b, t, o: (b, 0, 0)),
                pl.BlockSpec((1, 1, RB), lambda b, t, o: (b, 0, 0)),
                pl.BlockSpec((RB, SAMP * CH), lambda b, t, o: (b, 0)),
            ],
            out_specs=fixed(spread),
            scratch_shapes=[
                pltpu.VMEM((2, PIX, width), bf16),
                pltpu.VMEM((CH, points), bf16),
                pltpu.VMEM(shape, f32),
            ],
        ),
        out_shape=jax.ShapeDtypeStruct(spread, bf16),
        compiler_params=pltpu.CompilerParams(vmem_limit_bytes=VMEM),
        cost_estimate=pl.CostEstimate(
            flops=blocks * points * 3 * 4096 * 2 * 256,
            bytes_accessed=blocks * 5 * 2**20,
            transcendentals=0,
        ),
        name="scatter_points",
    )(owners, cells, fractions, live, grads)


SWAP = [(0, 1), (1, 0)]


def body(
    dp_axes,
    group_axes,
    tokens,
    dino,
    first_gain,
    first_shift,
    image_weight,
    cross_query,
    cross_keyval,
    cross_output,
    second_gain,
    second_shift,
    self_project,
    self_output,
    third_gain,
    third_shift,
    hidden_weight,
    hidden_bias,
    output_weight,
    deconv_weight,
    ray_mask,
    block_object,
    sample_cell,
    sample_frac,
    out_grad,
    sampled_grad,
):
    shard_axes = ("h",) + group_axes
    every = dp_axes + shard_axes
    outer, core = dp_axes
    group = 2 ** len(group_axes)
    heads = H // group
    half = lax.axis_index("h")
    side = lax.axis_index(core)
    over = lax.axis_index(outer)
    place = lax.axis_index(group_axes)
    me = place.reshape(1).astype(jnp.int32)
    rows = tokens.shape[0]
    count = 2 * rows
    patches = 2 * dino.shape[0]
    share = first_gain.shape[0]
    join = lax.optimization_barrier

    def own_object(values):
        mine = lax.dynamic_index_in_dim(values, half, 1, keepdims=False)
        other = lax.dynamic_index_in_dim(values, 1 - half, 1, keepdims=False)
        got = lax.ppermute(other, "h", SWAP)
        return jnp.concatenate(
            [jnp.where(half == 0, mine, got), jnp.where(half == 0, got, mine)], axis=0
        )

    def gather(pieces):
        return lax.all_gather(jnp.concatenate(pieces, axis=1), every, axis=0, tiled=True)

    def exchange(chunks):
        return [chunks[0]] + [
            lax.ppermute(chunks[k], group_axes, [(i, i ^ k) for i in range(group)])
            for k in range(1, group)
        ]

    def after(values, *other):
        return join((values, other))[0]

    def in_turn(call, *lists):
        done = []
        for operands in zip(*lists):
            done.append(call(*(after(operands, done[-1]) if done else operands)))
        return done

    def exchange_all(parts):
        done = []
        for chunks in parts:
            if done:
                chunks, done[-1] = join((chunks, done[-1]))
            done.append(exchange(chunks))
        return done

    columns = jnp.stack(
        [first_gain, first_shift, second_gain, second_shift, third_gain, third_shift], axis=1
    )
    columns = jnp.concatenate([columns, hidden_bias.reshape(share, FF // D)], axis=1)
    columns = jnp.pad(columns, ((0, 0), (0, 128 - columns.shape[1])))
    early = gather(
        [
            lower(cross_query),
            lower(cross_keyval),
            lower(image_weight).reshape(share, DINO),
            lower(columns),
        ]
    )
    query_w = early[:, :D]
    keyval_w = early[:, D : 3 * D]
    image_w = early[:, 3 * D : 3 * D + DINO].reshape(DINO, D)
    vectors = widen(early[:, 3 * D + DINO :])
    gain_a, shift_a, gain_b, shift_b, gain_c, shift_c = [vectors[:, i] for i in range(6)]
    bias = vectors[:, 6 : 6 + FF // D].reshape(FF)

    blocks = ray_mask.shape[0] // RB

    def by_sample(values):
        kinds = values.shape[0]
        values = values.reshape(kinds, blocks, RB, SAMP)
        return values.transpose(1, 0, 3, 2).reshape(blocks, kinds, SAMP * RB)

    cells = by_sample(sample_cell)
    fractions = by_sample(sample_frac)
    live = widen(ray_mask).reshape(blocks, 1, RB)
    plane_grad = scatter_points(sampled_grad, block_object, cells, fractions, live, 2, group)
    token_low = own_object(tokens)
    dino_values = own_object(dino)
    plane_grad, token_low, dino_values = join((plane_grad, token_low, dino_values))
    plane_low = lax.psum_scatter(
        plane_grad.reshape(2 * group * 4 * CH, count), shard_axes, scatter_dimension=0, tiled=True
    )
    token_values = widen(token_low)

    normed_full, unit_a, inverse_a = normalize(token_values, gain_a, shift_a)
    normed_a = lower(normed_full)
    image = lower(dot(dino_values, image_w, NN))
    queries = lower(dot(query_w, normed_a, ((0,), (1,)))).reshape(group, heads, HD, count)
    keyvals = lower(dot(keyval_w, image, ((0,), (1,)))).reshape(group, heads, 2 * HD, patches)
    cross_in = exchange_all(split_pair(queries, keyvals, me))
    middle = [lower(cross_output), lower(self_project), lower(self_output)]
    late = [lower(hidden_weight), lower(deconv_weight)]
    output_w = lower(output_weight)
    middle, late = gather(middle), gather(late)
    output_w = lax.all_gather(output_w, every, axis=0, tiled=True)
    cross_w = middle[:, :D]
    project_w = middle[:, D : 4 * D]
    self_w = middle[:, 4 * D :]
    hidden_w = late[:, :FF]
    deconv_w = late[:, FF:]
    cross_out = in_turn(lambda x: attend_forward(x, count), cross_in)
    cross_mix = assemble([exchange(o) for o, _ in cross_out], me).reshape(D, count)
    after_cross = token_values + dot(cross_mix, cross_w, TN)

    normed_full, unit_b, inverse_b = normalize(after_cross, gain_b, shift_b)
    normed_b = lower(normed_full)
    projected = lower(dot(project_w, normed_b, ((0,), (1,)))).reshape(group, heads, 3 * HD, count)
    projected, out_grad = join((split(projected, me), out_grad))
    out_cotangent = own_object(out_grad)
    self_qkv = exchange_all(projected)
    self_out = in_turn(lambda x: attend_forward(x, count), self_qkv)
    out_cotangent = after(out_cotangent, self_out[-1])
    self_mix = assemble([exchange(o) for o, _ in self_out], me).reshape(D, count)
    after_self = after_cross + dot(self_mix, self_w, TN)

    normed_full, unit_c, inverse_c = normalize(after_self, gain_c, shift_c)
    normed_c = lower(normed_full)
    hidden = dot(normed_c, hidden_w, NN) + bias
    activated = lower(gelu(hidden))
    result_low = lower(after_self + dot(activated, output_w, NN))

    planes = lower(dot(deconv_w, result_low, ((0,), (1,))))
    plane_all = lax.all_gather(planes, shard_axes, axis=0, tiled=True)
    plane_all = plane_all.reshape(2, group, 4 * CH, count)


    def grad_job(left, axis, right, right_axis, pieces=1):
        quarter = left.shape[axis] // 4
        dims = ((1 - axis,), (right_axis,))

        def block(y, c):
            return lax.dynamic_slice_in_dim(left, (2 * y + c) * quarter, quarter, axis)

        def blocks_of(c):
            parts = [block(1 - over, c), block(over, c)]
            return parts if quarter > 512 else [jnp.concatenate(parts, axis=axis)]

        others = [lower(dot(x, right, dims)) for x in blocks_of(1 - side)]
        others = yield (), [(x, core) for x in others]
        sums = [lower(dot(x, right, dims) + widen(g)) for x, g in zip(blocks_of(side), others)]
        away, kept = sums if quarter > 512 else (sums[0][:quarter], sums[0][quarter:])
        width = away.shape[1] // pieces
        got = []
        for i in range(pieces):
            got += yield kept, [(away[:, i * width : (i + 1) * width], outer)]
        return lower(widen(kept) + widen(jnp.concatenate(got, axis=1) if pieces > 1 else got[0]))

    def chain_job(values):
        left = list(shard_axes)
        values = [v.reshape((2,) * len(left) + (-1, v.shape[-1])) for v in values]
        for axis in group_axes[::-1] + ("h",):
            dim, here = left.index(axis), lax.axis_index(axis)
            left.pop(dim)
            away = [lax.dynamic_index_in_dim(v, 1 - here, dim, keepdims=False) for v in values]
            kept = [lax.dynamic_index_in_dim(v, here, dim, keepdims=False) for v in values]
            got = yield kept, [(x, axis) for x in away]
            values = [widen(k) + widen(g) for k, g in zip(kept, got)]
            if left:
                values = [lower(v) for v in values]
        return values

    def full_job(*args):
        part = yield from grad_job(*args)
        return (yield from chain_job([part]))[0]

    def together(runs):
        results, got = [None] * len(runs), [None] * len(runs)
        left = list(range(len(runs)))
        while True:
            kept, sent, sizes = [], [], []
            for i in list(left):
                try:
                    stand, moves = next(runs[i]) if got[i] is None else runs[i].send(got[i])
                except StopIteration as end:
                    results[i] = end.value
                    left.remove(i)
                    continue
                kept.append(stand)
                sent += moves
                sizes.append(len(moves))
            if not left:
                return results
            arrived = yield kept, sent
            for i, size in zip(left, sizes):
                got[i], arrived = arrived[:size], arrived[size:]

    def side_job(*runs):
        parts = yield from together(runs)
        return (yield from chain_job([jnp.concatenate(parts, axis=1)]))[0]

    def swap_job(arrays, pieces):
        done = []
        for values in arrays:
            size = values.shape[0] // 2
            step = size // pieces
            mine = lax.dynamic_slice_in_dim(values, half * size, size, 0)
            away = lower(lax.dynamic_slice_in_dim(values, (1 - half) * size, size, 0))
            got = []
            for i in range(pieces):
                got += yield done, [(away[i * step : (i + 1) * step], "h")]
            got = jnp.concatenate(got, axis=0).astype(mine.dtype)
            done.append(
                jnp.stack([jnp.where(half == 0, mine, got), jnp.where(half == 0, got, mine)], axis=1)
            )
        return done

    jobs, sums_of = {}, {}

    def turn(call, operands):
        kept, sent = {}, {}
        for name in list(jobs):
            job, got = jobs[name]
            try:
                kept[name], sent[name] = next(job) if got is None else job.send(got)
            except StopIteration as end:
                sums_of[name] = end.value
                del jobs[name]
        arrays = {name: [x for x, _ in sent[name]] for name in sent}
        operands, arrays, _ = join((operands, arrays, kept))
        moved = {
            name: [lax.ppermute(x, axis, SWAP) for x, (_, axis) in zip(arrays[name], sent[name])]
            for name in sent
        }
        raw = call(*operands)
        moved, settled = join((moved, raw))
        for name in sent:
            jobs[name] = (jobs[name][0], moved[name])
        return raw, settled

    def start(name, job):
        jobs[name] = (job, None)

    result_grad = widen(out_cotangent) + dot(plane_low, deconv_w, ((0,), (1,)))
    result_low_grad = lower(result_grad)
    activated_grad = dot(result_low_grad, output_w, NT)
    _, gelu_pull = jax.vjp(gelu, hidden)
    hidden_grad = lower(gelu_pull(activated_grad)[0])
    bias_grad = jnp.sum(widen(hidden_grad), axis=0)
    back_c, gain_c_grad, shift_c_grad = normalize_back(
        dot(hidden_grad, hidden_w, NT), unit_c, inverse_c, gain_c
    )
    self_grad = result_grad + back_c

    self_low = lower(self_grad)
    self_mix_grad = lower(dot(self_w, self_low, NT)).reshape(group, heads, HD, count)
    self_dout = exchange_all(split(self_mix_grad, me))
    start("output", full_job(activated, 1, result_low_grad, 0, 2))
    gone = ()
    self_back = []
    for j in range(heads):
        if j == min(2, heads - 1):
            start("hidden", full_job(normed_c, 1, hidden_grad, 0, 2))
            start("self", full_job(self_mix, 0, self_low, 0))
            start("deconv", full_job(result_low, 1, plane_low, 1))
        if j == min(1, heads - 1):
            start("tokens_out", swap_job([result_low], 4))
        raw, gone = turn(
            lambda s, g, o: attend_backward(s, g, *o),
            (after(self_qkv[j], gone), self_dout[j], self_out[j]),
        )
        self_back.append(raw)

    project_grad = assemble([exchange(g) for g in self_back], me).reshape(3 * D, count)
    back_b, gain_b_grad, shift_b_grad = normalize_back(
        dot(project_grad, project_w, ((0,), (1,))), unit_b, inverse_b, gain_b
    )
    cross_grad = self_grad + back_b

    cross_low = lower(cross_grad)
    cross_mix_grad = lower(dot(cross_w, cross_low, NT)).reshape(group, heads, HD, count)
    cross_dout = exchange_all(split(cross_mix_grad, me))
    start(
        "project",
        side_job(grad_job(normed_b, 1, project_grad, 1, 2), grad_job(cross_mix, 0, cross_low, 0)),
    )
    cut = heads // 2
    cross_back, parts, found = [], [], []

    def kv_grads(first, last):
        queries, keyvals = assemble_pair(parts[first:last], me, count)
        queries = queries.reshape(-1, count)
        keyvals = keyvals.reshape(-1, patches)
        start(f"keyval{first}", grad_job(image, 1, keyvals, 1))
        start(f"query{first}", grad_job(normed_a, 1, queries, 1))
        found.append((queries, keyvals))

    for j in range(heads):
        if cut and j == cut + 1:
            parts[:cut] = after(parts[:cut], gone)
            kv_grads(0, cut)
        raw, gone = turn(
            lambda s, g, o: attend_backward(s, g, *o),
            (after(cross_in[j], gone), cross_dout[j], cross_out[j]),
        )
        cross_back.append(raw)
        parts.append(exchange(raw))

    pieces = [(b, s) for b in range(blocks) for s in range(2)]
    span = SAMP * RB // 2
    sampled = {}

    def sample_turn(gone):
        b, s = pieces[len(sampled)]
        operands = (
            plane_all,
            block_object[b : b + 1],
            cells[b : b + 1, :, s * span : (s + 1) * span],
            fractions[b : b + 1, :, s * span : (s + 1) * span],
            live[b : b + 1],
        )
        _, sampled[b, s] = turn(sample_points, after(operands, gone))
        return sampled[b, s]

    gone = sample_turn(gone)
    parts[cut:] = after(parts[cut:], gone)
    kv_grads(cut, heads)

    def merge(pieces, height):
        folded = [p.reshape(group, -1, height, p.shape[-1]) for p in pieces]
        return jnp.concatenate(folded, axis=1).reshape(-1, pieces[0].shape[-1])

    def merge_columns(pieces, height):
        folded = [p.reshape(p.shape[0], group, -1, height) for p in pieces]
        return jnp.concatenate(folded, axis=2).reshape(pieces[0].shape[0], -1)

    query_back = merge([f[0] for f in found], HD)
    keyval_back = merge([f[1] for f in found], 2 * HD)
    image_grad = lower(dot(keyval_back, keyval_w, ((0,), (1,))))
    start("image", grad_job(dino_values, 1, image_grad, 0))
    back_a, gain_a_grad, shift_a_grad = normalize_back(
        dot(query_back, query_w, ((0,), (1,))), unit_a, inverse_a, gain_a
    )
    dino_grad = dot(image_grad, image_w, NT)
    tokens_grad = cross_grad + back_a

    sums = jnp.stack(
        [gain_a_grad, shift_a_grad, gain_b_grad, shift_b_grad, gain_c_grad, shift_c_grad], axis=1
    )
    sums = jnp.concatenate([sums, bias_grad.reshape(D, FF // D)], axis=1)
    sums = jnp.pad(sums, ((0, 0), (0, 128 - sums.shape[1])))

    def vector_job():
        def quarter_rows(y, c):
            return lax.dynamic_slice_in_dim(sums, (2 * y + c) * (D // 4), D // 4, 0)

        others = yield (), [(quarter_rows(y, 1 - side), core) for y in (1 - over, over)]
        away = quarter_rows(1 - over, side) + others[0]
        kept = quarter_rows(over, side) + others[1]
        got = yield kept, [(away, outer)]
        return lower(kept + got[0])

    start("vectors", vector_job())
    (dino_grad, tokens_grad), gone = join(((dino_grad, tokens_grad), gone))
    start("swap", swap_job([dino_grad, tokens_grad], 2))
    gone = sample_turn(gone)
    gone = sample_turn(gone)
    names = [f"{kind}{at}" for at in ([0, cut] if cut else [0]) for kind in ("keyval", "query")]
    names += ["vectors", "image"]
    while any(name in jobs for name in names):
        _, gone = turn(lambda *x: x, (gone,))
    last_part = jnp.concatenate([sums_of[name] for name in names[:-1]], axis=1)
    start("last", chain_job([last_part, sums_of["image"]]))
    gone = sample_turn(gone)
    while jobs:
        _, gone = turn(lambda *x: x, (gone,))
    last, image_sum = sums_of["last"]
    dino_grad, tokens_grad = sums_of["swap"]
    (tokens_out,) = sums_of["tokens_out"]
    sampled = jnp.concatenate(
        [jnp.concatenate([sampled[b, s] for s in range(2)], axis=1) for b in range(blocks)], axis=0
    )

    keyval_sums, query_sums = [], []
    at = 0
    for width in [group * n * HD for n in ([cut, heads - cut] if cut else [heads])]:
        keyval_sums.append(last[:, at : at + 2 * width])
        query_sums.append(last[:, at + 2 * width : at + 3 * width])
        at += 3 * width
    vector_sums = last[:, at:]

    return (
        tokens_out,
        sampled,
        tokens_grad,
        dino_grad,
        vector_sums[:, 0],
        vector_sums[:, 1],
        image_sum,
        merge_columns(query_sums, HD),
        merge_columns(keyval_sums, 2 * HD),
        sums_of["project"][:, 3 * D :],
        vector_sums[:, 2],
        vector_sums[:, 3],
        sums_of["project"][:, : 3 * D],
        sums_of["self"],
        vector_sums[:, 4],
        vector_sums[:, 5],
        sums_of["hidden"],
        vector_sums[:, 6 : 6 + FF // D].reshape(share * (FF // D)),
        sums_of["output"],
        sums_of["deconv"],
    )


def solution(mesh):
    dp_bits = mesh.shape["dp"].bit_length() - 1
    shard_bits = mesh.shape["shard"].bit_length() - 1
    dp_axes = tuple(f"d{i}" for i in range(dp_bits))
    group_axes = tuple(f"r{i}" for i in range(shard_bits - 1))
    shard_axes = ("h",) + group_axes
    fine = Mesh(mesh.devices.reshape((2,) * (dp_bits + shard_bits)), dp_axes + shard_axes)
    every = dp_axes + shard_axes
    rows = P(shard_axes, dp_axes, None)
    vector = P(every)
    matrix = P(every, None)
    points = P(None, every)
    return jax.shard_map(
        functools.partial(body, dp_axes, group_axes),
        mesh=fine,
        in_specs=(
            rows, rows,
            vector, vector, matrix, matrix, matrix, matrix,
            vector, vector, matrix, matrix,
            vector, vector, matrix, vector, matrix, matrix,
            vector, vector, points, points, rows, matrix,
        ),
        out_specs=(
            rows, matrix, rows, rows,
            vector, vector, matrix, matrix, matrix, matrix,
            vector, vector, matrix, matrix,
            vector, vector, matrix, vector, matrix, matrix,
        ),
        check_vma=False,
    )
```

time: 1500 us -> 1450 us (0.967)
  waiting for transfers between devices: 370 us -> 319 us
  other arithmetic: 62.4 us -> 92 us
  matrix products: 221 us -> 198 us
    ppermute x33 -> x58, waiting for transfers between devices: 164 us -> 76.3 us  [turn(): lax.ppermute(x, axis, SWAP)]
    all_gather x3, waiting for transfers between devices: 7.14 us -> 51.9 us  [gather(): lax.all_gather(jnp.concatenate(pieces, axis=1), every, axis=0, tiled=True)]
    reshape x5 -> x6, local copies, waits for them, and re-layouts: 38.3 us -> 2.19 us  [the longest x2 1.71 us: merge_columns(): return jnp.concatenate(folded, axis=2).reshape(pieces[0].shape[0], -1)]
    ppermute x120 -> x96, starting transfers between devices: 137 us -> 110 us  [exchange(): lax.ppermute(chunks[k], group_axes, [(i, i ^ k) for i in range(group)])]
    dot_general x54 -> x42, matrix products: 221 us -> 198 us  [dot(): lax.dot_general(left, right, (dims, ((), ())), preferred_element_type=f32)]
    convert_element_type x19 -> x42, other arithmetic: 26.5 us -> 48.9 us  [lower(): return value.astype(bf16)]
    reduce_scatter x7 -> x1, waiting for transfers between devices: 22 us -> 0.01 us  [body(): lax.psum_scatter(plane_grad.reshape(2 * group * 4 * CH, count), shard_axe...]
    ppermute x33 -> x58, starting transfers between devices: 32.4 us -> 48.1 us  [turn(): lax.ppermute(x, axis, SWAP)]
  transfers between devices with their start and end apart: 168 -> 163, of which waited for: 44 -> 50; matrix products, arithmetic and copies ran while one was open for 22% -> 18% of each run, Pallas kernels for 35% -> 36%
where the time goes in v2:
time: 1450 us; the launch traced here: 1440 us
  Pallas kernels  520 us (36%)
  waiting for transfers between devices  319 us (22%)
  matrix products  198 us (14%)
  starting transfers between devices  167 us (12%)
  local copies, waits for them, and re-layouts  123 us (8%)
  other arithmetic  92 us (6%)
  between operations  18.5 us (1%)
    pallas_call x8, Pallas kernels, attend_backward(): pl.pallas_call(functools.partial(backward_kernel, chunks=chunks, block=bl...  230 us
    dot_general x42, matrix products, dot(): lax.dot_general(left, right, (dims, ((), ())), preferred_element_type=f32)  198 us
    ppermute x96, waiting for transfers between devices, exchange(): lax.ppermute(chunks[k], group_axes, [(i, i ^ k) for i in range(group)])  191 us
    pallas_call x8, Pallas kernels, attend_forward(): pl.pallas_call(functools.partial(forward_kernel, chunks=chunks, block=blo...  124 us
    ppermute x96, starting transfers between devices, exchange(): lax.ppermute(chunks[k], group_axes, [(i, i ^ k) for i in range(group)])  110 us
    ppermute x58, waiting for transfers between devices, turn(): lax.ppermute(x, axis, SWAP)  76.3 us
    pallas_call x1, Pallas kernels, scatter_points(): pl.pallas_call(functools.partial(scatter_kernel, width=width), grid_spec=...  72.2 us
    pallas_call x4, Pallas kernels, sample_points(): pl.pallas_call(functools.partial(sample_kernel, width=width), grid_spec=p...  55.9 us
  transfers between devices with their start and end apart: 163, of which 50 were waited for; matrix products, arithmetic and copies ran while one was open for 18% of the time, Pallas kernels for 36%

profile of v2, /device:TPU:0, one launch (start us, length us, event | category | flops | bytes accessed | tf_op | source)
XLA Modules:
  0.0 1437.4 jit_solution(15248507798878378605)
XLA Ops:
  41.6 72.2 %scatter_points.1 = bf16[2,4,320,768]{3,2,1,0:T(8,128)(2,1)} custom-call(s32[2]{0:T(128)} %object_ref.1, s32[2,3,4096]{2,1,0:T(4,128)} %reshape.270.cell_ref, f32[2,6,4096]{2,1,0:T(8,128)} %reshape.271.frac_ref, f32[2,1,128]{2,1,0:T(1,128)} %bitcast.256, bf16[256,2560]{1,0:T(8,128)(2,1)} %grad_ref.1), custom_call_target="tpu_custom_call" | custom-call | flops 51539607552 | bytes 10485760 | tf_op jit(solution)/shard_map/scatter_points/pallas_call | solution.py:554
  121.1 51.9 %all-gather.6.cloned.1.call-done = bf16[1024,3968]{1,0:T(8,128)(2,1)} async-done(((bf16[32,3968]{1,0:T(8,128)(2,1)}), bf16[1024,3968]{1,0:T(8,128)(2,1)}) %all-gather.6.cloned.1.call-update) | async-done | bytes 8126480 | tf_op jit(solution)/shard_map/all_gather | solution.py:639
  190.3 6.2 convolution_convert_fusion.2
  196.5 6.1 split_pair.1
  206.9 14.5 %collective-permute-done.2.refs_1_ = bf16[64,2816]{1,0:T(8,128)(2,1)S(1)} collective-permute-done((bf16[64,2816]{1,0:T(8,128)(2,1)}, bf16[64,2816]{1,0:T(8,128)(2,1)S(1)}, u32[]{:S(2)}, u32[]{:S(2)}) %collective-permute-start.2) | collective-permute-done | bytes 360480 | tf_op jit(solution)/shard_map/ppermute | solution.py:643
  221.4 6.9 collective-permute-done.3.refs_2_
  228.3 22.3 %collective-permute-done.4.refs_3_ = bf16[64,2816]{1,0:T(8,128)(2,1)S(1)} collective-permute-done((bf16[64,2816]{1,0:T(8,128)(2,1)}, bf16[64,2816]{1,0:T(8,128)(2,1)S(1)}, u32[]{:S(2)}, u32[]{:S(2)}) %collective-permute-start.4) | collective-permute-done | bytes 360480 | tf_op jit(solution)/shard_map/ppermute | solution.py:643
  254.1 17.3 %attend_forward.8 = (bf16[64,768]{1,0:T(8,128)(2,1)}, bf16[64,768]{1,0:T(8,128)(2,1)}, bf16[64,768]{1,0:T(8,128)(2,1)}, bf16[64,768]{1,0:T(8,128)(2,1)}, f32[4,1,768]{2,1,0:T(1,128)}) custom-call(bf16[64,2816]{1,0:T(8,128)(2,1)} %get-tuple-element.956.refs_0_, bf16[64,2816]{1,0:T(8,128)(2,1)} %copy-done.184, bf16[64,2816]{1,0:T(8,128)(2,1)} %copy-done.185, ...), custom_call_target="tpu_custom_call" | custom-call | flops 12884901888 | bytes 1048576 | tf_op jit(solution)/shard_map/attend_forward/pallas_call | solution.py:145
  276.4 8.9 collective-permute-done.7.refs_3_
  289.4 17.3 %attend_forward.9 = (bf16[64,768]{1,0:T(8,128)(2,1)}, bf16[64,768]{1,0:T(8,128)(2,1)}, bf16[64,768]{1,0:T(8,128)(2,1)}, bf16[64,768]{1,0:T(8,128)(2,1)}, f32[4,1,768]{2,1,0:T(1,128)}) custom-call(bf16[64,2816]{1,0:T(8,128)(2,1)} %get-tuple-element.1002.refs_0_, bf16[64,2816]{1,0:T(8,128)(2,1)} %copy-done.181, bf16[64,2816]{1,0:T(8,128)(2,1)} %copy-done.182, ...), custom_call_target="tpu_custom_call" | custom-call | flops 12884901888 | bytes 1048576 | tf_op jit(solution)/shard_map/attend_forward/pallas_call | solution.py:145
  307.2 7.0 collective-permute-done.9.refs_2_
  317.8 17.4 %attend_forward.10 = (bf16[64,768]{1,0:T(8,128)(2,1)}, bf16[64,768]{1,0:T(8,128)(2,1)}, bf16[64,768]{1,0:T(8,128)(2,1)}, bf16[64,768]{1,0:T(8,128)(2,1)}, f32[4,1,768]{2,1,0:T(1,128)}) custom-call(bf16[64,2816]{1,0:T(8,128)(2,1)} %get-tuple-element.1048.refs_0_, bf16[64,2816]{1,0:T(8,128)(2,1)} %copy-done.179, bf16[64,2816]{1,0:T(8,128)(2,1)} %copy-done.180, ...), custom_call_target="tpu_custom_call" | custom-call | flops 12884901888 | bytes 1048576 | tf_op jit(solution)/shard_map/attend_forward/pallas_call | solution.py:145
  343.3 17.2 %attend_forward.11 = (bf16[64,768]{1,0:T(8,128)(2,1)}, bf16[64,768]{1,0:T(8,128)(2,1)}, bf16[64,768]{1,0:T(8,128)(2,1)}, bf16[64,768]{1,0:T(8,128)(2,1)}, f32[4,1,768]{2,1,0:T(1,128)}) custom-call(bf16[64,2816]{1,0:T(8,128)(2,1)} %get-tuple-element.1096.refs_0_, bf16[64,2816]{1,0:T(8,128)(2,1)} %copy-done.175, bf16[64,2816]{1,0:T(8,128)(2,1)} %copy-done.176, ...), custom_call_target="tpu_custom_call" | custom-call | flops 12884901888 | bytes 1048576 | tf_op jit(solution)/shard_map/attend_forward/pallas_call | solution.py:145
  381.7 7.3 fusion.8
  389.0 5.7 split.3
  403.8 15.1 %collective-permute-done.27.refs_2_ = bf16[192,768]{1,0:T(8,128)(2,1)S(1)} collective-permute-done((bf16[192,768]{1,0:T(8,128)(2,1)}, bf16[192,768]{1,0:T(8,128)(2,1)S(1)}, u32[]{:S(2)}, u32[]{:S(2)}) %collective-permute-start.27) | collective-permute-done | bytes 294944 | tf_op jit(solution)/shard_map/ppermute | solution.py:643
  418.8 6.8 collective-permute-done.28.refs_3_
  429.1 13.6 attend_forward.12
  445.6 8.8 collective-permute-done.31.refs_3_
  455.1 13.7 attend_forward.13
  471.9 5.8 collective-permute-done.34.refs_3_
  482.0 13.8 attend_forward.14
  500.8 7.7 collective-permute-done.37.refs_3_
  512.1 13.6 attend_forward.15
  549.1 9.3 fusion.2
  558.4 17.7 %convert_reduce_fusion = (f32[4096]{0:T(1024)}, bf16[768,4096]{1,0:T(8,128)(2,1)S(1)}, bf16[768,4096]{1,0:T(8,128)(2,1)}) fusion(f32[768,4096]{1,0:T(8,128)} %fusion.2, f32[4096]{0:T(1024)S(1)} %copy-done.171, bf16[768,1024]{1,0:T(8,128)(2,1)S(1)} %get-tuple-element.1449, bf16[4096,1024]{1,0:T(8,128)(2,1)} %all-gather.12.cloned.1.call-done), kind=kOutput, calls=%fused_computation | convolution fusion | flops 6499069952 | bytes 35160064 | tf_op jit(solution)/shard_map/dot_general | solution.py:44
  576.1 13.2 add_convert_fusion.8
  590.9 11.7 multiply_reduce_fusion
  605.9 5.7 fusion.55
  618.5 5.4 fusion.62
  641.7 8.2 convolution_convert_fusion
  657.9 7.9 collective-permute-done.55.refs_6_
  673.5 24.8 %attend_backward.8 = (bf16[192,768]{1,0:T(8,128)(2,1)}, bf16[192,768]{1,0:T(8,128)(2,1)}, bf16[192,768]{1,0:T(8,128)(2,1)}, bf16[192,768]{1,0:T(8,128)(2,1)}) custom-call(bf16[192,768]{1,0:T(8,128)(2,1)} %get-tuple-element.816.refs_0_, bf16[192,768]{1,0:T(8,128)(2,1)} %copy-done.187, bf16[192,768]{1,0:T(8,128)(2,1)} %copy-done.189, ...), custom_call_target="tpu_custom_call" | custom-call | flops 18874368000 | bytes 1572864 | tf_op jit(solution)/shard_map/attend_backward/pallas_call | solution.py:247
  707.6 5.9 fusion.81
  716.4 25.1 %attend_backward.10 = (bf16[192,768]{1,0:T(8,128)(2,1)}, bf16[192,768]{1,0:T(8,128)(2,1)}, bf16[192,768]{1,0:T(8,128)(2,1)}, bf16[192,768]{1,0:T(8,128)(2,1)}) custom-call(bf16[192,768]{1,0:T(8,128)(2,1)} %get-tuple-element.876.refs_0_, bf16[192,768]{1,0:T(8,128)(2,1)} %copy-done.196, bf16[192,768]{1,0:T(8,128)(2,1)} %copy-done.197, ...), custom_call_target="tpu_custom_call" | custom-call | flops 18874368000 | bytes 1572864 | tf_op jit(solution)/shard_map/attend_backward/pallas_call | solution.py:247
  741.6 19.9 %collective-permute-done.59 = bf16[1024,512]{1,0:T(8,128)(2,1)} collective-permute-done((bf16[1024,512]{1,0:T(8,128)(2,1)}, bf16[1024,512]{1,0:T(8,128)(2,1)}, u32[]{:S(2)}, u32[]{:S(2)}) %collective-permute-start.59) | collective-permute-done | bytes 1048608 | tf_op jit(solution)/shard_map/ppermute | solution.py:839
  762.4 25.2 %attend_backward.9 = (bf16[192,768]{1,0:T(8,128)(2,1)}, bf16[192,768]{1,0:T(8,128)(2,1)}, bf16[192,768]{1,0:T(8,128)(2,1)}, bf16[192,768]{1,0:T(8,128)(2,1)}) custom-call(bf16[192,768]{1,0:T(8,128)(2,1)} %get-tuple-element.837.refs_0_, bf16[192,768]{1,0:T(8,128)(2,1)} %copy-done.193, bf16[192,768]{1,0:T(8,128)(2,1)} %copy-done.194, ...), custom_call_target="tpu_custom_call" | custom-call | flops 18874368000 | bytes 1572864 | tf_op jit(solution)/shard_map/attend_backward/pallas_call | solution.py:247
  793.8 5.9 add_convert_fusion.1
  816.2 24.8 %attend_backward.11 = (bf16[192,768]{1,0:T(8,128)(2,1)}, bf16[192,768]{1,0:T(8,128)(2,1)}, bf16[192,768]{1,0:T(8,128)(2,1)}, bf16[192,768]{1,0:T(8,128)(2,1)}) custom-call(bf16[192,768]{1,0:T(8,128)(2,1)} %get-tuple-element.912.refs_0_, bf16[192,768]{1,0:T(8,128)(2,1)} %copy-done.188, bf16[192,768]{1,0:T(8,128)(2,1)} %copy-done.190, ...), custom_call_target="tpu_custom_call" | custom-call | flops 18874368000 | bytes 1572864 | tf_op jit(solution)/shard_map/attend_backward/pallas_call | solution.py:247
  852.8 5.8 collective-permute-done.86.refs_13_
  867.0 5.2 assemble.5
  872.2 10.8 multiply_reduce_fusion.1
  898.9 6.5 convolution_convert_fusion.1
  954.5 32.5 %attend_backward.12 = (bf16[64,2816]{1,0:T(8,128)(2,1)}, bf16[64,2816]{1,0:T(8,128)(2,1)}, bf16[64,2816]{1,0:T(8,128)(2,1)}, bf16[64,2816]{1,0:T(8,128)(2,1)}) custom-call(bf16[64,2816]{1,0:T(8,128)(2,1)} %get-tuple-element.956.refs_0_, bf16[64,2816]{1,0:T(8,128)(2,1)} %copy-done.184, bf16[64,2816]{1,0:T(8,128)(2,1)} %copy-done.185, ...), custom_call_target="tpu_custom_call" | custom-call | flops 25165824000 | bytes 2097152 | tf_op jit(solution)/shard_map/attend_backward/pallas_call | solution.py:247
  988.7 6.2 add_convert_fusion.2
  1011.0 32.5 %attend_backward.13 = (bf16[64,2816]{1,0:T(8,128)(2,1)}, bf16[64,2816]{1,0:T(8,128)(2,1)}, bf16[64,2816]{1,0:T(8,128)(2,1)}, bf16[64,2816]{1,0:T(8,128)(2,1)}) custom-call(bf16[64,2816]{1,0:T(8,128)(2,1)} %get-tuple-element.1002.refs_0_, bf16[64,2816]{1,0:T(8,128)(2,1)} %copy-done.181, bf16[64,2816]{1,0:T(8,128)(2,1)} %copy-done.182, ...), custom_call_target="tpu_custom_call" | custom-call | flops 25165824000 | bytes 2097152 | tf_op jit(solution)/shard_map/attend_backward/pallas_call | solution.py:247
  1060.1 32.2 %attend_backward.14 = (bf16[64,2816]{1,0:T(8,128)(2,1)}, bf16[64,2816]{1,0:T(8,128)(2,1)}, bf16[64,2816]{1,0:T(8,128)(2,1)}, bf16[64,2816]{1,0:T(8,128)(2,1)}) custom-call(bf16[64,2816]{1,0:T(8,128)(2,1)} %get-tuple-element.1048.refs_0_, bf16[64,2816]{1,0:T(8,128)(2,1)} %copy-done.179, bf16[64,2816]{1,0:T(8,128)(2,1)} %copy-done.180, ...), custom_call_target="tpu_custom_call" | custom-call | flops 25165824000 | bytes 2097152 | tf_op jit(solution)/shard_map/attend_backward/pallas_call | solution.py:247
  1106.1 11.2 collective-permute-done.99.refs_2_
  1117.9 6.8 collective-permute-done.105.refs_3_
  1147.6 32.5 %attend_backward.15 = (bf16[64,2816]{1,0:T(8,128)(2,1)}, bf16[64,2816]{1,0:T(8,128)(2,1)}, bf16[64,2816]{1,0:T(8,128)(2,1)}, bf16[64,2816]{1,0:T(8,128)(2,1)}) custom-call(bf16[64,2816]{1,0:T(8,128)(2,1)} %get-tuple-element.1096.refs_0_, bf16[64,2816]{1,0:T(8,128)(2,1)} %copy-done.175, bf16[64,2816]{1,0:T(8,128)(2,1)} %copy-done.176, ...), custom_call_target="tpu_custom_call" | custom-call | flops 25165824000 | bytes 2097152 | tf_op jit(solution)/shard_map/attend_backward/pallas_call | solution.py:247
  1196.6 13.9 sample_points.4
  1217.9 5.2 collective-permute-done.133.refs_6_
  1223.1 7.6 collective-permute-done.134.refs_3_
  1230.7 5.7 collective-permute-done.136.refs_7_
  1250.8 5.8 fusion.26
  1263.7 8.1 fusion.29
  1286.1 14.1 sample_points.5
  1308.1 11.0 collective-permute-done.139
  1330.2 13.8 sample_points.6
  1344.0 12.6 collective-permute-done.148
  1368.4 14.1 sample_points.7
  1386.8 5.0 collective-permute-done.151
  1401.5 9.5 collective-permute-done.154
  1420.1 5.0 collective-permute-done.156
  (1045 shorter events, 517.6 us)
Async XLA Ops:
  8.0 165.0 %all-gather.6.cloned.1.call-start = ((), (), s32[]{:S(2)}) async-start(), calls=%async_computation.1 | async-start | bytes 8380416 | tf_op jit(solution)/shard_map/all_gather | solution.py:639
  17.2 357.3 %all-gather.8.cloned.1.call-start = ((), (), s32[]{:S(2)}) async-start(), calls=%async_computation.2 | async-start | bytes 10813440 | tf_op jit(solution)/shard_map/all_gather | solution.py:639
  20.9 510.0 %reduce-scatter.2.cloned.1.call-start = ((), (), s32[]{:S(2)}) async-start(), calls=%async_computation.5 | async-start | bytes 4423680 | tf_op jit(solution)/shard_map/reduce_scatter | solution.py:698
  25.2 88.6 %collective-permute-start.1 = (bf16[512,768]{1,0:T(8,128)(2,1)}, bf16[512,768]{1,0:T(8,128)(2,1)}, u32[]{:S(2)}, u32[]{:S(2)}) collective-permute-start(bf16[512,768]{1,0:T(8,128)(2,1)} %bitcast.210), channel_id=1, source_target_pairs={{0,4},{4,0},{1,5},{5,1},{2,6},{6,2},{3,7},{7,3},{8,12},{12,8},{9,1... | collective-permute-start | bytes 2359304 | tf_op jit(solution)/shard_map/ppermute | solution.py:633
  33.7 82.7 %collective-permute-start = (bf16[384,1024]{1,0:T(8,128)(2,1)}, bf16[384,1024]{1,0:T(8,128)(2,1)}, u32[]{:S(2)}, u32[]{:S(2)}) collective-permute-start(bf16[384,1024]{1,0:T(8,128)(2,1)} %bitcast.211), channel_id=1, source_target_pairs={{0,4},{4,0},{1,5},{5,1},{2,6},{6,2},{3,7},{7,3},{8,12},{12,8},{9,1... | collective-permute-start | bytes 2359304 | tf_op jit(solution)/shard_map/ppermute | solution.py:633
  118.0 413.1 %all-gather.10.cloned.1.call-start = ((), (), s32[]{:S(2)}) async-start(), calls=%async_computation.3 | async-start | bytes 9461760 | tf_op jit(solution)/shard_map/all_gather | solution.py:639
  120.2 438.2 %all-gather.12.cloned.1.call-start = ((), (), s32[]{:S(2)}) async-start(), calls=%async_computation.4 | async-start | bytes 8650752 | tf_op jit(solution)/shard_map/all_gather | solution.py:713
  203.9 46.7 %collective-permute-start.4 = (bf16[64,2816]{1,0:T(8,128)(2,1)}, bf16[64,2816]{1,0:T(8,128)(2,1)S(1)}, u32[]{:S(2)}, u32[]{:S(2)}) collective-permute-start(bf16[64,2816]{1,0:T(8,128)(2,1)} %get-tuple-element.627), channel_id=1, source_target_pairs={{0,3},{1,2},{2,1},{3,0},{4,7},{5,6},{6,5},{7,4},{8,11},{9,10},{10,... | collective-permute-start | bytes 1081352 | tf_op jit(solution)/shard_map/ppermute | solution.py:643
  206.8 742.1 %all-gather.14.cloned.1.call-start = ((), (), s32[]{:S(2)}) async-start(), calls=%async_computation.6 | async-start | bytes 4423680 | tf_op jit(solution)/shard_map/all_gather | solution.py:741
  250.8 34.5 %collective-permute-start.7 = (bf16[64,2816]{1,0:T(8,128)(2,1)}, bf16[64,2816]{1,0:T(8,128)(2,1)S(1)}, u32[]{:S(2)}, u32[]{:S(2)}) collective-permute-start(bf16[64,2816]{1,0:T(8,128)(2,1)} %get-tuple-element.640), channel_id=1, source_target_pairs={{0,3},{1,2},{2,1},{3,0},{4,7},{5,6},{6,5},{7,4},{8,11},{9,10},{10,... | collective-permute-start | bytes 1081352 | tf_op jit(solution)/shard_map/ppermute | solution.py:643
  271.4 68.6 %collective-permute-start.14 = (bf16[64,768]{1,0:T(8,128)(2,1)}, bf16[64,768]{1,0:T(8,128)(2,1)S(1)}, u32[]{:S(2)}, u32[]{:S(2)}) collective-permute-start(bf16[64,768]{1,0:T(8,128)(2,1)} %get-tuple-element.965.refs_9_), channel_id=1, source_target_pairs={{0,1},{1,0},{2,3},{3,2},{4,5},{5,4},{6,7},{7,6},{8,9},{9,8},{10,11... | collective-permute-start | bytes 294920 | tf_op jit(solution)/shard_map/ppermute | solution.py:643
  271.5 68.9 %collective-permute-start.18 = (bf16[64,768]{1,0:T(8,128)(2,1)}, bf16[64,768]{1,0:T(8,128)(2,1)S(1)}, u32[]{:S(2)}, u32[]{:S(2)}) collective-permute-start(bf16[64,768]{1,0:T(8,128)(2,1)} %get-tuple-element.966.refs_10_), channel_id=1, source_target_pairs={{0,2},{1,3},{2,0},{3,1},{4,6},{5,7},{6,4},{7,5},{8,10},{9,11},{10,... | collective-permute-start | bytes 294920 | tf_op jit(solution)/shard_map/ppermute | solution.py:643
  400.4 68.4 %collective-permute-start.50 = (bf16[384,1024]{1,0:T(8,128)(2,1)S(1)}, bf16[384,1024]{1,0:T(8,128)(2,1)S(1)}, u32[]{:S(2)}, u32[]{:S(2)}) collective-permute-start(bf16[384,1024]{1,0:T(8,128)(2,1)S(1)} %dynamic-slice_bitcast_fusion.8), channel_id=1, source_target_pairs={{0,4},{4,0},{1,5},{5,1},{2,6},{6,2},{3,7},{7,3},{8,12},{12,8},{9,1... | collective-permute-start | bytes 2359304 | tf_op jit(solution)/shard_map/ppermute | solution.py:633
  442.7 66.9 %collective-permute-start.38 = (bf16[64,768]{1,0:T(8,128)(2,1)}, bf16[64,768]{1,0:T(8,128)(2,1)S(1)}, u32[]{:S(2)}, u32[]{:S(2)}) collective-permute-start(bf16[64,768]{1,0:T(8,128)(2,1)} %get-tuple-element.825.refs_9_), channel_id=1, source_target_pairs={{0,1},{1,0},{2,3},{3,2},{4,5},{5,4},{6,7},{7,6},{8,9},{9,8},{10,11... | collective-permute-start | bytes 294920 | tf_op jit(solution)/shard_map/ppermute | solution.py:643
  443.2 66.8 %collective-permute-start.42 = (bf16[64,768]{1,0:T(8,128)(2,1)}, bf16[64,768]{1,0:T(8,128)(2,1)S(1)}, u32[]{:S(2)}, u32[]{:S(2)}) collective-permute-start(bf16[64,768]{1,0:T(8,128)(2,1)} %get-tuple-element.826.refs_10_), channel_id=1, source_target_pairs={{0,2},{1,3},{2,0},{3,1},{4,6},{5,7},{6,4},{7,5},{8,10},{9,11},{10,... | collective-permute-start | bytes 294920 | tf_op jit(solution)/shard_map/ppermute | solution.py:643
  495.9 29.9 %collective-permute-start.46 = (bf16[64,768]{1,0:T(8,128)(2,1)S(1)}, bf16[64,768]{1,0:T(8,128)(2,1)S(1)}, u32[]{:S(2)}, u32[]{:S(2)}) collective-permute-start(bf16[64,768]{1,0:T(8,128)(2,1)S(1)} %copy-done.214), channel_id=1, source_target_pairs={{0,3},{1,2},{2,1},{3,0},{4,7},{5,6},{6,5},{7,4},{8,11},{9,10},{10,... | collective-permute-start | bytes 294920 | tf_op jit(solution)/shard_map/ppermute | solution.py:643
  615.0 36.3 %collective-permute-start.51 = (bf16[64,768]{1,0:T(8,128)(2,1)}, bf16[64,768]{1,0:T(8,128)(2,1)}, u32[]{:S(2)}, u32[]{:S(2)}) collective-permute-start(bf16[64,768]{1,0:T(8,128)(2,1)} %get-tuple-element.795), channel_id=1, source_target_pairs={{0,1},{1,0},{2,3},{3,2},{4,5},{5,4},{6,7},{7,6},{8,9},{9,8},{10,11... | collective-permute-start | bytes 294920 | tf_op jit(solution)/shard_map/ppermute | solution.py:643
  616.8 34.5 %collective-permute-start.52 = (bf16[64,768]{1,0:T(8,128)(2,1)}, bf16[64,768]{1,0:T(8,128)(2,1)}, u32[]{:S(2)}, u32[]{:S(2)}) collective-permute-start(bf16[64,768]{1,0:T(8,128)(2,1)} %get-tuple-element.796), channel_id=1, source_target_pairs={{0,2},{1,3},{2,0},{3,1},{4,6},{5,7},{6,4},{7,5},{8,10},{9,11},{10,... | collective-permute-start | bytes 294920 | tf_op jit(solution)/shard_map/ppermute | solution.py:643
  617.9 33.4 %collective-permute-start.53 = (bf16[64,768]{1,0:T(8,128)(2,1)}, bf16[64,768]{1,0:T(8,128)(2,1)}, u32[]{:S(2)}, u32[]{:S(2)}) collective-permute-start(bf16[64,768]{1,0:T(8,128)(2,1)} %get-tuple-element.797), channel_id=1, source_target_pairs={{0,3},{1,2},{2,1},{3,0},{4,7},{5,6},{6,5},{7,4},{8,11},{9,10},{10,... | collective-permute-start | bytes 294920 | tf_op jit(solution)/shard_map/ppermute | solution.py:643
  651.3 47.1 %collective-permute-start.57 = (bf16[1024,1024]{1,0:T(8,128)(2,1)}, bf16[1024,1024]{1,0:T(8,128)(2,1)}, u32[]{:S(2)}, u32[]{:S(2)}) collective-permute-start(bf16[1024,1024]{1,0:T(8,128)(2,1)} %convolution_convert_fusion.4), channel_id=1, source_target_pairs={{0,8},{8,0},{1,9},{9,1},{2,10},{10,2},{3,11},{11,3},{4,12},{12,4},... | collective-permute-start | bytes 6291464 | tf_op jit(solution)/shard_map/ppermute | solution.py:839
  651.4 47.0 %collective-permute-start.58 = (bf16[1024,1024]{1,0:T(8,128)(2,1)}, bf16[1024,1024]{1,0:T(8,128)(2,1)S(1)}, u32[]{:S(2)}, u32[]{:S(2)}) collective-permute-start(bf16[1024,1024]{1,0:T(8,128)(2,1)} %convolution_convert_fusion.3), channel_id=1, source_target_pairs={{0,8},{8,0},{1,9},{9,1},{2,10},{10,2},{3,11},{11,3},{4,12},{12,4},... | collective-permute-start | bytes 6291464 | tf_op jit(solution)/shard_map/ppermute | solution.py:839
  707.1 84.7 %collective-permute-start.65 = (bf16[512,4096]{1,0:T(8,128)(2,1)}, bf16[512,4096]{1,0:T(8,128)(2,1)}, u32[]{:S(2)}, u32[]{:S(2)}) collective-permute-start(bf16[512,4096]{1,0:T(8,128)(2,1)} %convolution_convert_fusion), channel_id=1, source_target_pairs={{0,8},{8,0},{1,9},{9,1},{2,10},{10,2},{3,11},{11,3},{4,12},{12,4},... | collective-permute-start | bytes 12582920 | tf_op jit(solution)/shard_map/ppermute | solution.py:839
  713.4 76.9 %collective-permute-start.66 = (bf16[1024,512]{1,0:T(8,128)(2,1)}, bf16[1024,512]{1,0:T(8,128)(2,1)}, u32[]{:S(2)}, u32[]{:S(2)}) collective-permute-start(bf16[1024,512]{1,0:T(8,128)(2,1)} %get-tuple-element.873), channel_id=1, source_target_pairs={{0,16},{16,0},{1,17},{17,1},{2,18},{18,2},{3,19},{19,3},{4,20},{20... | collective-permute-start | bytes 3145736 | tf_op jit(solution)/shard_map/ppermute | solution.py:839
  714.9 76.9 %collective-permute-start.67 = (bf16[512,1024]{1,0:T(8,128)(2,1)}, bf16[512,1024]{1,0:T(8,128)(2,1)}, u32[]{:S(2)}, u32[]{:S(2)}) collective-permute-start(bf16[512,1024]{1,0:T(8,128)(2,1)} %convolution_convert_fusion.7), channel_id=1, source_target_pairs={{0,8},{8,0},{1,9},{9,1},{2,10},{10,2},{3,11},{11,3},{4,12},{12,4},... | collective-permute-start | bytes 3145736 | tf_op jit(solution)/shard_map/ppermute | solution.py:839
  714.9 46.5 %collective-permute-start.59 = (bf16[1024,512]{1,0:T(8,128)(2,1)}, bf16[1024,512]{1,0:T(8,128)(2,1)}, u32[]{:S(2)}, u32[]{:S(2)}) collective-permute-start(bf16[1024,512]{1,0:T(8,128)(2,1)} %get-tuple-element.835), channel_id=1, source_target_pairs={{0,16},{16,0},{1,17},{17,1},{2,18},{18,2},{3,19},{19,3},{4,20},{20... | collective-permute-start | bytes 3145736 | tf_op jit(solution)/shard_map/ppermute | solution.py:839
  741.5 46.7 %collective-permute-start.64 = (bf16[512,320]{0,1:T(8,128)(2,1)}, bf16[512,320]{0,1:T(8,128)(2,1)S(1)}, u32[]{:S(2)}, u32[]{:S(2)}) collective-permute-start(bf16[512,320]{0,1:T(8,128)(2,1)} %convolution_convert_fusion.14), channel_id=1, source_target_pairs={{0,8},{8,0},{1,9},{9,1},{2,10},{10,2},{3,11},{11,3},{4,12},{12,4},... | collective-permute-start | bytes 983048 | tf_op jit(solution)/shard_map/ppermute | solution.py:839
  810.8 30.2 %collective-permute-start.85 = (bf16[192,768]{1,0:T(8,128)(2,1)S(1)}, bf16[192,768]{1,0:T(8,128)(2,1)S(1)}, u32[]{:S(2)}, u32[]{:S(2)}) collective-permute-start(bf16[192,768]{1,0:T(8,128)(2,1)S(1)} %copy-done.199), channel_id=1, source_target_pairs={{0,3},{1,2},{2,1},{3,0},{4,7},{5,6},{6,5},{7,4},{8,11},{9,10},{10,... | collective-permute-start | bytes 884744 | tf_op jit(solution)/shard_map/ppermute | solution.py:643
  811.8 31.2 %collective-permute-start.79 = (bf16[192,768]{1,0:T(8,128)(2,1)S(1)}, bf16[192,768]{1,0:T(8,128)(2,1)S(1)}, u32[]{:S(2)}, u32[]{:S(2)}) collective-permute-start(bf16[192,768]{1,0:T(8,128)(2,1)S(1)} %copy-done.203), channel_id=1, source_target_pairs={{0,1},{1,0},{2,3},{3,2},{4,5},{5,4},{6,7},{7,6},{8,9},{9,8},{10,11... | collective-permute-start | bytes 884744 | tf_op jit(solution)/shard_map/ppermute | solution.py:643
  812.5 31.6 %collective-permute-start.83 = (bf16[192,768]{1,0:T(8,128)(2,1)S(1)}, bf16[192,768]{1,0:T(8,128)(2,1)S(1)}, u32[]{:S(2)}, u32[]{:S(2)}) collective-permute-start(bf16[192,768]{1,0:T(8,128)(2,1)S(1)} %copy-done.202), channel_id=1, source_target_pairs={{0,2},{1,3},{2,0},{3,1},{4,6},{5,7},{6,4},{7,5},{8,10},{9,11},{10,... | collective-permute-start | bytes 884744 | tf_op jit(solution)/shard_map/ppermute | solution.py:643
  814.5 30.1 %collective-permute-start.87 = (bf16[192,768]{1,0:T(8,128)(2,1)S(1)}, bf16[192,768]{1,0:T(8,128)(2,1)S(1)}, u32[]{:S(2)}, u32[]{:S(2)}) collective-permute-start(bf16[192,768]{1,0:T(8,128)(2,1)S(1)} %copy-done.201), channel_id=1, source_target_pairs={{0,3},{1,2},{2,1},{3,0},{4,7},{5,6},{6,5},{7,4},{8,11},{9,10},{10,... | collective-permute-start | bytes 884744 | tf_op jit(solution)/shard_map/ppermute | solution.py:643
  815.6 31.0 %collective-permute-start.78 = (bf16[192,768]{1,0:T(8,128)(2,1)S(1)}, bf16[192,768]{1,0:T(8,128)(2,1)S(1)}, u32[]{:S(2)}, u32[]{:S(2)}) collective-permute-start(bf16[192,768]{1,0:T(8,128)(2,1)S(1)} %copy-done.204), channel_id=1, source_target_pairs={{0,1},{1,0},{2,3},{3,2},{4,5},{5,4},{6,7},{7,6},{8,9},{9,8},{10,11... | collective-permute-start | bytes 884744 | tf_op jit(solution)/shard_map/ppermute | solution.py:643
  851.4 63.5 %collective-permute-start.73 = (bf16[256,2048]{1,0:T(8,128)(2,1)}, bf16[256,2048]{1,0:T(8,128)(2,1)}, u32[]{:S(2)}, u32[]{:S(2)}) collective-permute-start(bf16[256,2048]{1,0:T(8,128)(2,1)} %get-tuple-element.908), channel_id=1, source_target_pairs={{0,16},{16,0},{1,17},{17,1},{2,18},{18,2},{3,19},{19,3},{4,20},{20... | collective-permute-start | bytes 3145736 | tf_op jit(solution)/shard_map/ppermute | solution.py:839
  858.7 56.2 %collective-permute-start.74 = (bf16[2,2,128,1024]{3,2,1,0:T(8,128)(2,1)}, bf16[2,2,128,1024]{3,2,1,0:T(8,128)(2,1)}, u32[]{:S(2)}, u32[]{:S(2)}) collective-permute-start(bf16[2,2,128,1024]{3,2,1,0:T(8,128)(2,1)} %get-tuple-element.909), channel_id=1, source_target_pairs={{0,1},{1,0},{2,3},{3,2},{4,5},{5,4},{6,7},{7,6},{8,9},{9,8},{10,11... | collective-permute-start | bytes 3145736 | tf_op jit(solution)/shard_map/ppermute | solution.py:839
  924.1 64.6 %collective-permute-start.95 = (bf16[512,3072]{1,0:T(8,128)(2,1)}, bf16[512,3072]{1,0:T(8,128)(2,1)}, u32[]{:S(2)}, u32[]{:S(2)}) collective-permute-start(bf16[512,3072]{1,0:T(8,128)(2,1)} %convolution_convert_fusion.1), channel_id=1, source_target_pairs={{0,8},{8,0},{1,9},{9,1},{2,10},{10,2},{3,11},{11,3},{4,12},{12,4},... | collective-permute-start | bytes 9437192 | tf_op jit(solution)/shard_map/ppermute | solution.py:839
  951.7 37.0 %collective-permute-start.93 = (bf16[256,2048]{1,0:T(8,128)(2,1)}, bf16[256,2048]{1,0:T(8,128)(2,1)S(1)}, u32[]{:S(2)}, u32[]{:S(2)}) collective-permute-start(bf16[256,2048]{1,0:T(8,128)(2,1)} %get-tuple-element.950), channel_id=1, source_target_pairs={{0,16},{16,0},{1,17},{17,1},{2,18},{18,2},{3,19},{19,3},{4,20},{20... | collective-permute-start | bytes 3145736 | tf_op jit(solution)/shard_map/ppermute | solution.py:839
  953.2 35.4 %collective-permute-start.96 = (bf16[512,1024]{1,0:T(8,128)(2,1)}, bf16[512,1024]{1,0:T(8,128)(2,1)S(1)}, u32[]{:S(2)}, u32[]{:S(2)}) collective-permute-start(bf16[512,1024]{1,0:T(8,128)(2,1)} %convolution_convert_fusion.6), channel_id=1, source_target_pairs={{0,8},{8,0},{1,9},{9,1},{2,10},{10,2},{3,11},{11,3},{4,12},{12,4},... | collective-permute-start | bytes 3145736 | tf_op jit(solution)/shard_map/ppermute | solution.py:839
  953.3 35.4 %collective-permute-start.94 = (bf16[2,128,1024]{2,1,0:T(8,128)(2,1)}, bf16[2,128,1024]{2,1,0:T(8,128)(2,1)S(1)}, u32[]{:S(2)}, u32[]{:S(2)}) collective-permute-start(bf16[2,128,1024]{2,1,0:T(8,128)(2,1)} %get-tuple-element.951), channel_id=1, source_target_pairs={{0,2},{2,0},{1,3},{3,1},{4,6},{6,4},{5,7},{7,5},{8,10},{10,8},{9,1... | collective-permute-start | bytes 1572872 | tf_op jit(solution)/shard_map/ppermute | solution.py:839
  953.3 35.4 %collective-permute-start.97 = (bf16[2,2,32,1024]{3,2,1,0:T(8,128)(2,1)}, bf16[2,2,32,1024]{3,2,1,0:T(8,128)(2,1)}, u32[]{:S(2)}, u32[]{:S(2)}) collective-permute-start(bf16[2,2,32,1024]{3,2,1,0:T(8,128)(2,1)} %get-tuple-element.954), channel_id=1, source_target_pairs={{0,1},{1,0},{2,3},{3,2},{4,5},{5,4},{6,7},{7,6},{8,9},{9,8},{10,11... | collective-permute-start | bytes 786440 | tf_op jit(solution)/shard_map/ppermute | solution.py:839
  1005.3 48.4 %collective-permute-start.112 = (bf16[2,2,32,4096]{3,2,1,0:T(8,128)(2,1)}, bf16[2,2,32,4096]{3,2,1,0:T(8,128)(2,1)}, u32[]{:S(2)}, u32[]{:S(2)}) collective-permute-start(bf16[2,2,32,4096]{3,2,1,0:T(8,128)(2,1)} %get-tuple-element.1036), channel_id=1, source_target_pairs={{0,1},{1,0},{2,3},{3,2},{4,5},{5,4},{6,7},{7,6},{8,9},{9,8},{10,11... | collective-permute-start | bytes 3145736 | tf_op jit(solution)/shard_map/ppermute | solution.py:839
  1006.1 47.5 %collective-permute-start.114 = (bf16[256,1536]{1,0:T(8,128)(2,1)}, bf16[256,1536]{1,0:T(8,128)(2,1)}, u32[]{:S(2)}, u32[]{:S(2)}) collective-permute-start(bf16[256,1536]{1,0:T(8,128)(2,1)} %get-tuple-element.1038), channel_id=1, source_target_pairs={{0,16},{16,0},{1,17},{17,1},{2,18},{18,2},{3,19},{19,3},{4,20},{20... | collective-permute-start | bytes 2359304 | tf_op jit(solution)/shard_map/ppermute | solution.py:839
  1006.7 47.0 %collective-permute-start.115 = (bf16[256,1024]{1,0:T(8,128)(2,1)}, bf16[256,1024]{1,0:T(8,128)(2,1)}, u32[]{:S(2)}, u32[]{:S(2)}) collective-permute-start(bf16[256,1024]{1,0:T(8,128)(2,1)} %slice.346), channel_id=1, source_target_pairs={{0,16},{16,0},{1,17},{17,1},{2,18},{18,2},{3,19},{19,3},{4,20},{20... | collective-permute-start | bytes 1572872 | tf_op jit(solution)/shard_map/ppermute | solution.py:839
  1008.2 45.5 %collective-permute-start.113 = (bf16[128,1024]{1,0:T(8,128)(2,1)}, bf16[128,1024]{1,0:T(8,128)(2,1)}, u32[]{:S(2)}, u32[]{:S(2)}) collective-permute-start(bf16[128,1024]{1,0:T(8,128)(2,1)} %get-tuple-element.1037), channel_id=1, source_target_pairs={{0,4},{4,0},{1,5},{5,1},{2,6},{6,2},{3,7},{7,3},{8,12},{12,8},{9,1... | collective-permute-start | bytes 786440 | tf_op jit(solution)/shard_map/ppermute | solution.py:839
  1010.9 35.8 %collective-permute-start.111 = (bf16[2,32,320]{2,1,0:T(8,128)(2,1)S(1)}, bf16[2,32,320]{2,1,0:T(8,128)(2,1)S(1)}, u32[]{:S(2)}, u32[]{:S(2)}) collective-permute-start(bf16[2,32,320]{2,1,0:T(8,128)(2,1)S(1)} %get-tuple-element.1035), channel_id=1, source_target_pairs={{0,2},{2,0},{1,3},{3,1},{4,6},{6,4},{5,7},{7,5},{8,10},{10,8},{9,1... | collective-permute-start | bytes 122888 | tf_op jit(solution)/shard_map/ppermute | solution.py:839
  1051.7 40.6 %collective-permute-start.100 = (bf16[64,2816]{1,0:T(8,128)(2,1)}, bf16[64,2816]{1,0:T(8,128)(2,1)}, u32[]{:S(2)}, u32[]{:S(2)}) collective-permute-start(bf16[64,2816]{1,0:T(8,128)(2,1)} %get-tuple-element.971), channel_id=1, source_target_pairs={{0,2},{1,3},{2,0},{3,1},{4,6},{5,7},{6,4},{7,5},{8,10},{9,11},{10,... | collective-permute-start | bytes 1081352 | tf_op jit(solution)/shard_map/ppermute | solution.py:643
  1056.6 40.6 %collective-permute-start.119 = (bf16[256,1536]{1,0:T(8,128)(2,1)}, bf16[256,1536]{1,0:T(8,128)(2,1)}, u32[]{:S(2)}, u32[]{:S(2)}) collective-permute-start(bf16[256,1536]{1,0:T(8,128)(2,1)} %get-tuple-element.1046), channel_id=1, source_target_pairs={{0,16},{16,0},{1,17},{17,1},{2,18},{18,2},{3,19},{19,3},{4,20},{20... | collective-permute-start | bytes 2359304 | tf_op jit(solution)/shard_map/ppermute | solution.py:839
  1057.1 40.0 %collective-permute-start.118 = (bf16[2,32,4096]{2,1,0:T(8,128)(2,1)S(1)}, bf16[2,32,4096]{2,1,0:T(8,128)(2,1)S(1)}, u32[]{:S(2)}, u32[]{:S(2)}) collective-permute-start(bf16[2,32,4096]{2,1,0:T(8,128)(2,1)S(1)} %get-tuple-element.1045), channel_id=1, source_target_pairs={{0,2},{2,0},{1,3},{3,1},{4,6},{6,4},{5,7},{7,5},{8,10},{10,8},{9,1... | collective-permute-start | bytes 1572872 | tf_op jit(solution)/shard_map/ppermute | solution.py:839
  1057.1 38.6 %collective-permute-start.120 = (bf16[32,1024]{1,0:T(8,128)(2,1)S(1)}, bf16[32,1024]{1,0:T(8,128)(2,1)S(1)}, u32[]{:S(2)}, u32[]{:S(2)}) collective-permute-start(bf16[32,1024]{1,0:T(8,128)(2,1)S(1)} %get-tuple-element.1047), channel_id=1, source_target_pairs={{0,4},{4,0},{1,5},{5,1},{2,6},{6,2},{3,7},{7,3},{8,12},{12,8},{9,1... | collective-permute-start | bytes 196616 | tf_op jit(solution)/shard_map/ppermute | solution.py:839
  1059.2 35.8 %collective-permute-start.117 = (bf16[32,320]{1,0:T(8,128)(2,1)}, bf16[32,320]{1,0:T(8,128)(2,1)S(1)}, u32[]{:S(2)}, u32[]{:S(2)}) collective-permute-start(bf16[32,320]{1,0:T(8,128)(2,1)} %get-tuple-element.1044), channel_id=1, source_target_pairs={{0,4},{4,0},{1,5},{5,1},{2,6},{6,2},{3,7},{7,3},{8,12},{12,8},{9,1... | collective-permute-start | bytes 61448 | tf_op jit(solution)/shard_map/ppermute | solution.py:839
  1095.7 29.0 %collective-permute-start.105 = (bf16[64,2816]{1,0:T(8,128)(2,1)}, bf16[64,2816]{1,0:T(8,128)(2,1)S(1)}, u32[]{:S(2)}, u32[]{:S(2)}) collective-permute-start(bf16[64,2816]{1,0:T(8,128)(2,1)} %get-tuple-element.1016), channel_id=1, source_target_pairs={{0,1},{1,0},{2,3},{3,2},{4,5},{5,4},{6,7},{7,6},{8,9},{9,8},{10,11... | collective-permute-start | bytes 1081352 | tf_op jit(solution)/shard_map/ppermute | solution.py:643
  1097.1 29.1 %collective-permute-start.106 = (bf16[64,2816]{1,0:T(8,128)(2,1)}, bf16[64,2816]{1,0:T(8,128)(2,1)S(1)}, u32[]{:S(2)}, u32[]{:S(2)}) collective-permute-start(bf16[64,2816]{1,0:T(8,128)(2,1)} %get-tuple-element.1017), channel_id=1, source_target_pairs={{0,2},{1,3},{2,0},{3,1},{4,6},{5,7},{6,4},{7,5},{8,10},{9,11},{10,... | collective-permute-start | bytes 1081352 | tf_op jit(solution)/shard_map/ppermute | solution.py:643
  1097.1 30.3 %collective-permute-start.107 = (bf16[64,2816]{1,0:T(8,128)(2,1)}, bf16[64,2816]{1,0:T(8,128)(2,1)}, u32[]{:S(2)}, u32[]{:S(2)}) collective-permute-start(bf16[64,2816]{1,0:T(8,128)(2,1)} %get-tuple-element.1018), channel_id=1, source_target_pairs={{0,3},{1,2},{2,1},{3,0},{4,7},{5,6},{6,5},{7,4},{8,11},{9,10},{10,... | collective-permute-start | bytes 1081352 | tf_op jit(solution)/shard_map/ppermute | solution.py:643
  1104.9 37.5 %collective-permute-start.121 = (bf16[64,768]{1,0:T(8,128)(2,1)}, bf16[64,768]{1,0:T(8,128)(2,1)}, u32[]{:S(2)}, u32[]{:S(2)}) collective-permute-start(bf16[64,768]{1,0:T(8,128)(2,1)} %get-tuple-element.1083), channel_id=1, source_target_pairs={{0,1},{1,0},{2,3},{3,2},{4,5},{5,4},{6,7},{7,6},{8,9},{9,8},{10,11... | collective-permute-start | bytes 294920 | tf_op jit(solution)/shard_map/ppermute | solution.py:643
  1126.1 84.3 %collective-permute-start.131 = (bf16[64,2816]{1,0:T(8,128)(2,1)}, bf16[64,2816]{1,0:T(8,128)(2,1)}, u32[]{:S(2)}, u32[]{:S(2)}) collective-permute-start(bf16[64,2816]{1,0:T(8,128)(2,1)} %get-tuple-element.1066), channel_id=1, source_target_pairs={{0,1},{1,0},{2,3},{3,2},{4,5},{5,4},{6,7},{7,6},{8,9},{9,8},{10,11... | collective-permute-start | bytes 1081352 | tf_op jit(solution)/shard_map/ppermute | solution.py:643
  1142.4 41.9 %collective-permute-start.125 = (bf16[512,1024]{1,0:T(8,128)(2,1)}, bf16[512,1024]{1,0:T(8,128)(2,1)}, u32[]{:S(2)}, u32[]{:S(2)}) collective-permute-start(bf16[512,1024]{1,0:T(8,128)(2,1)} %convolution_convert_fusion.9), channel_id=1, source_target_pairs={{0,8},{8,0},{1,9},{9,1},{2,10},{10,2},{3,11},{11,3},{4,12},{12,4},... | collective-permute-start | bytes 3145736 | tf_op jit(solution)/shard_map/ppermute | solution.py:839
  1142.5 41.8 %collective-permute-start.126 = (bf16[2,2,32,4096]{3,2,1,0:T(8,128)(2,1)S(1)}, bf16[2,2,32,4096]{3,2,1,0:T(8,128)(2,1)}, u32[]{:S(2)}, u32[]{:S(2)}) collective-permute-start(bf16[2,2,32,4096]{3,2,1,0:T(8,128)(2,1)S(1)} %copy-done.74), channel_id=1, source_target_pairs={{0,1},{1,0},{2,3},{3,2},{4,5},{5,4},{6,7},{7,6},{8,9},{9,8},{10,11... | collective-permute-start | bytes 3145736 | tf_op jit(solution)/shard_map/ppermute | solution.py:839
  1143.3 41.0 %collective-permute-start.127 = (bf16[512,512]{1,0:T(8,128)(2,1)}, bf16[512,512]{1,0:T(8,128)(2,1)}, u32[]{:S(2)}, u32[]{:S(2)}) collective-permute-start(bf16[512,512]{1,0:T(8,128)(2,1)} %convolution_convert_fusion.12), channel_id=1, source_target_pairs={{0,8},{8,0},{1,9},{9,1},{2,10},{10,2},{3,11},{11,3},{4,12},{12,4},... | collective-permute-start | bytes 1572872 | tf_op jit(solution)/shard_map/ppermute | solution.py:839
  1143.5 40.1 %collective-permute-start.124 = (bf16[32,4096]{1,0:T(8,128)(2,1)S(1)}, bf16[32,4096]{1,0:T(8,128)(2,1)}, u32[]{:S(2)}, u32[]{:S(2)}) collective-permute-start(bf16[32,4096]{1,0:T(8,128)(2,1)S(1)} %get-tuple-element.1092), channel_id=1, source_target_pairs={{0,4},{4,0},{1,5},{5,1},{2,6},{6,2},{3,7},{7,3},{8,12},{12,8},{9,1... | collective-permute-start | bytes 786440 | tf_op jit(solution)/shard_map/ppermute | solution.py:839
  1183.6 34.2 %collective-permute-start.132 = (bf16[64,2816]{1,0:T(8,128)(2,1)}, bf16[64,2816]{1,0:T(8,128)(2,1)S(1)}, u32[]{:S(2)}, u32[]{:S(2)}) collective-permute-start(bf16[64,2816]{1,0:T(8,128)(2,1)} %get-tuple-element.1067), channel_id=1, source_target_pairs={{0,2},{1,3},{2,0},{3,1},{4,6},{5,7},{6,4},{7,5},{8,10},{9,11},{10,... | collective-permute-start | bytes 1081352 | tf_op jit(solution)/shard_map/ppermute | solution.py:643
  1282.9 36.3 %collective-permute-start.138 = (bf16[512,1024]{1,0:T(8,128)(2,1)}, bf16[512,1024]{1,0:T(8,128)(2,1)}, u32[]{:S(2)}, u32[]{:S(2)}) collective-permute-start(bf16[512,1024]{1,0:T(8,128)(2,1)} %convolution_convert_fusion.8), channel_id=1, source_target_pairs={{0,8},{8,0},{1,9},{9,1},{2,10},{10,2},{3,11},{11,3},{4,12},{12,4},... | collective-permute-start | bytes 3145736 | tf_op jit(solution)/shard_map/ppermute | solution.py:839
  1282.9 36.3 %collective-permute-start.137 = (bf16[384,1024]{1,0:T(8,128)(2,1)}, bf16[384,1024]{1,0:T(8,128)(2,1)}, u32[]{:S(2)}, u32[]{:S(2)}) collective-permute-start(bf16[384,1024]{1,0:T(8,128)(2,1)} %convolution_convert_fusion.10), channel_id=1, source_target_pairs={{0,8},{8,0},{1,9},{9,1},{2,10},{10,2},{3,11},{11,3},{4,12},{12,4},... | collective-permute-start | bytes 2359304 | tf_op jit(solution)/shard_map/ppermute | solution.py:839
  1283.4 35.8 %collective-permute-start.140 = (bf16[512,512]{1,0:T(8,128)(2,1)}, bf16[512,512]{1,0:T(8,128)(2,1)}, u32[]{:S(2)}, u32[]{:S(2)}) collective-permute-start(bf16[512,512]{1,0:T(8,128)(2,1)} %convolution_convert_fusion.11), channel_id=1, source_target_pairs={{0,8},{8,0},{1,9},{9,1},{2,10},{10,2},{3,11},{11,3},{4,12},{12,4},... | collective-permute-start | bytes 1572872 | tf_op jit(solution)/shard_map/ppermute | solution.py:839
  1283.4 35.8 %collective-permute-start.141 = (bf16[256,768]{1,0:T(8,128)(2,1)}, bf16[256,768]{1,0:T(8,128)(2,1)}, u32[]{:S(2)}, u32[]{:S(2)}) collective-permute-start(bf16[256,768]{1,0:T(8,128)(2,1)} %get-tuple-element.1146), channel_id=1, source_target_pairs={{0,4},{4,0},{1,5},{5,1},{2,6},{6,2},{3,7},{7,3},{8,12},{12,8},{9,1... | collective-permute-start | bytes 1179656 | tf_op jit(solution)/shard_map/ppermute | solution.py:839
  1326.0 30.6 %collective-permute-start.145 = (bf16[256,1024]{1,0:T(8,128)(2,1)}, bf16[256,1024]{1,0:T(8,128)(2,1)S(1)}, u32[]{:S(2)}, u32[]{:S(2)}) collective-permute-start(bf16[256,1024]{1,0:T(8,128)(2,1)} %slice.360), channel_id=1, source_target_pairs={{0,16},{16,0},{1,17},{17,1},{2,18},{18,2},{3,19},{19,3},{4,20},{20... | collective-permute-start | bytes 1572872 | tf_op jit(solution)/shard_map/ppermute | solution.py:839
  1365.5 34.9 %collective-permute-start.152 = (bf16[192,1024]{1,0:T(8,128)(2,1)}, bf16[192,1024]{1,0:T(8,128)(2,1)}, u32[]{:S(2)}, u32[]{:S(2)}) collective-permute-start(bf16[192,1024]{1,0:T(8,128)(2,1)} %get-tuple-element.1199), channel_id=1, source_target_pairs={{0,4},{4,0},{1,5},{5,1},{2,6},{6,2},{3,7},{7,3},{8,12},{12,8},{9,1... | collective-permute-start | bytes 1179656 | tf_op jit(solution)/shard_map/ppermute | solution.py:839
  (345 other events, 4807.7 us)
Sparse Core Ops, SparseCore 0:
  17.4 155.5 all-gather.5
  175.9 132.4 all-gather.7
  311.3 91.6 all-gather.9
  406.3 117.5 all-gather.11
Sparse Core Ops, SparseCore 1:
  118.1 132.6 reduce-scatter.1
  638.7 73.2 all-gather.13

commit v3 on v2

--- a/solution.py
+++ b/solution.py
@@ -747,16 +747,13 @@
         dims = ((1 - axis,), (right_axis,))
 
         def block(y, c):
-            return lax.dynamic_slice_in_dim(left, (2 * y + c) * quarter, quarter, axis)
-
-        def blocks_of(c):
-            parts = [block(1 - over, c), block(over, c)]
-            return parts if quarter > 512 else [jnp.concatenate(parts, axis=axis)]
-
-        others = [lower(dot(x, right, dims)) for x in blocks_of(1 - side)]
+            part = lax.dynamic_slice_in_dim(left, (2 * y + c) * quarter, quarter, axis)
+            return dot(part, right, dims)
+
+        others = [lower(block(y, 1 - side)) for y in (1 - over, over)]
         others = yield (), [(x, core) for x in others]
-        sums = [lower(dot(x, right, dims) + widen(g)) for x, g in zip(blocks_of(side), others)]
-        away, kept = sums if quarter > 512 else (sums[0][:quarter], sums[0][quarter:])
+        away = lower(block(1 - over, side) + widen(others[0]))
+        kept = lower(block(over, side) + widen(others[1]))
         width = away.shape[1] // pieces
         got = []
         for i in range(pieces):
@@ -780,31 +777,6 @@
     def full_job(*args):
         part = yield from grad_job(*args)
         return (yield from chain_job([part]))[0]
-
-    def together(runs):
-        results, got = [None] * len(runs), [None] * len(runs)
-        left = list(range(len(runs)))
-        while True:
-            kept, sent, sizes = [], [], []
-            for i in list(left):
-                try:
-                    stand, moves = next(runs[i]) if got[i] is None else runs[i].send(got[i])
-                except StopIteration as end:
-                    results[i] = end.value
-                    left.remove(i)
-                    continue
-                kept.append(stand)
-                sent += moves
-                sizes.append(len(moves))
-            if not left:
-                return results
-            arrived = yield kept, sent
-            for i, size in zip(left, sizes):
-                got[i], arrived = arrived[:size], arrived[size:]
-
-    def side_job(*runs):
-        parts = yield from together(runs)
-        return (yield from chain_job([jnp.concatenate(parts, axis=1)]))[0]
 
     def swap_job(arrays, pieces):
         done = []
@@ -868,8 +840,8 @@
     for j in range(heads):
         if j == min(2, heads - 1):
             start("hidden", full_job(normed_c, 1, hidden_grad, 0, 2))
-            start("self", full_job(self_mix, 0, self_low, 0))
-            start("deconv", full_job(result_low, 1, plane_low, 1))
+            start("self", full_job(self_mix, 0, self_low, 0, 1))
+            start("deconv", full_job(result_low, 1, plane_low, 1, 1))
         if j == min(1, heads - 1):
             start("tokens_out", swap_job([result_low], 4))
         raw, gone = turn(
@@ -887,10 +859,8 @@
     cross_low = lower(cross_grad)
     cross_mix_grad = lower(dot(cross_w, cross_low, NT)).reshape(group, heads, HD, count)
     cross_dout = exchange_all(split(cross_mix_grad, me))
-    start(
-        "project",
-        side_job(grad_job(normed_b, 1, project_grad, 1, 2), grad_job(cross_mix, 0, cross_low, 0)),
-    )
+    start("project", full_job(normed_b, 1, project_grad, 1, 2))
+    start("cross", full_job(cross_mix, 0, cross_low, 0, 1))
     cut = heads // 2
     cross_back, parts, found = [], [], []
 
@@ -1006,10 +976,10 @@
         image_sum,
         merge_columns(query_sums, HD),
         merge_columns(keyval_sums, 2 * HD),
-        sums_of["project"][:, 3 * D :],
+        sums_of["cross"],
         vector_sums[:, 2],
         vector_sums[:, 3],
-        sums_of["project"][:, : 3 * D],
+        sums_of["project"],
         sums_of["self"],
         vector_sums[:, 4],
         vector_sums[:, 5],

time: 1450 us -> 1430 us (0.986)
  waiting for transfers between devices: 319 us -> 287 us
  local copies, waits for them, and re-layouts: 123 us -> 104 us
  matrix products: 198 us -> 214 us
    ppermute x58 -> x71, waiting for transfers between devices: 76.3 us -> 58.5 us  [turn(): lax.ppermute(x, axis, SWAP)]
    dot_general x42 -> x62, matrix products: 198 us -> 214 us  [dot(): lax.dot_general(left, right, (dims, ((), ())), preferred_element_type=f32)]
    ppermute x58 -> x71, starting transfers between devices: 48.1 us -> 61.9 us  [turn(): lax.ppermute(x, axis, SWAP)]
    convert_element_type x42 -> x53, other arithmetic: 48.9 us -> 56.7 us  [lower(): return value.astype(bf16)]
    unnamed x500 -> x546, local copies, waits for them, and re-layouts: 32.9 us -> 34.4 us
  transfers between devices with their start and end apart: 163 -> 176, of which waited for: 50 -> 44; matrix products, arithmetic and copies ran while one was open for 18% -> 18% of each run, Pallas kernels for 36% -> 36%
where the time goes in v3:
time: 1430 us; the launch traced here: 1420 us
  Pallas kernels  520 us (36%)
  waiting for transfers between devices  287 us (20%)
  matrix products  214 us (15%)
  starting transfers between devices  179 us (13%)
  local copies, waits for them, and re-layouts  104 us (7%)
  other arithmetic  91.8 us (6%)
  between operations  18.6 us (1%)
    pallas_call x8, Pallas kernels, attend_backward(): pl.pallas_call(functools.partial(backward_kernel, chunks=chunks, block=bl...  229 us
    dot_general x62, matrix products, dot(): lax.dot_general(left, right, (dims, ((), ())), preferred_element_type=f32)  214 us
    ppermute x96, waiting for transfers between devices, exchange(): lax.ppermute(chunks[k], group_axes, [(i, i ^ k) for i in range(group)])  177 us
    pallas_call x8, Pallas kernels, attend_forward(): pl.pallas_call(functools.partial(forward_kernel, chunks=chunks, block=blo...  125 us
    ppermute x96, starting transfers between devices, exchange(): lax.ppermute(chunks[k], group_axes, [(i, i ^ k) for i in range(group)])  109 us
    pallas_call x1, Pallas kernels, scatter_points(): pl.pallas_call(functools.partial(scatter_kernel, width=width), grid_spec=...  72 us
    ppermute x71, starting transfers between devices, turn(): lax.ppermute(x, axis, SWAP)  61.9 us
    ppermute x71, waiting for transfers between devices, turn(): lax.ppermute(x, axis, SWAP)  58.5 us
  transfers between devices with their start and end apart: 176, of which 44 were waited for; matrix products, arithmetic and copies ran while one was open for 18% of the time, Pallas kernels for 36%

profile of v3, /device:TPU:0, one launch (start us, length us, event | category | flops | bytes accessed | tf_op | source)
XLA Modules:
  0.0 1415.2 jit_solution(13336890166577540454)
XLA Ops:
  39.8 72.0 %scatter_points.1 = bf16[2,4,320,768]{3,2,1,0:T(8,128)(2,1)} custom-call(s32[2]{0:T(128)} %object_ref.1, s32[2,3,4096]{2,1,0:T(4,128)} %reshape.274.cell_ref, f32[2,6,4096]{2,1,0:T(8,128)} %reshape.275.frac_ref, f32[2,1,128]{2,1,0:T(1,128)} %bitcast.316, bf16[256,2560]{1,0:T(8,128)(2,1)} %grad_ref.1), custom_call_target="tpu_custom_call" | custom-call | flops 51539607552 | bytes 10485760 | tf_op jit(solution)/shard_map/scatter_points/pallas_call | solution.py:554
  119.1 51.6 %all-gather.6.cloned.1.call-done = bf16[1024,3968]{1,0:T(8,128)(2,1)} async-done(((bf16[32,3968]{1,0:T(8,128)(2,1)}), bf16[1024,3968]{1,0:T(8,128)(2,1)}) %all-gather.6.cloned.1.call-update) | async-done | bytes 8126480 | tf_op jit(solution)/shard_map/all_gather | solution.py:639
  184.1 5.4 fusion.51
  189.6 6.3 convolution_convert_fusion.4
  195.9 6.0 split_pair.1
  206.2 14.6 %collective-permute-done.2.refs_1_ = bf16[64,2816]{1,0:T(8,128)(2,1)S(1)} collective-permute-done((bf16[64,2816]{1,0:T(8,128)(2,1)}, bf16[64,2816]{1,0:T(8,128)(2,1)S(1)}, u32[]{:S(2)}, u32[]{:S(2)}) %collective-permute-start.2) | collective-permute-done | bytes 360480 | tf_op jit(solution)/shard_map/ppermute | solution.py:643
  220.8 6.3 collective-permute-done.3.refs_2_
  227.1 21.2 %collective-permute-done.4.refs_3_ = bf16[64,2816]{1,0:T(8,128)(2,1)S(1)} collective-permute-done((bf16[64,2816]{1,0:T(8,128)(2,1)}, bf16[64,2816]{1,0:T(8,128)(2,1)S(1)}, u32[]{:S(2)}, u32[]{:S(2)}) %collective-permute-start.4) | collective-permute-done | bytes 360480 | tf_op jit(solution)/shard_map/ppermute | solution.py:643
  251.8 17.7 %attend_forward.8 = (bf16[64,768]{1,0:T(8,128)(2,1)}, bf16[64,768]{1,0:T(8,128)(2,1)}, bf16[64,768]{1,0:T(8,128)(2,1)}, bf16[64,768]{1,0:T(8,128)(2,1)}, f32[4,1,768]{2,1,0:T(1,128)}) custom-call(bf16[64,2816]{1,0:T(8,128)(2,1)} %get-tuple-element.990.refs_0_, bf16[64,2816]{1,0:T(8,128)(2,1)} %copy-done.185, bf16[64,2816]{1,0:T(8,128)(2,1)} %copy-done.186, ...), custom_call_target="tpu_custom_call" | custom-call | flops 12884901888 | bytes 1048576 | tf_op jit(solution)/shard_map/attend_forward/pallas_call | solution.py:145
  273.8 11.0 collective-permute-done.7.refs_3_
  288.4 17.2 %attend_forward.9 = (bf16[64,768]{1,0:T(8,128)(2,1)}, bf16[64,768]{1,0:T(8,128)(2,1)}, bf16[64,768]{1,0:T(8,128)(2,1)}, bf16[64,768]{1,0:T(8,128)(2,1)}, f32[4,1,768]{2,1,0:T(1,128)}) custom-call(bf16[64,2816]{1,0:T(8,128)(2,1)} %get-tuple-element.1044.refs_0_, bf16[64,2816]{1,0:T(8,128)(2,1)} %copy-done.182, bf16[64,2816]{1,0:T(8,128)(2,1)} %copy-done.183, ...), custom_call_target="tpu_custom_call" | custom-call | flops 12884901888 | bytes 1048576 | tf_op jit(solution)/shard_map/attend_forward/pallas_call | solution.py:145
  305.6 5.5 collective-permute-done.9.refs_2_
  314.7 17.4 %attend_forward.10 = (bf16[64,768]{1,0:T(8,128)(2,1)}, bf16[64,768]{1,0:T(8,128)(2,1)}, bf16[64,768]{1,0:T(8,128)(2,1)}, bf16[64,768]{1,0:T(8,128)(2,1)}, f32[4,1,768]{2,1,0:T(1,128)}) custom-call(bf16[64,2816]{1,0:T(8,128)(2,1)} %get-tuple-element.1086.refs_0_, bf16[64,2816]{1,0:T(8,128)(2,1)} %copy-done.180, bf16[64,2816]{1,0:T(8,128)(2,1)} %copy-done.181, ...), custom_call_target="tpu_custom_call" | custom-call | flops 12884901888 | bytes 1048576 | tf_op jit(solution)/shard_map/attend_forward/pallas_call | solution.py:145
  341.1 17.2 %attend_forward.11 = (bf16[64,768]{1,0:T(8,128)(2,1)}, bf16[64,768]{1,0:T(8,128)(2,1)}, bf16[64,768]{1,0:T(8,128)(2,1)}, bf16[64,768]{1,0:T(8,128)(2,1)}, f32[4,1,768]{2,1,0:T(1,128)}) custom-call(bf16[64,2816]{1,0:T(8,128)(2,1)} %get-tuple-element.1137.refs_0_, bf16[64,2816]{1,0:T(8,128)(2,1)} %copy-done.176, bf16[64,2816]{1,0:T(8,128)(2,1)} %copy-done.177, ...), custom_call_target="tpu_custom_call" | custom-call | flops 12884901888 | bytes 1048576 | tf_op jit(solution)/shard_map/attend_forward/pallas_call | solution.py:145
  380.6 7.1 fusion.8
  387.7 5.4 split.3
  401.7 17.4 %collective-permute-done.27.refs_2_ = bf16[192,768]{1,0:T(8,128)(2,1)S(1)} collective-permute-done((bf16[192,768]{1,0:T(8,128)(2,1)}, bf16[192,768]{1,0:T(8,128)(2,1)S(1)}, u32[]{:S(2)}, u32[]{:S(2)}) %collective-permute-start.27) | collective-permute-done | bytes 294944 | tf_op jit(solution)/shard_map/ppermute | solution.py:643
  419.1 6.2 collective-permute-done.28.refs_3_
  428.8 13.6 attend_forward.12
  443.7 11.7 collective-permute-done.31.refs_3_
  456.0 13.6 attend_forward.13
  472.9 19.1 %collective-permute-done.34.refs_3_ = bf16[192,768]{1,0:T(8,128)(2,1)S(1)} collective-permute-done((bf16[192,768]{1,0:T(8,128)(2,1)S(1)}, bf16[192,768]{1,0:T(8,128)(2,1)S(1)}, u32[]{:S(2)}, u32[]{:S(2)}) %collective-permute-start.34) | collective-permute-done | bytes 294944 | tf_op jit(solution)/shard_map/ppermute | solution.py:643
  495.6 14.2 %attend_forward.14 = (bf16[64,768]{1,0:T(8,128)(2,1)}, bf16[64,768]{1,0:T(8,128)(2,1)}, bf16[64,768]{1,0:T(8,128)(2,1)}, bf16[64,768]{1,0:T(8,128)(2,1)}, f32[4,1,768]{2,1,0:T(1,128)}) custom-call(bf16[192,768]{1,0:T(8,128)(2,1)} %get-tuple-element.905.refs_0_, bf16[192,768]{1,0:T(8,128)(2,1)} %copy-done.198, bf16[192,768]{1,0:T(8,128)(2,1)} %copy-done.199, ...), custom_call_target="tpu_custom_call" | custom-call | flops 9663676416 | bytes 786432 | tf_op jit(solution)/shard_map/attend_forward/pallas_call | solution.py:145
  517.4 13.6 attend_forward.15
  536.7 4.5 fusion.30
  546.0 5.1 fusion.199
  553.3 9.2 fusion.2
  562.5 18.1 %convert_reduce_fusion = (f32[4096]{0:T(1024)}, bf16[768,4096]{1,0:T(8,128)(2,1)S(1)}, bf16[768,4096]{1,0:T(8,128)(2,1)}) fusion(f32[768,4096]{1,0:T(8,128)} %fusion.2, f32[4096]{0:T(1024)S(1)} %add.529, bf16[768,1024]{1,0:T(8,128)(2,1)} %get-tuple-element.1479, bf16[4096,1024]{1,0:T(8,128)(2,1)} %all-gather.12.cloned.1.call-done), kind=kOutput, calls=%fused_computation | convolution fusion | flops 6499069952 | bytes 35160064 | tf_op jit(solution)/shard_map/dot_general | solution.py:44
  580.6 4.5 convolution_convert_fusion
  585.1 11.7 multiply_reduce_fusion
  608.0 4.6 fusion.57
  619.9 5.8 fusion.64
  625.7 4.7 convolution_convert_fusion.5
  645.4 6.9 add_convert_fusion.8
  666.2 25.0 %attend_backward.8 = (bf16[192,768]{1,0:T(8,128)(2,1)}, bf16[192,768]{1,0:T(8,128)(2,1)}, bf16[192,768]{1,0:T(8,128)(2,1)}, bf16[192,768]{1,0:T(8,128)(2,1)}) custom-call(bf16[192,768]{1,0:T(8,128)(2,1)} %get-tuple-element.842.refs_0_, bf16[192,768]{1,0:T(8,128)(2,1)} %copy-done.190, bf16[192,768]{1,0:T(8,128)(2,1)} %copy-done.191, ...), custom_call_target="tpu_custom_call" | custom-call | flops 18874368000 | bytes 1572864 | tf_op jit(solution)/shard_map/attend_backward/pallas_call | solution.py:247
  691.4 4.4 add_convert_fusion.6
  709.4 24.9 %attend_backward.10 = (bf16[192,768]{1,0:T(8,128)(2,1)}, bf16[192,768]{1,0:T(8,128)(2,1)}, bf16[192,768]{1,0:T(8,128)(2,1)}, bf16[192,768]{1,0:T(8,128)(2,1)}) custom-call(bf16[192,768]{1,0:T(8,128)(2,1)} %get-tuple-element.905.refs_0_, bf16[192,768]{1,0:T(8,128)(2,1)} %copy-done.198, bf16[192,768]{1,0:T(8,128)(2,1)} %copy-done.199, ...), custom_call_target="tpu_custom_call" | custom-call | flops 18874368000 | bytes 1572864 | tf_op jit(solution)/shard_map/attend_backward/pallas_call | solution.py:247
  735.0 25.2 %attend_backward.9 = (bf16[192,768]{1,0:T(8,128)(2,1)}, bf16[192,768]{1,0:T(8,128)(2,1)}, bf16[192,768]{1,0:T(8,128)(2,1)}, bf16[192,768]{1,0:T(8,128)(2,1)}) custom-call(bf16[192,768]{1,0:T(8,128)(2,1)} %get-tuple-element.863.refs_0_, bf16[192,768]{1,0:T(8,128)(2,1)} %copy-done.195, bf16[192,768]{1,0:T(8,128)(2,1)} %copy-done.196, ...), custom_call_target="tpu_custom_call" | custom-call | flops 18874368000 | bytes 1572864 | tf_op jit(solution)/shard_map/attend_backward/pallas_call | solution.py:247
  791.6 25.0 %attend_backward.11 = (bf16[192,768]{1,0:T(8,128)(2,1)}, bf16[192,768]{1,0:T(8,128)(2,1)}, bf16[192,768]{1,0:T(8,128)(2,1)}, bf16[192,768]{1,0:T(8,128)(2,1)}) custom-call(bf16[192,768]{1,0:T(8,128)(2,1)} %get-tuple-element.944.refs_0_, bf16[192,768]{1,0:T(8,128)(2,1)} %copy-done.192, bf16[192,768]{1,0:T(8,128)(2,1)} %copy-done.193, ...), custom_call_target="tpu_custom_call" | custom-call | flops 18874368000 | bytes 1572864 | tf_op jit(solution)/shard_map/attend_backward/pallas_call | solution.py:247
  828.4 4.9 collective-permute-done.89.refs_13_
  843.0 5.2 assemble.5
  848.2 10.6 multiply_reduce_fusion.1
  861.4 4.7 fusion.54
  873.5 4.9 convolution_convert_fusion.3
  923.6 32.4 %attend_backward.12 = (bf16[64,2816]{1,0:T(8,128)(2,1)}, bf16[64,2816]{1,0:T(8,128)(2,1)}, bf16[64,2816]{1,0:T(8,128)(2,1)}, bf16[64,2816]{1,0:T(8,128)(2,1)}) custom-call(bf16[64,2816]{1,0:T(8,128)(2,1)} %get-tuple-element.990.refs_0_, bf16[64,2816]{1,0:T(8,128)(2,1)} %copy-done.185, bf16[64,2816]{1,0:T(8,128)(2,1)} %copy-done.186, ...), custom_call_target="tpu_custom_call" | custom-call | flops 25165824000 | bytes 2097152 | tf_op jit(solution)/shard_map/attend_backward/pallas_call | solution.py:247
  959.6 5.7 fusion.12
  988.3 32.2 %attend_backward.13 = (bf16[64,2816]{1,0:T(8,128)(2,1)}, bf16[64,2816]{1,0:T(8,128)(2,1)}, bf16[64,2816]{1,0:T(8,128)(2,1)}, bf16[64,2816]{1,0:T(8,128)(2,1)}) custom-call(bf16[64,2816]{1,0:T(8,128)(2,1)} %get-tuple-element.1044.refs_0_, bf16[64,2816]{1,0:T(8,128)(2,1)} %copy-done.182, bf16[64,2816]{1,0:T(8,128)(2,1)} %copy-done.183, ...), custom_call_target="tpu_custom_call" | custom-call | flops 25165824000 | bytes 2097152 | tf_op jit(solution)/shard_map/attend_backward/pallas_call | solution.py:247
  1034.5 4.8 collective-permute-done.124.refs_2_
  1050.9 32.2 %attend_backward.14 = (bf16[64,2816]{1,0:T(8,128)(2,1)}, bf16[64,2816]{1,0:T(8,128)(2,1)}, bf16[64,2816]{1,0:T(8,128)(2,1)}, bf16[64,2816]{1,0:T(8,128)(2,1)}) custom-call(bf16[64,2816]{1,0:T(8,128)(2,1)} %get-tuple-element.1086.refs_0_, bf16[64,2816]{1,0:T(8,128)(2,1)} %copy-done.180, bf16[64,2816]{1,0:T(8,128)(2,1)} %copy-done.181, ...), custom_call_target="tpu_custom_call" | custom-call | flops 25165824000 | bytes 2097152 | tf_op jit(solution)/shard_map/attend_backward/pallas_call | solution.py:247
  1115.7 32.5 %attend_backward.15 = (bf16[64,2816]{1,0:T(8,128)(2,1)}, bf16[64,2816]{1,0:T(8,128)(2,1)}, bf16[64,2816]{1,0:T(8,128)(2,1)}, bf16[64,2816]{1,0:T(8,128)(2,1)}) custom-call(bf16[64,2816]{1,0:T(8,128)(2,1)} %get-tuple-element.1137.refs_0_, bf16[64,2816]{1,0:T(8,128)(2,1)} %copy-done.176, bf16[64,2816]{1,0:T(8,128)(2,1)} %copy-done.177, ...), custom_call_target="tpu_custom_call" | custom-call | flops 25165824000 | bytes 2097152 | tf_op jit(solution)/shard_map/attend_backward/pallas_call | solution.py:247
  1166.8 14.0 sample_points.4
  1192.5 8.0 collective-permute-done.143.refs_6_
  1200.6 7.5 collective-permute-done.145.refs_5_
  1208.0 5.6 collective-permute-done.146.refs_7_
  1230.1 6.3 fusion.28
  1242.6 8.1 fusion.31
  1265.2 14.3 %sample_points.5 = bf16[128,1280]{1,0:T(8,128)(2,1)} custom-call(s32[1]{0:T(128)} %get-tuple-element.1197.object_ref, s32[1,3,2048]{2,1,0:T(4,128)} %get-tuple-element.1198.cell_ref, f32[1,6,2048]{2,1,0:T(8,128)} %get-tuple-element.1199.frac_ref, f32[1,1,128]{2,1,0:T(1,128)} %get-tuple-element.1200.live_ref, bf16[2,4,320,768]{3,2,1,0:T(8,128)(2,1)} %bitcast.322), custom_call_target="tpu_custom_call" | custom-call | flops 12884901888 | bytes 5242880 | tf_op jit(solution)/shard_map/sample_points/pallas_call | solution.py:479
  1286.8 16.4 %collective-permute-done.154 = bf16[256,768]{1,0:T(8,128)(2,1)S(1)} collective-permute-done((bf16[256,768]{1,0:T(8,128)(2,1)}, bf16[256,768]{1,0:T(8,128)(2,1)S(1)}, u32[]{:S(2)}, u32[]{:S(2)}) %collective-permute-start.154) | collective-permute-done | bytes 393248 | tf_op jit(solution)/shard_map/ppermute | solution.py:811
  1311.6 13.8 sample_points.6
  1325.5 12.0 collective-permute-done.161
  1347.2 14.0 sample_points.7
  1365.0 5.4 collective-permute-done.164
  1380.8 8.8 collective-permute-done.167
  1398.7 4.5 collective-permute-done.169
  (1134 shorter events, 516.7 us)
Async XLA Ops:
  8.1 162.7 %all-gather.6.cloned.1.call-start = ((), (), s32[]{:S(2)}) async-start(), calls=%async_computation.1 | async-start | bytes 8380416 | tf_op jit(solution)/shard_map/all_gather | solution.py:639
  17.3 356.2 %all-gather.8.cloned.1.call-start = ((), (), s32[]{:S(2)}) async-start(), calls=%async_computation.2 | async-start | bytes 10813440 | tf_op jit(solution)/shard_map/all_gather | solution.py:639
  19.2 517.5 %reduce-scatter.2.cloned.1.call-start = ((), (), s32[]{:S(2)}) async-start(), calls=%async_computation.5 | async-start | bytes 4423680 | tf_op jit(solution)/shard_map/reduce_scatter | solution.py:698
  23.5 88.3 %collective-permute-start.1 = (bf16[512,768]{1,0:T(8,128)(2,1)}, bf16[512,768]{1,0:T(8,128)(2,1)}, u32[]{:S(2)}, u32[]{:S(2)}) collective-permute-start(bf16[512,768]{1,0:T(8,128)(2,1)} %bitcast.249), channel_id=1, source_target_pairs={{0,4},{4,0},{1,5},{5,1},{2,6},{6,2},{3,7},{7,3},{8,12},{12,8},{9,1... | collective-permute-start | bytes 2359304 | tf_op jit(solution)/shard_map/ppermute | solution.py:633
  32.0 82.4 %collective-permute-start = (bf16[384,1024]{1,0:T(8,128)(2,1)}, bf16[384,1024]{1,0:T(8,128)(2,1)}, u32[]{:S(2)}, u32[]{:S(2)}) collective-permute-start(bf16[384,1024]{1,0:T(8,128)(2,1)} %bitcast.250), channel_id=1, source_target_pairs={{0,4},{4,0},{1,5},{5,1},{2,6},{6,2},{3,7},{7,3},{8,12},{12,8},{9,1... | collective-permute-start | bytes 2359304 | tf_op jit(solution)/shard_map/ppermute | solution.py:633
  116.0 420.7 %all-gather.10.cloned.1.call-start = ((), (), s32[]{:S(2)}) async-start(), calls=%async_computation.3 | async-start | bytes 9461760 | tf_op jit(solution)/shard_map/all_gather | solution.py:639
  118.2 444.3 %all-gather.12.cloned.1.call-start = ((), (), s32[]{:S(2)}) async-start(), calls=%async_computation.4 | async-start | bytes 8650752 | tf_op jit(solution)/shard_map/all_gather | solution.py:713
  203.4 44.9 %collective-permute-start.4 = (bf16[64,2816]{1,0:T(8,128)(2,1)}, bf16[64,2816]{1,0:T(8,128)(2,1)S(1)}, u32[]{:S(2)}, u32[]{:S(2)}) collective-permute-start(bf16[64,2816]{1,0:T(8,128)(2,1)} %get-tuple-element.653), channel_id=1, source_target_pairs={{0,3},{1,2},{2,1},{3,0},{4,7},{5,6},{6,5},{7,4},{8,11},{9,10},{10,... | collective-permute-start | bytes 1081352 | tf_op jit(solution)/shard_map/ppermute | solution.py:643
  206.2 823.3 %all-gather.14.cloned.1.call-start = ((), (), s32[]{:S(2)}) async-start(), calls=%async_computation.6 | async-start | bytes 4423680 | tf_op jit(solution)/shard_map/all_gather | solution.py:741
  248.3 36.5 %collective-permute-start.7 = (bf16[64,2816]{1,0:T(8,128)(2,1)}, bf16[64,2816]{1,0:T(8,128)(2,1)S(1)}, u32[]{:S(2)}, u32[]{:S(2)}) collective-permute-start(bf16[64,2816]{1,0:T(8,128)(2,1)} %get-tuple-element.666), channel_id=1, source_target_pairs={{0,3},{1,2},{2,1},{3,0},{4,7},{5,6},{6,5},{7,4},{8,11},{9,10},{10,... | collective-permute-start | bytes 1081352 | tf_op jit(solution)/shard_map/ppermute | solution.py:643
  269.5 68.6 %collective-permute-start.14 = (bf16[64,768]{1,0:T(8,128)(2,1)}, bf16[64,768]{1,0:T(8,128)(2,1)S(1)}, u32[]{:S(2)}, u32[]{:S(2)}) collective-permute-start(bf16[64,768]{1,0:T(8,128)(2,1)} %get-tuple-element.999.refs_9_), channel_id=1, source_target_pairs={{0,1},{1,0},{2,3},{3,2},{4,5},{5,4},{6,7},{7,6},{8,9},{9,8},{10,11... | collective-permute-start | bytes 294920 | tf_op jit(solution)/shard_map/ppermute | solution.py:643
  269.5 71.2 %collective-permute-start.18 = (bf16[64,768]{1,0:T(8,128)(2,1)}, bf16[64,768]{1,0:T(8,128)(2,1)S(1)}, u32[]{:S(2)}, u32[]{:S(2)}) collective-permute-start(bf16[64,768]{1,0:T(8,128)(2,1)} %get-tuple-element.1000.refs_10_), channel_id=1, source_target_pairs={{0,2},{1,3},{2,0},{3,1},{4,6},{5,7},{6,4},{7,5},{8,10},{9,11},{10,... | collective-permute-start | bytes 294920 | tf_op jit(solution)/shard_map/ppermute | solution.py:643
  397.0 28.3 %collective-permute-start.28 = (bf16[192,768]{1,0:T(8,128)(2,1)}, bf16[192,768]{1,0:T(8,128)(2,1)}, u32[]{:S(2)}, u32[]{:S(2)}) collective-permute-start(bf16[192,768]{1,0:T(8,128)(2,1)} %get-tuple-element.740), channel_id=1, source_target_pairs={{0,3},{1,2},{2,1},{3,0},{4,7},{5,6},{6,5},{7,4},{8,11},{9,10},{10,... | collective-permute-start | bytes 884744 | tf_op jit(solution)/shard_map/ppermute | solution.py:643
  398.8 70.9 %collective-permute-start.50 = (bf16[384,1024]{1,0:T(8,128)(2,1)S(1)}, bf16[384,1024]{1,0:T(8,128)(2,1)S(1)}, u32[]{:S(2)}, u32[]{:S(2)}) collective-permute-start(bf16[384,1024]{1,0:T(8,128)(2,1)S(1)} %dynamic-slice_bitcast_fusion.8), channel_id=1, source_target_pairs={{0,4},{4,0},{1,5},{5,1},{2,6},{6,2},{3,7},{7,3},{8,12},{12,8},{9,1... | collective-permute-start | bytes 2359304 | tf_op jit(solution)/shard_map/ppermute | solution.py:633
  426.5 28.8 %collective-permute-start.31 = (bf16[192,768]{1,0:T(8,128)(2,1)}, bf16[192,768]{1,0:T(8,128)(2,1)S(1)}, u32[]{:S(2)}, u32[]{:S(2)}) collective-permute-start(bf16[192,768]{1,0:T(8,128)(2,1)} %get-tuple-element.753), channel_id=1, source_target_pairs={{0,3},{1,2},{2,1},{3,0},{4,7},{5,6},{6,5},{7,4},{8,11},{9,10},{10,... | collective-permute-start | bytes 884744 | tf_op jit(solution)/shard_map/ppermute | solution.py:643
  442.4 71.9 %collective-permute-start.38 = (bf16[64,768]{1,0:T(8,128)(2,1)}, bf16[64,768]{1,0:T(8,128)(2,1)S(1)}, u32[]{:S(2)}, u32[]{:S(2)}) collective-permute-start(bf16[64,768]{1,0:T(8,128)(2,1)} %get-tuple-element.851.refs_9_), channel_id=1, source_target_pairs={{0,1},{1,0},{2,3},{3,2},{4,5},{5,4},{6,7},{7,6},{8,9},{9,8},{10,11... | collective-permute-start | bytes 294920 | tf_op jit(solution)/shard_map/ppermute | solution.py:643
  443.6 72.3 %collective-permute-start.42 = (bf16[64,768]{1,0:T(8,128)(2,1)}, bf16[64,768]{1,0:T(8,128)(2,1)S(1)}, u32[]{:S(2)}, u32[]{:S(2)}) collective-permute-start(bf16[64,768]{1,0:T(8,128)(2,1)} %get-tuple-element.852.refs_10_), channel_id=1, source_target_pairs={{0,2},{1,3},{2,0},{3,1},{4,6},{5,7},{6,4},{7,5},{8,10},{9,11},{10,... | collective-permute-start | bytes 294920 | tf_op jit(solution)/shard_map/ppermute | solution.py:643
  616.3 36.8 %collective-permute-start.51 = (bf16[64,768]{1,0:T(8,128)(2,1)}, bf16[64,768]{1,0:T(8,128)(2,1)S(1)}, u32[]{:S(2)}, u32[]{:S(2)}) collective-permute-start(bf16[64,768]{1,0:T(8,128)(2,1)} %get-tuple-element.821), channel_id=1, source_target_pairs={{0,1},{1,0},{2,3},{3,2},{4,5},{5,4},{6,7},{7,6},{8,9},{9,8},{10,11... | collective-permute-start | bytes 294920 | tf_op jit(solution)/shard_map/ppermute | solution.py:643
  617.8 35.3 %collective-permute-start.52 = (bf16[64,768]{1,0:T(8,128)(2,1)}, bf16[64,768]{1,0:T(8,128)(2,1)S(1)}, u32[]{:S(2)}, u32[]{:S(2)}) collective-permute-start(bf16[64,768]{1,0:T(8,128)(2,1)} %get-tuple-element.822), channel_id=1, source_target_pairs={{0,2},{1,3},{2,0},{3,1},{4,6},{5,7},{6,4},{7,5},{8,10},{9,11},{10,... | collective-permute-start | bytes 294920 | tf_op jit(solution)/shard_map/ppermute | solution.py:643
  618.3 34.8 %collective-permute-start.53 = (bf16[64,768]{1,0:T(8,128)(2,1)}, bf16[64,768]{1,0:T(8,128)(2,1)S(1)}, u32[]{:S(2)}, u32[]{:S(2)}) collective-permute-start(bf16[64,768]{1,0:T(8,128)(2,1)} %get-tuple-element.823), channel_id=1, source_target_pairs={{0,3},{1,2},{2,1},{3,0},{4,7},{5,6},{6,5},{7,4},{8,11},{9,10},{10,... | collective-permute-start | bytes 294920 | tf_op jit(solution)/shard_map/ppermute | solution.py:643
  653.8 37.6 %collective-permute-start.57 = (bf16[1024,1024]{1,0:T(8,128)(2,1)}, bf16[1024,1024]{1,0:T(8,128)(2,1)}, u32[]{:S(2)}, u32[]{:S(2)}) collective-permute-start(bf16[1024,1024]{1,0:T(8,128)(2,1)} %convolution_convert_fusion.6), channel_id=1, source_target_pairs={{0,8},{8,0},{1,9},{9,1},{2,10},{10,2},{3,11},{11,3},{4,12},{12,4},... | collective-permute-start | bytes 6291464 | tf_op jit(solution)/shard_map/ppermute | solution.py:811
  653.8 37.6 %collective-permute-start.58 = (bf16[1024,1024]{1,0:T(8,128)(2,1)}, bf16[1024,1024]{1,0:T(8,128)(2,1)S(1)}, u32[]{:S(2)}, u32[]{:S(2)}) collective-permute-start(bf16[1024,1024]{1,0:T(8,128)(2,1)} %convolution_convert_fusion.5), channel_id=1, source_target_pairs={{0,8},{8,0},{1,9},{9,1},{2,10},{10,2},{3,11},{11,3},{4,12},{12,4},... | collective-permute-start | bytes 6291464 | tf_op jit(solution)/shard_map/ppermute | solution.py:811
  662.7 28.6 %collective-permute-start.61 = (bf16[64,768]{1,0:T(8,128)(2,1)S(1)}, bf16[64,768]{1,0:T(8,128)(2,1)S(1)}, u32[]{:S(2)}, u32[]{:S(2)}) collective-permute-start(bf16[64,768]{1,0:T(8,128)(2,1)S(1)} %copy-done.236), channel_id=1, source_target_pairs={{0,1},{1,0},{2,3},{3,2},{4,5},{5,4},{6,7},{7,6},{8,9},{9,8},{10,11... | collective-permute-start | bytes 294920 | tf_op jit(solution)/shard_map/ppermute | solution.py:643
  703.9 60.0 %collective-permute-start.66 = (bf16[256,4096]{1,0:T(8,128)(2,1)}, bf16[256,4096]{1,0:T(8,128)(2,1)}, u32[]{:S(2)}, u32[]{:S(2)}) collective-permute-start(bf16[256,4096]{1,0:T(8,128)(2,1)} %convolution_convert_fusion.1), channel_id=1, source_target_pairs={{0,8},{8,0},{1,9},{9,1},{2,10},{10,2},{3,11},{11,3},{4,12},{12,4},... | collective-permute-start | bytes 6291464 | tf_op jit(solution)/shard_map/ppermute | solution.py:811
  704.0 60.4 %collective-permute-start.67 = (bf16[256,4096]{1,0:T(8,128)(2,1)}, bf16[256,4096]{1,0:T(8,128)(2,1)}, u32[]{:S(2)}, u32[]{:S(2)}) collective-permute-start(bf16[256,4096]{1,0:T(8,128)(2,1)} %convolution_convert_fusion), channel_id=1, source_target_pairs={{0,8},{8,0},{1,9},{9,1},{2,10},{10,2},{3,11},{11,3},{4,12},{12,4},... | collective-permute-start | bytes 6291464 | tf_op jit(solution)/shard_map/ppermute | solution.py:811
  704.4 29.9 %collective-permute-start.71 = (bf16[96,1024]{1,0:T(8,128)(2,1)}, bf16[96,1024]{1,0:T(8,128)(2,1)S(1)}, u32[]{:S(2)}, u32[]{:S(2)}) collective-permute-start(bf16[96,1024]{1,0:T(8,128)(2,1)} %get-tuple-element.904), channel_id=1, source_target_pairs={{0,4},{4,0},{1,5},{5,1},{2,6},{6,2},{3,7},{7,3},{8,12},{12,8},{9,1... | collective-permute-start | bytes 589832 | tf_op jit(solution)/shard_map/ppermute | solution.py:811
  734.3 27.9 %collective-permute-start.68 = (bf16[1024,512]{1,0:T(8,128)(2,1)}, bf16[1024,512]{1,0:T(8,128)(2,1)}, u32[]{:S(2)}, u32[]{:S(2)}) collective-permute-start(bf16[1024,512]{1,0:T(8,128)(2,1)} %get-tuple-element.901), channel_id=1, source_target_pairs={{0,16},{16,0},{1,17},{17,1},{2,18},{18,2},{3,19},{19,3},{4,20},{20... | collective-permute-start | bytes 3145736 | tf_op jit(solution)/shard_map/ppermute | solution.py:811
  760.3 28.4 %collective-permute-start.80 = (bf16[192,768]{1,0:T(8,128)(2,1)}, bf16[192,768]{1,0:T(8,128)(2,1)S(1)}, u32[]{:S(2)}, u32[]{:S(2)}) collective-permute-start(bf16[192,768]{1,0:T(8,128)(2,1)} %get-tuple-element.856), channel_id=1, source_target_pairs={{0,1},{1,0},{2,3},{3,2},{4,5},{5,4},{6,7},{7,6},{8,9},{9,8},{10,11... | collective-permute-start | bytes 884744 | tf_op jit(solution)/shard_map/ppermute | solution.py:643
  761.5 28.8 %collective-permute-start.84 = (bf16[192,768]{1,0:T(8,128)(2,1)}, bf16[192,768]{1,0:T(8,128)(2,1)}, u32[]{:S(2)}, u32[]{:S(2)}) collective-permute-start(bf16[192,768]{1,0:T(8,128)(2,1)} %get-tuple-element.857), channel_id=1, source_target_pairs={{0,2},{1,3},{2,0},{3,1},{4,6},{5,7},{6,4},{7,5},{8,10},{9,11},{10,... | collective-permute-start | bytes 884744 | tf_op jit(solution)/shard_map/ppermute | solution.py:643
  784.9 31.6 %collective-permute-start.88 = (bf16[192,768]{1,0:T(8,128)(2,1)S(1)}, bf16[192,768]{1,0:T(8,128)(2,1)S(1)}, u32[]{:S(2)}, u32[]{:S(2)}) collective-permute-start(bf16[192,768]{1,0:T(8,128)(2,1)S(1)} %copy-done.205), channel_id=1, source_target_pairs={{0,3},{1,2},{2,1},{3,0},{4,7},{5,6},{6,5},{7,4},{8,11},{9,10},{10,... | collective-permute-start | bytes 884744 | tf_op jit(solution)/shard_map/ppermute | solution.py:643
  786.6 30.8 %collective-permute-start.82 = (bf16[192,768]{1,0:T(8,128)(2,1)S(1)}, bf16[192,768]{1,0:T(8,128)(2,1)S(1)}, u32[]{:S(2)}, u32[]{:S(2)}) collective-permute-start(bf16[192,768]{1,0:T(8,128)(2,1)S(1)} %copy-done.209), channel_id=1, source_target_pairs={{0,1},{1,0},{2,3},{3,2},{4,5},{5,4},{6,7},{7,6},{8,9},{9,8},{10,11... | collective-permute-start | bytes 884744 | tf_op jit(solution)/shard_map/ppermute | solution.py:643
  787.8 31.2 %collective-permute-start.86 = (bf16[192,768]{1,0:T(8,128)(2,1)S(1)}, bf16[192,768]{1,0:T(8,128)(2,1)S(1)}, u32[]{:S(2)}, u32[]{:S(2)}) collective-permute-start(bf16[192,768]{1,0:T(8,128)(2,1)S(1)} %copy-done.207), channel_id=1, source_target_pairs={{0,2},{1,3},{2,0},{3,1},{4,6},{5,7},{6,4},{7,5},{8,10},{9,11},{10,... | collective-permute-start | bytes 884744 | tf_op jit(solution)/shard_map/ppermute | solution.py:643
  788.6 31.6 %collective-permute-start.90 = (bf16[192,768]{1,0:T(8,128)(2,1)S(1)}, bf16[192,768]{1,0:T(8,128)(2,1)S(1)}, u32[]{:S(2)}, u32[]{:S(2)}) collective-permute-start(bf16[192,768]{1,0:T(8,128)(2,1)S(1)} %copy-done.206), channel_id=1, source_target_pairs={{0,3},{1,2},{2,1},{3,0},{4,7},{5,6},{6,5},{7,4},{8,11},{9,10},{10,... | collective-permute-start | bytes 884744 | tf_op jit(solution)/shard_map/ppermute | solution.py:643
  790.3 30.6 %collective-permute-start.81 = (bf16[192,768]{1,0:T(8,128)(2,1)S(1)}, bf16[192,768]{1,0:T(8,128)(2,1)S(1)}, u32[]{:S(2)}, u32[]{:S(2)}) collective-permute-start(bf16[192,768]{1,0:T(8,128)(2,1)S(1)} %copy-done.211), channel_id=1, source_target_pairs={{0,1},{1,0},{2,3},{3,2},{4,5},{5,4},{6,7},{7,6},{8,9},{9,8},{10,11... | collective-permute-start | bytes 884744 | tf_op jit(solution)/shard_map/ppermute | solution.py:643
  826.6 65.2 %collective-permute-start.76 = (bf16[256,2048]{1,0:T(8,128)(2,1)}, bf16[256,2048]{1,0:T(8,128)(2,1)}, u32[]{:S(2)}, u32[]{:S(2)}) collective-permute-start(bf16[256,2048]{1,0:T(8,128)(2,1)} %get-tuple-element.940), channel_id=1, source_target_pairs={{0,16},{16,0},{1,17},{17,1},{2,18},{18,2},{3,19},{19,3},{4,20},{20... | collective-permute-start | bytes 3145736 | tf_op jit(solution)/shard_map/ppermute | solution.py:811
  833.3 59.2 %collective-permute-start.77 = (bf16[2,2,128,1024]{3,2,1,0:T(8,128)(2,1)}, bf16[2,2,128,1024]{3,2,1,0:T(8,128)(2,1)}, u32[]{:S(2)}, u32[]{:S(2)}) collective-permute-start(bf16[2,2,128,1024]{3,2,1,0:T(8,128)(2,1)} %get-tuple-element.941), channel_id=1, source_target_pairs={{0,1},{1,0},{2,3},{3,2},{4,5},{5,4},{6,7},{7,6},{8,9},{9,8},{10,11... | collective-permute-start | bytes 3145736 | tf_op jit(solution)/shard_map/ppermute | solution.py:811
  834.5 57.3 %collective-permute-start.78 = (bf16[256,1024]{1,0:T(8,128)(2,1)}, bf16[256,1024]{1,0:T(8,128)(2,1)}, u32[]{:S(2)}, u32[]{:S(2)}) collective-permute-start(bf16[256,1024]{1,0:T(8,128)(2,1)} %fusion.70), channel_id=1, source_target_pairs={{0,16},{16,0},{1,17},{17,1},{2,18},{18,2},{3,19},{19,3},{4,20},{20... | collective-permute-start | bytes 1572872 | tf_op jit(solution)/shard_map/ppermute | solution.py:811
  918.4 41.2 %collective-permute-start.100 = (bf16[256,3072]{1,0:T(8,128)(2,1)}, bf16[256,3072]{1,0:T(8,128)(2,1)}, u32[]{:S(2)}, u32[]{:S(2)}) collective-permute-start(bf16[256,3072]{1,0:T(8,128)(2,1)} %convolution_convert_fusion.3), channel_id=1, source_target_pairs={{0,8},{8,0},{1,9},{9,1},{2,10},{10,2},{3,11},{11,3},{4,12},{12,4},... | collective-permute-start | bytes 4718600 | tf_op jit(solution)/shard_map/ppermute | solution.py:811
  920.3 39.3 %collective-permute-start.101 = (bf16[256,3072]{1,0:T(8,128)(2,1)}, bf16[256,3072]{1,0:T(8,128)(2,1)}, u32[]{:S(2)}, u32[]{:S(2)}) collective-permute-start(bf16[256,3072]{1,0:T(8,128)(2,1)} %convolution_convert_fusion.2), channel_id=1, source_target_pairs={{0,8},{8,0},{1,9},{9,1},{2,10},{10,2},{3,11},{11,3},{4,12},{12,4},... | collective-permute-start | bytes 4718600 | tf_op jit(solution)/shard_map/ppermute | solution.py:811
  921.6 37.3 %collective-permute-start.98 = (bf16[256,2048]{1,0:T(8,128)(2,1)}, bf16[256,2048]{1,0:T(8,128)(2,1)S(1)}, u32[]{:S(2)}, u32[]{:S(2)}) collective-permute-start(bf16[256,2048]{1,0:T(8,128)(2,1)} %get-tuple-element.984), channel_id=1, source_target_pairs={{0,16},{16,0},{1,17},{17,1},{2,18},{18,2},{3,19},{19,3},{4,20},{20... | collective-permute-start | bytes 3145736 | tf_op jit(solution)/shard_map/ppermute | solution.py:811
  923.5 32.5 %collective-permute-start.96 = (bf16[256,1024]{1,0:T(8,128)(2,1)}, bf16[256,1024]{1,0:T(8,128)(2,1)S(1)}, u32[]{:S(2)}, u32[]{:S(2)}) collective-permute-start(bf16[256,1024]{1,0:T(8,128)(2,1)} %convolution_convert_fusion.12), channel_id=1, source_target_pairs={{0,8},{8,0},{1,9},{9,1},{2,10},{10,2},{3,11},{11,3},{4,12},{12,4},... | collective-permute-start | bytes 1572872 | tf_op jit(solution)/shard_map/ppermute | solution.py:811
  923.5 33.6 %collective-permute-start.99 = (bf16[2,128,1024]{2,1,0:T(8,128)(2,1)}, bf16[2,128,1024]{2,1,0:T(8,128)(2,1)S(1)}, u32[]{:S(2)}, u32[]{:S(2)}) collective-permute-start(bf16[2,128,1024]{2,1,0:T(8,128)(2,1)} %get-tuple-element.985), channel_id=1, source_target_pairs={{0,2},{2,0},{1,3},{3,1},{4,6},{6,4},{5,7},{7,5},{8,10},{10,8},{9,1... | collective-permute-start | bytes 1572872 | tf_op jit(solution)/shard_map/ppermute | solution.py:811
  982.6 38.0 %collective-permute-start.109 = (bf16[2,2,32,4096]{3,2,1,0:T(8,128)(2,1)S(1)}, bf16[2,2,32,4096]{3,2,1,0:T(8,128)(2,1)S(1)}, u32[]{:S(2)}, u32[]{:S(2)}) collective-permute-start(bf16[2,2,32,4096]{3,2,1,0:T(8,128)(2,1)S(1)} %get-tuple-element.1040), channel_id=1, source_target_pairs={{0,1},{1,0},{2,3},{3,2},{4,5},{5,4},{6,7},{7,6},{8,9},{9,8},{10,11... | collective-permute-start | bytes 3145736 | tf_op jit(solution)/shard_map/ppermute | solution.py:811
  983.5 37.0 %collective-permute-start.111 = (bf16[256,1536]{1,0:T(8,128)(2,1)}, bf16[256,1536]{1,0:T(8,128)(2,1)S(1)}, u32[]{:S(2)}, u32[]{:S(2)}) collective-permute-start(bf16[256,1536]{1,0:T(8,128)(2,1)} %get-tuple-element.1042), channel_id=1, source_target_pairs={{0,16},{16,0},{1,17},{17,1},{2,18},{18,2},{3,19},{19,3},{4,20},{20... | collective-permute-start | bytes 2359304 | tf_op jit(solution)/shard_map/ppermute | solution.py:811
  984.0 36.6 %collective-permute-start.107 = (bf16[256,1024]{1,0:T(8,128)(2,1)}, bf16[256,1024]{1,0:T(8,128)(2,1)S(1)}, u32[]{:S(2)}, u32[]{:S(2)}) collective-permute-start(bf16[256,1024]{1,0:T(8,128)(2,1)} %fusion.73), channel_id=1, source_target_pairs={{0,16},{16,0},{1,17},{17,1},{2,18},{18,2},{3,19},{19,3},{4,20},{20... | collective-permute-start | bytes 1572872 | tf_op jit(solution)/shard_map/ppermute | solution.py:811
  985.6 34.9 %collective-permute-start.110 = (bf16[128,1024]{1,0:T(8,128)(2,1)}, bf16[128,1024]{1,0:T(8,128)(2,1)S(1)}, u32[]{:S(2)}, u32[]{:S(2)}) collective-permute-start(bf16[128,1024]{1,0:T(8,128)(2,1)} %get-tuple-element.1041), channel_id=1, source_target_pairs={{0,4},{4,0},{1,5},{5,1},{2,6},{6,2},{3,7},{7,3},{8,12},{12,8},{9,1... | collective-permute-start | bytes 786440 | tf_op jit(solution)/shard_map/ppermute | solution.py:811
  986.3 34.2 %collective-permute-start.112 = (bf16[2,32,1024]{2,1,0:T(8,128)(2,1)}, bf16[2,32,1024]{2,1,0:T(8,128)(2,1)}, u32[]{:S(2)}, u32[]{:S(2)}) collective-permute-start(bf16[2,32,1024]{2,1,0:T(8,128)(2,1)} %get-tuple-element.1043), channel_id=1, source_target_pairs={{0,2},{2,0},{1,3},{3,1},{4,6},{6,4},{5,7},{7,5},{8,10},{10,8},{9,1... | collective-permute-start | bytes 393224 | tf_op jit(solution)/shard_map/ppermute | solution.py:811
  1044.6 39.4 %collective-permute-start.125 = (bf16[64,2816]{1,0:T(8,128)(2,1)}, bf16[64,2816]{1,0:T(8,128)(2,1)S(1)}, u32[]{:S(2)}, u32[]{:S(2)}) collective-permute-start(bf16[64,2816]{1,0:T(8,128)(2,1)} %get-tuple-element.1005), channel_id=1, source_target_pairs={{0,2},{1,3},{2,0},{3,1},{4,6},{5,7},{6,4},{7,5},{8,10},{9,11},{10,... | collective-permute-start | bytes 1081352 | tf_op jit(solution)/shard_map/ppermute | solution.py:643
  1045.1 39.7 %collective-permute-start.126 = (bf16[64,2816]{1,0:T(8,128)(2,1)S(1)}, bf16[64,2816]{1,0:T(8,128)(2,1)S(1)}, u32[]{:S(2)}, u32[]{:S(2)}) collective-permute-start(bf16[64,2816]{1,0:T(8,128)(2,1)S(1)} %copy-done.188), channel_id=1, source_target_pairs={{0,3},{1,2},{2,1},{3,0},{4,7},{5,6},{6,5},{7,4},{8,11},{9,10},{10,... | collective-permute-start | bytes 1081352 | tf_op jit(solution)/shard_map/ppermute | solution.py:643
  1047.4 38.0 %collective-permute-start.127 = (bf16[64,2816]{1,0:T(8,128)(2,1)}, bf16[64,2816]{1,0:T(8,128)(2,1)S(1)}, u32[]{:S(2)}, u32[]{:S(2)}) collective-permute-start(bf16[64,2816]{1,0:T(8,128)(2,1)} %get-tuple-element.1058), channel_id=1, source_target_pairs={{0,1},{1,0},{2,3},{3,2},{4,5},{5,4},{6,7},{7,6},{8,9},{9,8},{10,11... | collective-permute-start | bytes 1081352 | tf_op jit(solution)/shard_map/ppermute | solution.py:643
  1048.1 39.5 %collective-permute-start.128 = (bf16[64,2816]{1,0:T(8,128)(2,1)}, bf16[64,2816]{1,0:T(8,128)(2,1)S(1)}, u32[]{:S(2)}, u32[]{:S(2)}) collective-permute-start(bf16[64,2816]{1,0:T(8,128)(2,1)} %get-tuple-element.1059), channel_id=1, source_target_pairs={{0,2},{1,3},{2,0},{3,1},{4,6},{5,7},{6,4},{7,5},{8,10},{9,11},{10,... | collective-permute-start | bytes 1081352 | tf_op jit(solution)/shard_map/ppermute | solution.py:643
  1048.7 38.9 %collective-permute-start.129 = (bf16[64,2816]{1,0:T(8,128)(2,1)}, bf16[64,2816]{1,0:T(8,128)(2,1)S(1)}, u32[]{:S(2)}, u32[]{:S(2)}) collective-permute-start(bf16[64,2816]{1,0:T(8,128)(2,1)} %get-tuple-element.1060), channel_id=1, source_target_pairs={{0,3},{1,2},{2,1},{3,0},{4,7},{5,6},{6,5},{7,4},{8,11},{9,10},{10,... | collective-permute-start | bytes 1081352 | tf_op jit(solution)/shard_map/ppermute | solution.py:643
  1111.3 41.6 %collective-permute-start.134 = (bf16[2,2,32,3072]{3,2,1,0:T(8,128)(2,1)}, bf16[2,2,32,3072]{3,2,1,0:T(8,128)(2,1)}, u32[]{:S(2)}, u32[]{:S(2)}) collective-permute-start(bf16[2,2,32,3072]{3,2,1,0:T(8,128)(2,1)} %get-tuple-element.1134), channel_id=1, source_target_pairs={{0,1},{1,0},{2,3},{3,2},{4,5},{5,4},{6,7},{7,6},{8,9},{9,8},{10,11... | collective-permute-start | bytes 2359304 | tf_op jit(solution)/shard_map/ppermute | solution.py:811
  1112.2 40.7 %collective-permute-start.132 = (bf16[256,1024]{1,0:T(8,128)(2,1)}, bf16[256,1024]{1,0:T(8,128)(2,1)}, u32[]{:S(2)}, u32[]{:S(2)}) collective-permute-start(bf16[256,1024]{1,0:T(8,128)(2,1)} %convolution_convert_fusion.11), channel_id=1, source_target_pairs={{0,8},{8,0},{1,9},{9,1},{2,10},{10,2},{3,11},{11,3},{4,12},{12,4},... | collective-permute-start | bytes 1572872 | tf_op jit(solution)/shard_map/ppermute | solution.py:811
  1112.2 40.7 %collective-permute-start.133 = (bf16[256,1024]{1,0:T(8,128)(2,1)}, bf16[256,1024]{1,0:T(8,128)(2,1)}, u32[]{:S(2)}, u32[]{:S(2)}) collective-permute-start(bf16[256,1024]{1,0:T(8,128)(2,1)} %convolution_convert_fusion.10), channel_id=1, source_target_pairs={{0,8},{8,0},{1,9},{9,1},{2,10},{10,2},{3,11},{11,3},{4,12},{12,4},... | collective-permute-start | bytes 1572872 | tf_op jit(solution)/shard_map/ppermute | solution.py:811
  1112.7 37.0 %collective-permute-start.131 = (bf16[32,4096]{1,0:T(8,128)(2,1)S(1)}, bf16[32,4096]{1,0:T(8,128)(2,1)}, u32[]{:S(2)}, u32[]{:S(2)}) collective-permute-start(bf16[32,4096]{1,0:T(8,128)(2,1)S(1)} %get-tuple-element.1131), channel_id=1, source_target_pairs={{0,4},{4,0},{1,5},{5,1},{2,6},{6,2},{3,7},{7,3},{8,12},{12,8},{9,1... | collective-permute-start | bytes 786440 | tf_op jit(solution)/shard_map/ppermute | solution.py:811
  1113.9 35.9 %collective-permute-start.130 = (bf16[2,32,1024]{2,1,0:T(8,128)(2,1)}, bf16[2,32,1024]{2,1,0:T(8,128)(2,1)S(1)}, u32[]{:S(2)}, u32[]{:S(2)}) collective-permute-start(bf16[2,32,1024]{2,1,0:T(8,128)(2,1)} %get-tuple-element.1130), channel_id=1, source_target_pairs={{0,2},{2,0},{1,3},{3,1},{4,6},{6,4},{5,7},{7,5},{8,10},{10,8},{9,1... | collective-permute-start | bytes 393224 | tf_op jit(solution)/shard_map/ppermute | solution.py:811
  1152.1 28.6 %collective-permute-start.141 = (bf16[64,2816]{1,0:T(8,128)(2,1)}, bf16[64,2816]{1,0:T(8,128)(2,1)}, u32[]{:S(2)}, u32[]{:S(2)}) collective-permute-start(bf16[64,2816]{1,0:T(8,128)(2,1)} %get-tuple-element.1105), channel_id=1, source_target_pairs={{0,1},{1,0},{2,3},{3,2},{4,5},{5,4},{6,7},{7,6},{8,9},{9,8},{10,11... | collective-permute-start | bytes 1081352 | tf_op jit(solution)/shard_map/ppermute | solution.py:643
  1184.9 28.8 %collective-permute-start.146 = (bf16[64,2816]{1,0:T(8,128)(2,1)}, bf16[64,2816]{1,0:T(8,128)(2,1)}, u32[]{:S(2)}, u32[]{:S(2)}) collective-permute-start(bf16[64,2816]{1,0:T(8,128)(2,1)} %get-tuple-element.1153), channel_id=1, source_target_pairs={{0,3},{1,2},{2,1},{3,0},{4,7},{5,6},{6,5},{7,4},{8,11},{9,10},{10,... | collective-permute-start | bytes 1081352 | tf_op jit(solution)/shard_map/ppermute | solution.py:643
  1307.6 29.9 %collective-permute-start.158 = (bf16[256,1024]{1,0:T(8,128)(2,1)S(1)}, bf16[256,1024]{1,0:T(8,128)(2,1)S(1)}, u32[]{:S(2)}, u32[]{:S(2)}) collective-permute-start(bf16[256,1024]{1,0:T(8,128)(2,1)S(1)} %add_convert_fusion.18), channel_id=1, source_target_pairs={{0,16},{16,0},{1,17},{17,1},{2,18},{18,2},{3,19},{19,3},{4,20},{20... | collective-permute-start | bytes 1572872 | tf_op jit(solution)/shard_map/ppermute | solution.py:811
  1308.9 28.6 %collective-permute-start.157 = (bf16[192,1024]{1,0:T(8,128)(2,1)}, bf16[192,1024]{1,0:T(8,128)(2,1)S(1)}, u32[]{:S(2)}, u32[]{:S(2)}) collective-permute-start(bf16[192,1024]{1,0:T(8,128)(2,1)} %add_convert_fusion.28), channel_id=1, source_target_pairs={{0,16},{16,0},{1,17},{17,1},{2,18},{18,2},{3,19},{19,3},{4,20},{20... | collective-permute-start | bytes 1179656 | tf_op jit(solution)/shard_map/ppermute | solution.py:811
  1309.6 27.9 %collective-permute-start.160 = (bf16[256,768]{1,0:T(8,128)(2,1)S(1)}, bf16[256,768]{1,0:T(8,128)(2,1)S(1)}, u32[]{:S(2)}, u32[]{:S(2)}) collective-permute-start(bf16[256,768]{1,0:T(8,128)(2,1)S(1)} %copy-done.81), channel_id=1, source_target_pairs={{0,4},{4,0},{1,5},{5,1},{2,6},{6,2},{3,7},{7,3},{8,12},{12,8},{9,1... | collective-permute-start | bytes 1179656 | tf_op jit(solution)/shard_map/ppermute | solution.py:811
  1342.2 28.2 %collective-permute-start.162 = (bf16[2,2,32,3200]{3,2,1,0:T(8,128)(2,1)S(1)}, bf16[2,2,32,3200]{3,2,1,0:T(8,128)(2,1)S(1)}, u32[]{:S(2)}, u32[]{:S(2)}) collective-permute-start(bf16[2,2,32,3200]{3,2,1,0:T(8,128)(2,1)S(1)} %get-tuple-element.1241), channel_id=1, source_target_pairs={{0,1},{1,0},{2,3},{3,2},{4,5},{5,4},{6,7},{7,6},{8,9},{9,8},{10,11... | collective-permute-start | bytes 2457608 | tf_op jit(solution)/shard_map/ppermute | solution.py:811
  1344.3 34.6 %collective-permute-start.165 = (bf16[192,1024]{1,0:T(8,128)(2,1)}, bf16[192,1024]{1,0:T(8,128)(2,1)}, u32[]{:S(2)}, u32[]{:S(2)}) collective-permute-start(bf16[192,1024]{1,0:T(8,128)(2,1)} %get-tuple-element.1250), channel_id=1, source_target_pairs={{0,4},{4,0},{1,5},{5,1},{2,6},{6,2},{3,7},{7,3},{8,12},{12,8},{9,1... | collective-permute-start | bytes 1179656 | tf_op jit(solution)/shard_map/ppermute | solution.py:811
  (381 other events, 5103.2 us)
Sparse Core Ops, SparseCore 0:
  17.4 153.3 all-gather.5
  173.7 131.8 all-gather.7
  308.5 90.7 all-gather.9
  402.6 111.6 all-gather.11
Sparse Core Ops, SparseCore 1:
  116.1 132.6 reduce-scatter.1
  915.1 94.1 all-gather.13

commit v4 on v3

--- a/solution.py
+++ b/solution.py
@@ -695,9 +695,6 @@
     token_low = own_object(tokens)
     dino_values = own_object(dino)
     plane_grad, token_low, dino_values = join((plane_grad, token_low, dino_values))
-    plane_low = lax.psum_scatter(
-        plane_grad.reshape(2 * group * 4 * CH, count), shard_axes, scatter_dimension=0, tiled=True
-    )
     token_values = widen(token_low)
 
     normed_full, unit_a, inverse_a = normalize(token_values, gain_a, shift_a)
@@ -709,6 +706,10 @@
     middle = [lower(cross_output), lower(self_project), lower(self_output)]
     late = [lower(hidden_weight), lower(deconv_weight)]
     output_w = lower(output_weight)
+    plane_grad = after(plane_grad, cross_in[0])
+    plane_low = lax.psum_scatter(
+        plane_grad.reshape(2 * group * 4 * CH, count), shard_axes, scatter_dimension=0, tiled=True
+    )
     middle, late = gather(middle), gather(late)
     output_w = lax.all_gather(output_w, every, axis=0, tiled=True)
     cross_w = middle[:, :D]

time: 1430 us -> 1460 us (1.021)
  waiting for transfers between devices: 287 us -> 326 us
    all_gather x1, waiting for transfers between devices: 0.01 us -> 51.2 us  [body(): output_w = lax.all_gather(output_w, every, axis=0, tiled=True)]
    unnamed x546 -> x530, local copies, waits for them, and re-layouts: 34.4 us -> 30.5 us
  transfers between devices with their start and end apart: 176 -> 176, of which waited for: 44 -> 50; matrix products, arithmetic and copies ran while one was open for 18% -> 18% of each run, Pallas kernels for 36% -> 35%
where the time goes in v4:
time: 1460 us; the launch traced here: 1450 us
  Pallas kernels  520 us (36%)
  waiting for transfers between devices  326 us (22%)
  matrix products  218 us (15%)
  starting transfers between devices  177 us (12%)
  local copies, waits for them, and re-layouts  99.9 us (7%)
  other arithmetic  94.3 us (6%)
  between operations  17.4 us (1%)
    pallas_call x8, Pallas kernels, attend_backward(): pl.pallas_call(functools.partial(backward_kernel, chunks=chunks, block=bl...  229 us
    dot_general x62, matrix products, dot(): lax.dot_general(left, right, (dims, ((), ())), preferred_element_type=f32)  218 us
    ppermute x96, waiting for transfers between devices, exchange(): lax.ppermute(chunks[k], group_axes, [(i, i ^ k) for i in range(group)])  174 us
    pallas_call x8, Pallas kernels, attend_forward(): pl.pallas_call(functools.partial(forward_kernel, chunks=chunks, block=blo...  125 us
    ppermute x96, starting transfers between devices, exchange(): lax.ppermute(chunks[k], group_axes, [(i, i ^ k) for i in range(group)])  110 us
    pallas_call x1, Pallas kernels, scatter_points(): pl.pallas_call(functools.partial(scatter_kernel, width=width), grid_spec=...  72 us
    ppermute x71, waiting for transfers between devices, turn(): lax.ppermute(x, axis, SWAP)  58.6 us
    ppermute x71, starting transfers between devices, turn(): lax.ppermute(x, axis, SWAP)  58.5 us
  transfers between devices with their start and end apart: 176, of which 50 were waited for; matrix products, arithmetic and copies ran while one was open for 18% of the time, Pallas kernels for 35%

profile of v4, /device:TPU:0, one launch (start us, length us, event | category | flops | bytes accessed | tf_op | source)
XLA Modules:
  0.0 1452.0 jit_solution(14957590231003874227)
XLA Ops:
  40.0 72.0 %scatter_points.1 = bf16[2,4,320,768]{3,2,1,0:T(8,128)(2,1)} custom-call(s32[2]{0:T(128)} %object_ref.1, s32[2,3,4096]{2,1,0:T(4,128)} %reshape.274.cell_ref, f32[2,6,4096]{2,1,0:T(8,128)} %reshape.275.frac_ref, f32[2,1,128]{2,1,0:T(1,128)} %bitcast.314, bf16[256,2560]{1,0:T(8,128)(2,1)} %grad_ref.1), custom_call_target="tpu_custom_call" | custom-call | flops 51539607552 | bytes 10485760 | tf_op jit(solution)/shard_map/scatter_points/pallas_call | solution.py:554
  117.0 41.8 %all-gather.6.cloned.1.call-done = bf16[1024,3968]{1,0:T(8,128)(2,1)} async-done(((bf16[32,3968]{1,0:T(8,128)(2,1)}), bf16[1024,3968]{1,0:T(8,128)(2,1)}) %all-gather.6.cloned.1.call-update) | async-done | bytes 8126480 | tf_op jit(solution)/shard_map/all_gather | solution.py:639
  172.0 5.4 fusion.51
  177.4 6.3 convolution_convert_fusion.4
  183.7 6.0 split_pair.1
  193.3 13.5 collective-permute-done.2.refs_1_
  207.0 13.3 collective-permute-done.4.refs_3_
  224.7 17.6 %attend_forward.8 = (bf16[64,768]{1,0:T(8,128)(2,1)}, bf16[64,768]{1,0:T(8,128)(2,1)}, bf16[64,768]{1,0:T(8,128)(2,1)}, bf16[64,768]{1,0:T(8,128)(2,1)}, f32[4,1,768]{2,1,0:T(1,128)}) custom-call(bf16[64,2816]{1,0:T(8,128)(2,1)} %get-tuple-element.992.refs_0_, bf16[64,2816]{1,0:T(8,128)(2,1)} %copy-done.183, bf16[64,2816]{1,0:T(8,128)(2,1)} %copy-done.184, ...), custom_call_target="tpu_custom_call" | custom-call | flops 12884901888 | bytes 1048576 | tf_op jit(solution)/shard_map/attend_forward/pallas_call | solution.py:145
  243.4 4.8 collective-permute-done.6.refs_2_
  248.2 12.7 collective-permute-done.7.refs_3_
  264.3 17.3 %attend_forward.9 = (bf16[64,768]{1,0:T(8,128)(2,1)}, bf16[64,768]{1,0:T(8,128)(2,1)}, bf16[64,768]{1,0:T(8,128)(2,1)}, bf16[64,768]{1,0:T(8,128)(2,1)}, f32[4,1,768]{2,1,0:T(1,128)}) custom-call(bf16[64,2816]{1,0:T(8,128)(2,1)} %get-tuple-element.1046.refs_0_, bf16[64,2816]{1,0:T(8,128)(2,1)} %copy-done.180, bf16[64,2816]{1,0:T(8,128)(2,1)} %copy-done.181, ...), custom_call_target="tpu_custom_call" | custom-call | flops 12884901888 | bytes 1048576 | tf_op jit(solution)/shard_map/attend_forward/pallas_call | solution.py:145
  289.0 17.4 %attend_forward.10 = (bf16[64,768]{1,0:T(8,128)(2,1)}, bf16[64,768]{1,0:T(8,128)(2,1)}, bf16[64,768]{1,0:T(8,128)(2,1)}, bf16[64,768]{1,0:T(8,128)(2,1)}, f32[4,1,768]{2,1,0:T(1,128)}) custom-call(bf16[64,2816]{1,0:T(8,128)(2,1)} %get-tuple-element.1088.refs_0_, bf16[64,2816]{1,0:T(8,128)(2,1)} %copy-done.178, bf16[64,2816]{1,0:T(8,128)(2,1)} %copy-done.179, ...), custom_call_target="tpu_custom_call" | custom-call | flops 12884901888 | bytes 1048576 | tf_op jit(solution)/shard_map/attend_forward/pallas_call | solution.py:145
  312.3 17.2 %attend_forward.11 = (bf16[64,768]{1,0:T(8,128)(2,1)}, bf16[64,768]{1,0:T(8,128)(2,1)}, bf16[64,768]{1,0:T(8,128)(2,1)}, bf16[64,768]{1,0:T(8,128)(2,1)}, f32[4,1,768]{2,1,0:T(1,128)}) custom-call(bf16[64,2816]{1,0:T(8,128)(2,1)} %get-tuple-element.1139.refs_0_, bf16[64,2816]{1,0:T(8,128)(2,1)} %copy-done.174, bf16[64,2816]{1,0:T(8,128)(2,1)} %copy-done.175, ...), custom_call_target="tpu_custom_call" | custom-call | flops 12884901888 | bytes 1048576 | tf_op jit(solution)/shard_map/attend_forward/pallas_call | solution.py:145
  352.1 7.1 fusion.8
  359.2 5.5 split.3
  373.2 15.8 %collective-permute-done.27.refs_2_ = bf16[192,768]{1,0:T(8,128)(2,1)S(1)} collective-permute-done((bf16[192,768]{1,0:T(8,128)(2,1)}, bf16[192,768]{1,0:T(8,128)(2,1)S(1)}, u32[]{:S(2)}, u32[]{:S(2)}) %collective-permute-start.27) | collective-permute-done | bytes 294944 | tf_op jit(solution)/shard_map/ppermute | solution.py:643
  389.0 7.1 collective-permute-done.28.refs_3_
  399.5 13.6 attend_forward.12
  413.7 11.5 collective-permute-done.30.refs_2_
  425.2 19.1 %collective-permute-done.31.refs_3_ = bf16[192,768]{1,0:T(8,128)(2,1)S(1)} collective-permute-done((bf16[192,768]{1,0:T(8,128)(2,1)}, bf16[192,768]{1,0:T(8,128)(2,1)S(1)}, u32[]{:S(2)}, u32[]{:S(2)}) %collective-permute-start.31) | collective-permute-done | bytes 294944 | tf_op jit(solution)/shard_map/ppermute | solution.py:643
  447.8 13.7 attend_forward.13
  467.3 14.1 attend_forward.14
  489.6 13.6 attend_forward.15
  513.3 4.6 collective-permute-done.48.refs_14_
  524.1 4.9 fusion.199
  531.3 12.4 fusion.2
  543.7 5.1 fusion.30
  548.8 51.2 %all-gather.12.cloned.1.call-done = bf16[4096,1024]{1,0:T(8,128)(2,1)} async-done(((bf16[128,1024]{1,0:T(8,128)(2,1)}), bf16[4096,1024]{1,0:T(8,128)(2,1)}) %all-gather.12.cloned.1.call-update) | async-done | bytes 8388624 | tf_op jit(solution)/shard_map/all_gather | solution.py:714
  600.0 18.0 %convert_reduce_fusion = (f32[4096]{0:T(1024)}, bf16[768,4096]{1,0:T(8,128)(2,1)S(1)}, bf16[768,4096]{1,0:T(8,128)(2,1)}) fusion(f32[768,4096]{1,0:T(8,128)} %fusion.2, f32[4096]{0:T(1024)S(1)} %add.529, bf16[768,1024]{1,0:T(8,128)(2,1)} %get-tuple-element.1481, bf16[4096,1024]{1,0:T(8,128)(2,1)} %all-gather.12.cloned.1.call-done), kind=kOutput, calls=%fused_computation | convolution fusion | flops 6499069952 | bytes 35160064 | tf_op jit(solution)/shard_map/dot_general | solution.py:44
  618.0 4.5 convolution_convert_fusion
  622.6 11.7 multiply_reduce_fusion
  645.5 4.6 fusion.57
  657.4 5.8 fusion.64
  663.2 4.7 convolution_convert_fusion.5
  683.0 6.9 add_convert_fusion.8
  704.2 25.0 %attend_backward.8 = (bf16[192,768]{1,0:T(8,128)(2,1)}, bf16[192,768]{1,0:T(8,128)(2,1)}, bf16[192,768]{1,0:T(8,128)(2,1)}, bf16[192,768]{1,0:T(8,128)(2,1)}) custom-call(bf16[192,768]{1,0:T(8,128)(2,1)} %get-tuple-element.844.refs_0_, bf16[192,768]{1,0:T(8,128)(2,1)} %copy-done.189, bf16[192,768]{1,0:T(8,128)(2,1)} %copy-done.190, ...), custom_call_target="tpu_custom_call" | custom-call | flops 18874368000 | bytes 1572864 | tf_op jit(solution)/shard_map/attend_backward/pallas_call | solution.py:247
  746.5 24.9 %attend_backward.10 = (bf16[192,768]{1,0:T(8,128)(2,1)}, bf16[192,768]{1,0:T(8,128)(2,1)}, bf16[192,768]{1,0:T(8,128)(2,1)}, bf16[192,768]{1,0:T(8,128)(2,1)}) custom-call(bf16[192,768]{1,0:T(8,128)(2,1)} %get-tuple-element.907.refs_0_, bf16[192,768]{1,0:T(8,128)(2,1)} %copy-done.197, bf16[192,768]{1,0:T(8,128)(2,1)} %copy-done.198, ...), custom_call_target="tpu_custom_call" | custom-call | flops 18874368000 | bytes 1572864 | tf_op jit(solution)/shard_map/attend_backward/pallas_call | solution.py:247
  772.8 25.2 %attend_backward.9 = (bf16[192,768]{1,0:T(8,128)(2,1)}, bf16[192,768]{1,0:T(8,128)(2,1)}, bf16[192,768]{1,0:T(8,128)(2,1)}, bf16[192,768]{1,0:T(8,128)(2,1)}) custom-call(bf16[192,768]{1,0:T(8,128)(2,1)} %get-tuple-element.865.refs_0_, bf16[192,768]{1,0:T(8,128)(2,1)} %copy-done.194, bf16[192,768]{1,0:T(8,128)(2,1)} %copy-done.195, ...), custom_call_target="tpu_custom_call" | custom-call | flops 18874368000 | bytes 1572864 | tf_op jit(solution)/shard_map/attend_backward/pallas_call | solution.py:247
  829.4 25.0 %attend_backward.11 = (bf16[192,768]{1,0:T(8,128)(2,1)}, bf16[192,768]{1,0:T(8,128)(2,1)}, bf16[192,768]{1,0:T(8,128)(2,1)}, bf16[192,768]{1,0:T(8,128)(2,1)}) custom-call(bf16[192,768]{1,0:T(8,128)(2,1)} %get-tuple-element.946.refs_0_, bf16[192,768]{1,0:T(8,128)(2,1)} %copy-done.191, bf16[192,768]{1,0:T(8,128)(2,1)} %copy-done.192, ...), custom_call_target="tpu_custom_call" | custom-call | flops 18874368000 | bytes 1572864 | tf_op jit(solution)/shard_map/attend_backward/pallas_call | solution.py:247
  865.4 5.8 collective-permute-done.89.refs_13_
  880.8 5.2 assemble.5
  886.1 10.6 multiply_reduce_fusion.1
  899.3 4.7 fusion.54
  911.3 4.9 convolution_convert_fusion.3
  960.4 32.5 %attend_backward.12 = (bf16[64,2816]{1,0:T(8,128)(2,1)}, bf16[64,2816]{1,0:T(8,128)(2,1)}, bf16[64,2816]{1,0:T(8,128)(2,1)}, bf16[64,2816]{1,0:T(8,128)(2,1)}) custom-call(bf16[64,2816]{1,0:T(8,128)(2,1)} %get-tuple-element.992.refs_0_, bf16[64,2816]{1,0:T(8,128)(2,1)} %copy-done.183, bf16[64,2816]{1,0:T(8,128)(2,1)} %copy-done.184, ...), custom_call_target="tpu_custom_call" | custom-call | flops 25165824000 | bytes 2097152 | tf_op jit(solution)/shard_map/attend_backward/pallas_call | solution.py:247
  996.5 5.7 fusion.12
  1025.3 32.2 %attend_backward.13 = (bf16[64,2816]{1,0:T(8,128)(2,1)}, bf16[64,2816]{1,0:T(8,128)(2,1)}, bf16[64,2816]{1,0:T(8,128)(2,1)}, bf16[64,2816]{1,0:T(8,128)(2,1)}) custom-call(bf16[64,2816]{1,0:T(8,128)(2,1)} %get-tuple-element.1046.refs_0_, bf16[64,2816]{1,0:T(8,128)(2,1)} %copy-done.180, bf16[64,2816]{1,0:T(8,128)(2,1)} %copy-done.181, ...), custom_call_target="tpu_custom_call" | custom-call | flops 25165824000 | bytes 2097152 | tf_op jit(solution)/shard_map/attend_backward/pallas_call | solution.py:247
  1072.1 4.7 collective-permute-done.124.refs_2_
  1088.6 32.2 %attend_backward.14 = (bf16[64,2816]{1,0:T(8,128)(2,1)}, bf16[64,2816]{1,0:T(8,128)(2,1)}, bf16[64,2816]{1,0:T(8,128)(2,1)}, bf16[64,2816]{1,0:T(8,128)(2,1)}) custom-call(bf16[64,2816]{1,0:T(8,128)(2,1)} %get-tuple-element.1088.refs_0_, bf16[64,2816]{1,0:T(8,128)(2,1)} %copy-done.178, bf16[64,2816]{1,0:T(8,128)(2,1)} %copy-done.179, ...), custom_call_target="tpu_custom_call" | custom-call | flops 25165824000 | bytes 2097152 | tf_op jit(solution)/shard_map/attend_backward/pallas_call | solution.py:247
  1153.2 32.4 %attend_backward.15 = (bf16[64,2816]{1,0:T(8,128)(2,1)}, bf16[64,2816]{1,0:T(8,128)(2,1)}, bf16[64,2816]{1,0:T(8,128)(2,1)}, bf16[64,2816]{1,0:T(8,128)(2,1)}) custom-call(bf16[64,2816]{1,0:T(8,128)(2,1)} %get-tuple-element.1139.refs_0_, bf16[64,2816]{1,0:T(8,128)(2,1)} %copy-done.174, bf16[64,2816]{1,0:T(8,128)(2,1)} %copy-done.175, ...), custom_call_target="tpu_custom_call" | custom-call | flops 25165824000 | bytes 2097152 | tf_op jit(solution)/shard_map/attend_backward/pallas_call | solution.py:247
  1204.6 14.0 sample_points.4
  1230.3 7.8 collective-permute-done.143.refs_6_
  1238.1 7.7 collective-permute-done.145.refs_5_
  1245.8 5.4 collective-permute-done.146.refs_7_
  1267.6 6.3 fusion.28
  1280.1 8.1 fusion.31
  1302.8 14.3 sample_points.5
  1324.4 16.4 %collective-permute-done.154 = bf16[256,768]{1,0:T(8,128)(2,1)S(1)} collective-permute-done((bf16[256,768]{1,0:T(8,128)(2,1)}, bf16[256,768]{1,0:T(8,128)(2,1)S(1)}, u32[]{:S(2)}, u32[]{:S(2)}) %collective-permute-start.154) | collective-permute-done | bytes 393248 | tf_op jit(solution)/shard_map/ppermute | solution.py:812
  1349.2 13.8 sample_points.6
  1363.0 12.0 collective-permute-done.161
  1384.8 14.0 sample_points.7
  1402.6 4.5 collective-permute-done.164
  1417.5 8.8 collective-permute-done.167
  1435.4 4.9 collective-permute-done.169
  (1117 shorter events, 524.9 us)
Async XLA Ops:
  7.2 151.6 %all-gather.6.cloned.1.call-start = ((), (), s32[]{:S(2)}) async-start(), calls=%async_computation.1 | async-start | bytes 8380416 | tf_op jit(solution)/shard_map/all_gather | solution.py:639
  16.4 328.6 %all-gather.8.cloned.1.call-start = ((), (), s32[]{:S(2)}) async-start(), calls=%async_computation.2 | async-start | bytes 10813440 | tf_op jit(solution)/shard_map/all_gather | solution.py:639
  18.4 512.9 %all-gather.10.cloned.1.call-start = ((), (), s32[]{:S(2)}) async-start(), calls=%async_computation.3 | async-start | bytes 9461760 | tf_op jit(solution)/shard_map/all_gather | solution.py:639
  19.3 524.4 %reduce-scatter.2.cloned.1.call-start = ((), (), s32[]{:S(2)}) async-start(), calls=%async_computation.5 | async-start | bytes 4423680 | tf_op jit(solution)/shard_map/reduce_scatter | solution.py:710
  23.7 88.4 %collective-permute-start.1 = (bf16[512,768]{1,0:T(8,128)(2,1)}, bf16[512,768]{1,0:T(8,128)(2,1)}, u32[]{:S(2)}, u32[]{:S(2)}) collective-permute-start(bf16[512,768]{1,0:T(8,128)(2,1)} %bitcast.249), channel_id=1, source_target_pairs={{0,4},{4,0},{1,5},{5,1},{2,6},{6,2},{3,7},{7,3},{8,12},{12,8},{9,1... | collective-permute-start | bytes 2359304 | tf_op jit(solution)/shard_map/ppermute | solution.py:633
  32.1 82.5 %collective-permute-start = (bf16[384,1024]{1,0:T(8,128)(2,1)}, bf16[384,1024]{1,0:T(8,128)(2,1)}, u32[]{:S(2)}, u32[]{:S(2)}) collective-permute-start(bf16[384,1024]{1,0:T(8,128)(2,1)} %bitcast.250), channel_id=1, source_target_pairs={{0,4},{4,0},{1,5},{5,1},{2,6},{6,2},{3,7},{7,3},{8,12},{12,8},{9,1... | collective-permute-start | bytes 2359304 | tf_op jit(solution)/shard_map/ppermute | solution.py:633
  220.3 379.7 %all-gather.12.cloned.1.call-start = ((), (), s32[]{:S(2)}) async-start(), calls=%async_computation.4 | async-start | bytes 8650752 | tf_op jit(solution)/shard_map/all_gather | solution.py:714
  221.1 846.0 %all-gather.14.cloned.1.call-start = ((), (), s32[]{:S(2)}) async-start(), calls=%async_computation.6 | async-start | bytes 4423680 | tf_op jit(solution)/shard_map/all_gather | solution.py:742
  222.1 38.7 %collective-permute-start.7 = (bf16[64,2816]{1,0:T(8,128)(2,1)}, bf16[64,2816]{1,0:T(8,128)(2,1)S(1)}, u32[]{:S(2)}, u32[]{:S(2)}) collective-permute-start(bf16[64,2816]{1,0:T(8,128)(2,1)} %get-tuple-element.667), channel_id=1, source_target_pairs={{0,3},{1,2},{2,1},{3,0},{4,7},{5,6},{6,5},{7,4},{8,11},{9,10},{10,... | collective-permute-start | bytes 1081352 | tf_op jit(solution)/shard_map/ppermute | solution.py:643
  242.3 67.7 %collective-permute-start.14 = (bf16[64,768]{1,0:T(8,128)(2,1)}, bf16[64,768]{1,0:T(8,128)(2,1)S(1)}, u32[]{:S(2)}, u32[]{:S(2)}) collective-permute-start(bf16[64,768]{1,0:T(8,128)(2,1)} %get-tuple-element.1001.refs_9_), channel_id=1, source_target_pairs={{0,1},{1,0},{2,3},{3,2},{4,5},{5,4},{6,7},{7,6},{8,9},{9,8},{10,11... | collective-permute-start | bytes 294920 | tf_op jit(solution)/shard_map/ppermute | solution.py:643
  243.3 68.3 %collective-permute-start.18 = (bf16[64,768]{1,0:T(8,128)(2,1)}, bf16[64,768]{1,0:T(8,128)(2,1)S(1)}, u32[]{:S(2)}, u32[]{:S(2)}) collective-permute-start(bf16[64,768]{1,0:T(8,128)(2,1)} %get-tuple-element.1002.refs_10_), channel_id=1, source_target_pairs={{0,2},{1,3},{2,0},{3,1},{4,6},{5,7},{6,4},{7,5},{8,10},{9,11},{10,... | collective-permute-start | bytes 294920 | tf_op jit(solution)/shard_map/ppermute | solution.py:643
  367.3 28.7 %collective-permute-start.28 = (bf16[192,768]{1,0:T(8,128)(2,1)}, bf16[192,768]{1,0:T(8,128)(2,1)}, u32[]{:S(2)}, u32[]{:S(2)}) collective-permute-start(bf16[192,768]{1,0:T(8,128)(2,1)} %get-tuple-element.741), channel_id=1, source_target_pairs={{0,3},{1,2},{2,1},{3,0},{4,7},{5,6},{6,5},{7,4},{8,11},{9,10},{10,... | collective-permute-start | bytes 884744 | tf_op jit(solution)/shard_map/ppermute | solution.py:643
  370.0 91.5 %collective-permute-start.50 = (bf16[384,1024]{1,0:T(8,128)(2,1)S(1)}, bf16[384,1024]{1,0:T(8,128)(2,1)S(1)}, u32[]{:S(2)}, u32[]{:S(2)}) collective-permute-start(bf16[384,1024]{1,0:T(8,128)(2,1)S(1)} %dynamic-slice_bitcast_fusion.8), channel_id=1, source_target_pairs={{0,4},{4,0},{1,5},{5,1},{2,6},{6,2},{3,7},{7,3},{8,12},{12,8},{9,1... | collective-permute-start | bytes 2359304 | tf_op jit(solution)/shard_map/ppermute | solution.py:633
  396.6 28.6 %collective-permute-start.30 = (bf16[192,768]{1,0:T(8,128)(2,1)}, bf16[192,768]{1,0:T(8,128)(2,1)S(1)}, u32[]{:S(2)}, u32[]{:S(2)}) collective-permute-start(bf16[192,768]{1,0:T(8,128)(2,1)} %get-tuple-element.753), channel_id=1, source_target_pairs={{0,2},{1,3},{2,0},{3,1},{4,6},{5,7},{6,4},{7,5},{8,10},{9,11},{10,... | collective-permute-start | bytes 884744 | tf_op jit(solution)/shard_map/ppermute | solution.py:643
  396.6 47.7 %collective-permute-start.31 = (bf16[192,768]{1,0:T(8,128)(2,1)}, bf16[192,768]{1,0:T(8,128)(2,1)S(1)}, u32[]{:S(2)}, u32[]{:S(2)}) collective-permute-start(bf16[192,768]{1,0:T(8,128)(2,1)} %get-tuple-element.754), channel_id=1, source_target_pairs={{0,3},{1,2},{2,1},{3,0},{4,7},{5,6},{6,5},{7,4},{8,11},{9,10},{10,... | collective-permute-start | bytes 884744 | tf_op jit(solution)/shard_map/ppermute | solution.py:643
  413.2 74.8 %collective-permute-start.38 = (bf16[64,768]{1,0:T(8,128)(2,1)}, bf16[64,768]{1,0:T(8,128)(2,1)S(1)}, u32[]{:S(2)}, u32[]{:S(2)}) collective-permute-start(bf16[64,768]{1,0:T(8,128)(2,1)} %get-tuple-element.853.refs_9_), channel_id=1, source_target_pairs={{0,1},{1,0},{2,3},{3,2},{4,5},{5,4},{6,7},{7,6},{8,9},{9,8},{10,11... | collective-permute-start | bytes 294920 | tf_op jit(solution)/shard_map/ppermute | solution.py:643
  653.8 36.8 %collective-permute-start.51 = (bf16[64,768]{1,0:T(8,128)(2,1)}, bf16[64,768]{1,0:T(8,128)(2,1)S(1)}, u32[]{:S(2)}, u32[]{:S(2)}) collective-permute-start(bf16[64,768]{1,0:T(8,128)(2,1)} %get-tuple-element.823), channel_id=1, source_target_pairs={{0,1},{1,0},{2,3},{3,2},{4,5},{5,4},{6,7},{7,6},{8,9},{9,8},{10,11... | collective-permute-start | bytes 294920 | tf_op jit(solution)/shard_map/ppermute | solution.py:643
  655.3 35.4 %collective-permute-start.52 = (bf16[64,768]{1,0:T(8,128)(2,1)}, bf16[64,768]{1,0:T(8,128)(2,1)S(1)}, u32[]{:S(2)}, u32[]{:S(2)}) collective-permute-start(bf16[64,768]{1,0:T(8,128)(2,1)} %get-tuple-element.824), channel_id=1, source_target_pairs={{0,2},{1,3},{2,0},{3,1},{4,6},{5,7},{6,4},{7,5},{8,10},{9,11},{10,... | collective-permute-start | bytes 294920 | tf_op jit(solution)/shard_map/ppermute | solution.py:643
  656.8 33.9 %collective-permute-start.53 = (bf16[64,768]{1,0:T(8,128)(2,1)}, bf16[64,768]{1,0:T(8,128)(2,1)S(1)}, u32[]{:S(2)}, u32[]{:S(2)}) collective-permute-start(bf16[64,768]{1,0:T(8,128)(2,1)} %get-tuple-element.825), channel_id=1, source_target_pairs={{0,3},{1,2},{2,1},{3,0},{4,7},{5,6},{6,5},{7,4},{8,11},{9,10},{10,... | collective-permute-start | bytes 294920 | tf_op jit(solution)/shard_map/ppermute | solution.py:643
  691.3 38.0 %collective-permute-start.57 = (bf16[1024,1024]{1,0:T(8,128)(2,1)}, bf16[1024,1024]{1,0:T(8,128)(2,1)}, u32[]{:S(2)}, u32[]{:S(2)}) collective-permute-start(bf16[1024,1024]{1,0:T(8,128)(2,1)} %convolution_convert_fusion.6), channel_id=1, source_target_pairs={{0,8},{8,0},{1,9},{9,1},{2,10},{10,2},{3,11},{11,3},{4,12},{12,4},... | collective-permute-start | bytes 6291464 | tf_op jit(solution)/shard_map/ppermute | solution.py:812
  691.3 38.0 %collective-permute-start.58 = (bf16[1024,1024]{1,0:T(8,128)(2,1)}, bf16[1024,1024]{1,0:T(8,128)(2,1)S(1)}, u32[]{:S(2)}, u32[]{:S(2)}) collective-permute-start(bf16[1024,1024]{1,0:T(8,128)(2,1)} %convolution_convert_fusion.5), channel_id=1, source_target_pairs={{0,8},{8,0},{1,9},{9,1},{2,10},{10,2},{3,11},{11,3},{4,12},{12,4},... | collective-permute-start | bytes 6291464 | tf_op jit(solution)/shard_map/ppermute | solution.py:812
  700.7 28.6 %collective-permute-start.61 = (bf16[64,768]{1,0:T(8,128)(2,1)S(1)}, bf16[64,768]{1,0:T(8,128)(2,1)S(1)}, u32[]{:S(2)}, u32[]{:S(2)}) collective-permute-start(bf16[64,768]{1,0:T(8,128)(2,1)S(1)} %copy-done.231), channel_id=1, source_target_pairs={{0,1},{1,0},{2,3},{3,2},{4,5},{5,4},{6,7},{7,6},{8,9},{9,8},{10,11... | collective-permute-start | bytes 294920 | tf_op jit(solution)/shard_map/ppermute | solution.py:643
  741.8 59.4 %collective-permute-start.66 = (bf16[256,4096]{1,0:T(8,128)(2,1)}, bf16[256,4096]{1,0:T(8,128)(2,1)}, u32[]{:S(2)}, u32[]{:S(2)}) collective-permute-start(bf16[256,4096]{1,0:T(8,128)(2,1)} %convolution_convert_fusion.1), channel_id=1, source_target_pairs={{0,8},{8,0},{1,9},{9,1},{2,10},{10,2},{3,11},{11,3},{4,12},{12,4},... | collective-permute-start | bytes 6291464 | tf_op jit(solution)/shard_map/ppermute | solution.py:812
  741.9 60.2 %collective-permute-start.67 = (bf16[256,4096]{1,0:T(8,128)(2,1)}, bf16[256,4096]{1,0:T(8,128)(2,1)}, u32[]{:S(2)}, u32[]{:S(2)}) collective-permute-start(bf16[256,4096]{1,0:T(8,128)(2,1)} %convolution_convert_fusion), channel_id=1, source_target_pairs={{0,8},{8,0},{1,9},{9,1},{2,10},{10,2},{3,11},{11,3},{4,12},{12,4},... | collective-permute-start | bytes 6291464 | tf_op jit(solution)/shard_map/ppermute | solution.py:812
  742.4 29.0 %collective-permute-start.71 = (bf16[96,1024]{1,0:T(8,128)(2,1)}, bf16[96,1024]{1,0:T(8,128)(2,1)S(1)}, u32[]{:S(2)}, u32[]{:S(2)}) collective-permute-start(bf16[96,1024]{1,0:T(8,128)(2,1)} %get-tuple-element.906), channel_id=1, source_target_pairs={{0,4},{4,0},{1,5},{5,1},{2,6},{6,2},{3,7},{7,3},{8,12},{12,8},{9,1... | collective-permute-start | bytes 589832 | tf_op jit(solution)/shard_map/ppermute | solution.py:812
  743.9 28.4 %collective-permute-start.59 = (bf16[1024,512]{1,0:T(8,128)(2,1)}, bf16[1024,512]{1,0:T(8,128)(2,1)}, u32[]{:S(2)}, u32[]{:S(2)}) collective-permute-start(bf16[1024,512]{1,0:T(8,128)(2,1)} %get-tuple-element.863), channel_id=1, source_target_pairs={{0,16},{16,0},{1,17},{17,1},{2,18},{18,2},{3,19},{19,3},{4,20},{20... | collective-permute-start | bytes 3145736 | tf_op jit(solution)/shard_map/ppermute | solution.py:812
  771.4 29.2 %collective-permute-start.68 = (bf16[1024,512]{1,0:T(8,128)(2,1)}, bf16[1024,512]{1,0:T(8,128)(2,1)}, u32[]{:S(2)}, u32[]{:S(2)}) collective-permute-start(bf16[1024,512]{1,0:T(8,128)(2,1)} %get-tuple-element.903), channel_id=1, source_target_pairs={{0,16},{16,0},{1,17},{17,1},{2,18},{18,2},{3,19},{19,3},{4,20},{20... | collective-permute-start | bytes 3145736 | tf_op jit(solution)/shard_map/ppermute | solution.py:812
  798.0 29.0 %collective-permute-start.80 = (bf16[192,768]{1,0:T(8,128)(2,1)}, bf16[192,768]{1,0:T(8,128)(2,1)S(1)}, u32[]{:S(2)}, u32[]{:S(2)}) collective-permute-start(bf16[192,768]{1,0:T(8,128)(2,1)} %get-tuple-element.858), channel_id=1, source_target_pairs={{0,1},{1,0},{2,3},{3,2},{4,5},{5,4},{6,7},{7,6},{8,9},{9,8},{10,11... | collective-permute-start | bytes 884744 | tf_op jit(solution)/shard_map/ppermute | solution.py:643
  799.3 28.9 %collective-permute-start.84 = (bf16[192,768]{1,0:T(8,128)(2,1)}, bf16[192,768]{1,0:T(8,128)(2,1)}, u32[]{:S(2)}, u32[]{:S(2)}) collective-permute-start(bf16[192,768]{1,0:T(8,128)(2,1)} %get-tuple-element.859), channel_id=1, source_target_pairs={{0,2},{1,3},{2,0},{3,1},{4,6},{5,7},{6,4},{7,5},{8,10},{9,11},{10,... | collective-permute-start | bytes 884744 | tf_op jit(solution)/shard_map/ppermute | solution.py:643
  823.3 31.0 %collective-permute-start.88 = (bf16[192,768]{1,0:T(8,128)(2,1)S(1)}, bf16[192,768]{1,0:T(8,128)(2,1)S(1)}, u32[]{:S(2)}, u32[]{:S(2)}) collective-permute-start(bf16[192,768]{1,0:T(8,128)(2,1)S(1)} %copy-done.203), channel_id=1, source_target_pairs={{0,3},{1,2},{2,1},{3,0},{4,7},{5,6},{6,5},{7,4},{8,11},{9,10},{10,... | collective-permute-start | bytes 884744 | tf_op jit(solution)/shard_map/ppermute | solution.py:643
  824.4 31.3 %collective-permute-start.82 = (bf16[192,768]{1,0:T(8,128)(2,1)S(1)}, bf16[192,768]{1,0:T(8,128)(2,1)S(1)}, u32[]{:S(2)}, u32[]{:S(2)}) collective-permute-start(bf16[192,768]{1,0:T(8,128)(2,1)S(1)} %copy-done.207), channel_id=1, source_target_pairs={{0,1},{1,0},{2,3},{3,2},{4,5},{5,4},{6,7},{7,6},{8,9},{9,8},{10,11... | collective-permute-start | bytes 884744 | tf_op jit(solution)/shard_map/ppermute | solution.py:643
  825.7 31.2 %collective-permute-start.86 = (bf16[192,768]{1,0:T(8,128)(2,1)S(1)}, bf16[192,768]{1,0:T(8,128)(2,1)S(1)}, u32[]{:S(2)}, u32[]{:S(2)}) collective-permute-start(bf16[192,768]{1,0:T(8,128)(2,1)S(1)} %copy-done.205), channel_id=1, source_target_pairs={{0,2},{1,3},{2,0},{3,1},{4,6},{5,7},{6,4},{7,5},{8,10},{9,11},{10,... | collective-permute-start | bytes 884744 | tf_op jit(solution)/shard_map/ppermute | solution.py:643
  827.1 31.0 %collective-permute-start.90 = (bf16[192,768]{1,0:T(8,128)(2,1)S(1)}, bf16[192,768]{1,0:T(8,128)(2,1)S(1)}, u32[]{:S(2)}, u32[]{:S(2)}) collective-permute-start(bf16[192,768]{1,0:T(8,128)(2,1)S(1)} %copy-done.204), channel_id=1, source_target_pairs={{0,3},{1,2},{2,1},{3,0},{4,7},{5,6},{6,5},{7,4},{8,11},{9,10},{10,... | collective-permute-start | bytes 884744 | tf_op jit(solution)/shard_map/ppermute | solution.py:643
  828.2 31.2 %collective-permute-start.81 = (bf16[192,768]{1,0:T(8,128)(2,1)S(1)}, bf16[192,768]{1,0:T(8,128)(2,1)S(1)}, u32[]{:S(2)}, u32[]{:S(2)}) collective-permute-start(bf16[192,768]{1,0:T(8,128)(2,1)S(1)} %copy-done.209), channel_id=1, source_target_pairs={{0,1},{1,0},{2,3},{3,2},{4,5},{5,4},{6,7},{7,6},{8,9},{9,8},{10,11... | collective-permute-start | bytes 884744 | tf_op jit(solution)/shard_map/ppermute | solution.py:643
  864.4 65.3 %collective-permute-start.76 = (bf16[256,2048]{1,0:T(8,128)(2,1)}, bf16[256,2048]{1,0:T(8,128)(2,1)}, u32[]{:S(2)}, u32[]{:S(2)}) collective-permute-start(bf16[256,2048]{1,0:T(8,128)(2,1)} %get-tuple-element.942), channel_id=1, source_target_pairs={{0,16},{16,0},{1,17},{17,1},{2,18},{18,2},{3,19},{19,3},{4,20},{20... | collective-permute-start | bytes 3145736 | tf_op jit(solution)/shard_map/ppermute | solution.py:812
  871.2 59.3 %collective-permute-start.77 = (bf16[2,2,128,1024]{3,2,1,0:T(8,128)(2,1)}, bf16[2,2,128,1024]{3,2,1,0:T(8,128)(2,1)}, u32[]{:S(2)}, u32[]{:S(2)}) collective-permute-start(bf16[2,2,128,1024]{3,2,1,0:T(8,128)(2,1)} %get-tuple-element.943), channel_id=1, source_target_pairs={{0,1},{1,0},{2,3},{3,2},{4,5},{5,4},{6,7},{7,6},{8,9},{9,8},{10,11... | collective-permute-start | bytes 3145736 | tf_op jit(solution)/shard_map/ppermute | solution.py:812
  872.3 57.4 %collective-permute-start.78 = (bf16[256,1024]{1,0:T(8,128)(2,1)}, bf16[256,1024]{1,0:T(8,128)(2,1)}, u32[]{:S(2)}, u32[]{:S(2)}) collective-permute-start(bf16[256,1024]{1,0:T(8,128)(2,1)} %fusion.70), channel_id=1, source_target_pairs={{0,16},{16,0},{1,17},{17,1},{2,18},{18,2},{3,19},{19,3},{4,20},{20... | collective-permute-start | bytes 1572872 | tf_op jit(solution)/shard_map/ppermute | solution.py:812
  956.4 40.1 %collective-permute-start.100 = (bf16[256,3072]{1,0:T(8,128)(2,1)}, bf16[256,3072]{1,0:T(8,128)(2,1)}, u32[]{:S(2)}, u32[]{:S(2)}) collective-permute-start(bf16[256,3072]{1,0:T(8,128)(2,1)} %convolution_convert_fusion.3), channel_id=1, source_target_pairs={{0,8},{8,0},{1,9},{9,1},{2,10},{10,2},{3,11},{11,3},{4,12},{12,4},... | collective-permute-start | bytes 4718600 | tf_op jit(solution)/shard_map/ppermute | solution.py:812
  958.2 38.3 %collective-permute-start.101 = (bf16[256,3072]{1,0:T(8,128)(2,1)}, bf16[256,3072]{1,0:T(8,128)(2,1)}, u32[]{:S(2)}, u32[]{:S(2)}) collective-permute-start(bf16[256,3072]{1,0:T(8,128)(2,1)} %convolution_convert_fusion.2), channel_id=1, source_target_pairs={{0,8},{8,0},{1,9},{9,1},{2,10},{10,2},{3,11},{11,3},{4,12},{12,4},... | collective-permute-start | bytes 4718600 | tf_op jit(solution)/shard_map/ppermute | solution.py:812
  959.3 36.7 %collective-permute-start.98 = (bf16[256,2048]{1,0:T(8,128)(2,1)}, bf16[256,2048]{1,0:T(8,128)(2,1)S(1)}, u32[]{:S(2)}, u32[]{:S(2)}) collective-permute-start(bf16[256,2048]{1,0:T(8,128)(2,1)} %get-tuple-element.986), channel_id=1, source_target_pairs={{0,16},{16,0},{1,17},{17,1},{2,18},{18,2},{3,19},{19,3},{4,20},{20... | collective-permute-start | bytes 3145736 | tf_op jit(solution)/shard_map/ppermute | solution.py:812
  960.4 32.6 %collective-permute-start.96 = (bf16[256,1024]{1,0:T(8,128)(2,1)}, bf16[256,1024]{1,0:T(8,128)(2,1)S(1)}, u32[]{:S(2)}, u32[]{:S(2)}) collective-permute-start(bf16[256,1024]{1,0:T(8,128)(2,1)} %convolution_convert_fusion.12), channel_id=1, source_target_pairs={{0,8},{8,0},{1,9},{9,1},{2,10},{10,2},{3,11},{11,3},{4,12},{12,4},... | collective-permute-start | bytes 1572872 | tf_op jit(solution)/shard_map/ppermute | solution.py:812
  960.4 33.8 %collective-permute-start.99 = (bf16[2,128,1024]{2,1,0:T(8,128)(2,1)}, bf16[2,128,1024]{2,1,0:T(8,128)(2,1)S(1)}, u32[]{:S(2)}, u32[]{:S(2)}) collective-permute-start(bf16[2,128,1024]{2,1,0:T(8,128)(2,1)} %get-tuple-element.987), channel_id=1, source_target_pairs={{0,2},{2,0},{1,3},{3,1},{4,6},{6,4},{5,7},{7,5},{8,10},{10,8},{9,1... | collective-permute-start | bytes 1572872 | tf_op jit(solution)/shard_map/ppermute | solution.py:812
  1019.4 38.1 %collective-permute-start.109 = (bf16[2,2,32,4096]{3,2,1,0:T(8,128)(2,1)S(1)}, bf16[2,2,32,4096]{3,2,1,0:T(8,128)(2,1)S(1)}, u32[]{:S(2)}, u32[]{:S(2)}) collective-permute-start(bf16[2,2,32,4096]{3,2,1,0:T(8,128)(2,1)S(1)} %get-tuple-element.1042), channel_id=1, source_target_pairs={{0,1},{1,0},{2,3},{3,2},{4,5},{5,4},{6,7},{7,6},{8,9},{9,8},{10,11... | collective-permute-start | bytes 3145736 | tf_op jit(solution)/shard_map/ppermute | solution.py:812
  1020.6 36.9 %collective-permute-start.111 = (bf16[256,1536]{1,0:T(8,128)(2,1)}, bf16[256,1536]{1,0:T(8,128)(2,1)S(1)}, u32[]{:S(2)}, u32[]{:S(2)}) collective-permute-start(bf16[256,1536]{1,0:T(8,128)(2,1)} %get-tuple-element.1044), channel_id=1, source_target_pairs={{0,16},{16,0},{1,17},{17,1},{2,18},{18,2},{3,19},{19,3},{4,20},{20... | collective-permute-start | bytes 2359304 | tf_op jit(solution)/shard_map/ppermute | solution.py:812
  1021.6 35.9 %collective-permute-start.107 = (bf16[256,1024]{1,0:T(8,128)(2,1)}, bf16[256,1024]{1,0:T(8,128)(2,1)S(1)}, u32[]{:S(2)}, u32[]{:S(2)}) collective-permute-start(bf16[256,1024]{1,0:T(8,128)(2,1)} %fusion.73), channel_id=1, source_target_pairs={{0,16},{16,0},{1,17},{17,1},{2,18},{18,2},{3,19},{19,3},{4,20},{20... | collective-permute-start | bytes 1572872 | tf_op jit(solution)/shard_map/ppermute | solution.py:812
  1022.6 34.9 %collective-permute-start.110 = (bf16[128,1024]{1,0:T(8,128)(2,1)}, bf16[128,1024]{1,0:T(8,128)(2,1)S(1)}, u32[]{:S(2)}, u32[]{:S(2)}) collective-permute-start(bf16[128,1024]{1,0:T(8,128)(2,1)} %get-tuple-element.1043), channel_id=1, source_target_pairs={{0,4},{4,0},{1,5},{5,1},{2,6},{6,2},{3,7},{7,3},{8,12},{12,8},{9,1... | collective-permute-start | bytes 786440 | tf_op jit(solution)/shard_map/ppermute | solution.py:812
  1023.3 34.2 %collective-permute-start.112 = (bf16[2,32,1024]{2,1,0:T(8,128)(2,1)}, bf16[2,32,1024]{2,1,0:T(8,128)(2,1)}, u32[]{:S(2)}, u32[]{:S(2)}) collective-permute-start(bf16[2,32,1024]{2,1,0:T(8,128)(2,1)} %get-tuple-element.1045), channel_id=1, source_target_pairs={{0,2},{2,0},{1,3},{3,1},{4,6},{6,4},{5,7},{7,5},{8,10},{10,8},{9,1... | collective-permute-start | bytes 393224 | tf_op jit(solution)/shard_map/ppermute | solution.py:812
  1082.0 39.6 %collective-permute-start.125 = (bf16[64,2816]{1,0:T(8,128)(2,1)}, bf16[64,2816]{1,0:T(8,128)(2,1)S(1)}, u32[]{:S(2)}, u32[]{:S(2)}) collective-permute-start(bf16[64,2816]{1,0:T(8,128)(2,1)} %get-tuple-element.1007), channel_id=1, source_target_pairs={{0,2},{1,3},{2,0},{3,1},{4,6},{5,7},{6,4},{7,5},{8,10},{9,11},{10,... | collective-permute-start | bytes 1081352 | tf_op jit(solution)/shard_map/ppermute | solution.py:643
  1082.5 39.8 %collective-permute-start.126 = (bf16[64,2816]{1,0:T(8,128)(2,1)S(1)}, bf16[64,2816]{1,0:T(8,128)(2,1)S(1)}, u32[]{:S(2)}, u32[]{:S(2)}) collective-permute-start(bf16[64,2816]{1,0:T(8,128)(2,1)S(1)} %copy-done.185), channel_id=1, source_target_pairs={{0,3},{1,2},{2,1},{3,0},{4,7},{5,6},{6,5},{7,4},{8,11},{9,10},{10,... | collective-permute-start | bytes 1081352 | tf_op jit(solution)/shard_map/ppermute | solution.py:643
  1085.1 37.7 %collective-permute-start.127 = (bf16[64,2816]{1,0:T(8,128)(2,1)}, bf16[64,2816]{1,0:T(8,128)(2,1)S(1)}, u32[]{:S(2)}, u32[]{:S(2)}) collective-permute-start(bf16[64,2816]{1,0:T(8,128)(2,1)} %get-tuple-element.1060), channel_id=1, source_target_pairs={{0,1},{1,0},{2,3},{3,2},{4,5},{5,4},{6,7},{7,6},{8,9},{9,8},{10,11... | collective-permute-start | bytes 1081352 | tf_op jit(solution)/shard_map/ppermute | solution.py:643
  1085.6 39.7 %collective-permute-start.128 = (bf16[64,2816]{1,0:T(8,128)(2,1)}, bf16[64,2816]{1,0:T(8,128)(2,1)S(1)}, u32[]{:S(2)}, u32[]{:S(2)}) collective-permute-start(bf16[64,2816]{1,0:T(8,128)(2,1)} %get-tuple-element.1061), channel_id=1, source_target_pairs={{0,2},{1,3},{2,0},{3,1},{4,6},{5,7},{6,4},{7,5},{8,10},{9,11},{10,... | collective-permute-start | bytes 1081352 | tf_op jit(solution)/shard_map/ppermute | solution.py:643
  1086.1 39.2 %collective-permute-start.129 = (bf16[64,2816]{1,0:T(8,128)(2,1)}, bf16[64,2816]{1,0:T(8,128)(2,1)S(1)}, u32[]{:S(2)}, u32[]{:S(2)}) collective-permute-start(bf16[64,2816]{1,0:T(8,128)(2,1)} %get-tuple-element.1062), channel_id=1, source_target_pairs={{0,3},{1,2},{2,1},{3,0},{4,7},{5,6},{6,5},{7,4},{8,11},{9,10},{10,... | collective-permute-start | bytes 1081352 | tf_op jit(solution)/shard_map/ppermute | solution.py:643
  1149.1 41.3 %collective-permute-start.134 = (bf16[2,2,32,3072]{3,2,1,0:T(8,128)(2,1)}, bf16[2,2,32,3072]{3,2,1,0:T(8,128)(2,1)}, u32[]{:S(2)}, u32[]{:S(2)}) collective-permute-start(bf16[2,2,32,3072]{3,2,1,0:T(8,128)(2,1)} %get-tuple-element.1136), channel_id=1, source_target_pairs={{0,1},{1,0},{2,3},{3,2},{4,5},{5,4},{6,7},{7,6},{8,9},{9,8},{10,11... | collective-permute-start | bytes 2359304 | tf_op jit(solution)/shard_map/ppermute | solution.py:812
  1149.7 40.6 %collective-permute-start.132 = (bf16[256,1024]{1,0:T(8,128)(2,1)}, bf16[256,1024]{1,0:T(8,128)(2,1)}, u32[]{:S(2)}, u32[]{:S(2)}) collective-permute-start(bf16[256,1024]{1,0:T(8,128)(2,1)} %convolution_convert_fusion.11), channel_id=1, source_target_pairs={{0,8},{8,0},{1,9},{9,1},{2,10},{10,2},{3,11},{11,3},{4,12},{12,4},... | collective-permute-start | bytes 1572872 | tf_op jit(solution)/shard_map/ppermute | solution.py:812
  1149.7 40.6 %collective-permute-start.133 = (bf16[256,1024]{1,0:T(8,128)(2,1)}, bf16[256,1024]{1,0:T(8,128)(2,1)}, u32[]{:S(2)}, u32[]{:S(2)}) collective-permute-start(bf16[256,1024]{1,0:T(8,128)(2,1)} %convolution_convert_fusion.10), channel_id=1, source_target_pairs={{0,8},{8,0},{1,9},{9,1},{2,10},{10,2},{3,11},{11,3},{4,12},{12,4},... | collective-permute-start | bytes 1572872 | tf_op jit(solution)/shard_map/ppermute | solution.py:812
  1150.2 37.0 %collective-permute-start.131 = (bf16[32,4096]{1,0:T(8,128)(2,1)S(1)}, bf16[32,4096]{1,0:T(8,128)(2,1)}, u32[]{:S(2)}, u32[]{:S(2)}) collective-permute-start(bf16[32,4096]{1,0:T(8,128)(2,1)S(1)} %get-tuple-element.1133), channel_id=1, source_target_pairs={{0,4},{4,0},{1,5},{5,1},{2,6},{6,2},{3,7},{7,3},{8,12},{12,8},{9,1... | collective-permute-start | bytes 786440 | tf_op jit(solution)/shard_map/ppermute | solution.py:812
  1151.5 35.8 %collective-permute-start.130 = (bf16[2,32,1024]{2,1,0:T(8,128)(2,1)}, bf16[2,32,1024]{2,1,0:T(8,128)(2,1)S(1)}, u32[]{:S(2)}, u32[]{:S(2)}) collective-permute-start(bf16[2,32,1024]{2,1,0:T(8,128)(2,1)} %get-tuple-element.1132), channel_id=1, source_target_pairs={{0,2},{2,0},{1,3},{3,1},{4,6},{6,4},{5,7},{7,5},{8,10},{10,8},{9,1... | collective-permute-start | bytes 393224 | tf_op jit(solution)/shard_map/ppermute | solution.py:812
  1189.6 29.0 %collective-permute-start.141 = (bf16[64,2816]{1,0:T(8,128)(2,1)}, bf16[64,2816]{1,0:T(8,128)(2,1)}, u32[]{:S(2)}, u32[]{:S(2)}) collective-permute-start(bf16[64,2816]{1,0:T(8,128)(2,1)} %get-tuple-element.1107), channel_id=1, source_target_pairs={{0,1},{1,0},{2,3},{3,2},{4,5},{5,4},{6,7},{7,6},{8,9},{9,8},{10,11... | collective-permute-start | bytes 1081352 | tf_op jit(solution)/shard_map/ppermute | solution.py:643
  1222.4 28.8 %collective-permute-start.146 = (bf16[64,2816]{1,0:T(8,128)(2,1)}, bf16[64,2816]{1,0:T(8,128)(2,1)}, u32[]{:S(2)}, u32[]{:S(2)}) collective-permute-start(bf16[64,2816]{1,0:T(8,128)(2,1)} %get-tuple-element.1155), channel_id=1, source_target_pairs={{0,3},{1,2},{2,1},{3,0},{4,7},{5,6},{6,5},{7,4},{8,11},{9,10},{10,... | collective-permute-start | bytes 1081352 | tf_op jit(solution)/shard_map/ppermute | solution.py:643
  1345.1 29.9 %collective-permute-start.158 = (bf16[256,1024]{1,0:T(8,128)(2,1)S(1)}, bf16[256,1024]{1,0:T(8,128)(2,1)S(1)}, u32[]{:S(2)}, u32[]{:S(2)}) collective-permute-start(bf16[256,1024]{1,0:T(8,128)(2,1)S(1)} %add_convert_fusion.18), channel_id=1, source_target_pairs={{0,16},{16,0},{1,17},{17,1},{2,18},{18,2},{3,19},{19,3},{4,20},{20... | collective-permute-start | bytes 1572872 | tf_op jit(solution)/shard_map/ppermute | solution.py:812
  1345.8 29.2 %collective-permute-start.157 = (bf16[192,1024]{1,0:T(8,128)(2,1)}, bf16[192,1024]{1,0:T(8,128)(2,1)S(1)}, u32[]{:S(2)}, u32[]{:S(2)}) collective-permute-start(bf16[192,1024]{1,0:T(8,128)(2,1)} %add_convert_fusion.28), channel_id=1, source_target_pairs={{0,16},{16,0},{1,17},{17,1},{2,18},{18,2},{3,19},{19,3},{4,20},{20... | collective-permute-start | bytes 1179656 | tf_op jit(solution)/shard_map/ppermute | solution.py:812
  1347.1 27.9 %collective-permute-start.160 = (bf16[256,768]{1,0:T(8,128)(2,1)S(1)}, bf16[256,768]{1,0:T(8,128)(2,1)S(1)}, u32[]{:S(2)}, u32[]{:S(2)}) collective-permute-start(bf16[256,768]{1,0:T(8,128)(2,1)S(1)} %copy-done.79), channel_id=1, source_target_pairs={{0,4},{4,0},{1,5},{5,1},{2,6},{6,2},{3,7},{7,3},{8,12},{12,8},{9,1... | collective-permute-start | bytes 1179656 | tf_op jit(solution)/shard_map/ppermute | solution.py:812
  1347.1 27.9 %collective-permute-start.159 = (bf16[256,512]{1,0:T(8,128)(2,1)S(1)}, bf16[256,512]{1,0:T(8,128)(2,1)S(1)}, u32[]{:S(2)}, u32[]{:S(2)}) collective-permute-start(bf16[256,512]{1,0:T(8,128)(2,1)S(1)} %add_convert_fusion.33), channel_id=1, source_target_pairs={{0,16},{16,0},{1,17},{17,1},{2,18},{18,2},{3,19},{19,3},{4,20},{20... | collective-permute-start | bytes 786440 | tf_op jit(solution)/shard_map/ppermute | solution.py:812
  1381.8 33.8 %collective-permute-start.165 = (bf16[192,1024]{1,0:T(8,128)(2,1)}, bf16[192,1024]{1,0:T(8,128)(2,1)}, u32[]{:S(2)}, u32[]{:S(2)}) collective-permute-start(bf16[192,1024]{1,0:T(8,128)(2,1)} %get-tuple-element.1252), channel_id=1, source_target_pairs={{0,4},{4,0},{1,5},{5,1},{2,6},{6,2},{3,7},{7,3},{8,12},{12,8},{9,1... | collective-permute-start | bytes 1179656 | tf_op jit(solution)/shard_map/ppermute | solution.py:812
  (373 other events, 4899.6 us)
Sparse Core Ops, SparseCore 0:
  16.5 142.2 all-gather.5
  161.7 118.8 all-gather.7
  283.5 89.8 all-gather.9
  376.9 140.0 reduce-scatter.1
  520.2 79.7 all-gather.11
  953.1 93.2 all-gather.13
